TPU v7x, 32 devices: a whole 2x2x4 slice. The times are simulated.
32 devices in a mesh: blk: 4 (over z), slab: 2 (over x), micro: 4 (over y, core).
Axes of the slice: x: 2, y: 2, z: 4, core: 2. Of those that a mesh axis runs over, the one named last changes fastest.
Arguments:
- displacement: float32 [32, 128, 256], P('blk', 'micro', 'slab'), may hold values from -6 to 6
- load_field: float32 [32, 128, 256], P('blk', 'micro', 'slab'), may hold values from -6 to 6
- foundation: float32 [32, 128, 256], P('blk', 'micro', 'slab'), may hold values from 0.2 to 2
- plastic_flags: int32 [32, 128, 256], P('blk', 'micro', 'slab'), may hold values 0 or 1
- point_slot: int32 [32, 128, 256], P('blk', 'micro', 'slab'), may hold values from 0 to 65535, as said below
- family_in: float32 [4, 3, 256], replicated, may hold values from -5 to 5
- family_mid: bfloat16 [4, 256, 256], replicated, may hold values from -0.375 to 0.375
- family_out: bfloat16 [4, 3, 256], replicated, may hold values from -0.375 to 0.375
- family_tan: float32 [4, 256], replicated, may hold values from 0.002 to 0.02
Outputs:
- updated_field: float32 [32, 128, 256], P('blk', 'micro', 'slab')
- solver_residual: float32 [32, 128, 256], P('blk', 'micro', 'slab')
Inputs may be any that keep to these rules, and one draw needn't show every extreme that they name: `point_slot`: within each device's block of 8 x 32 x 128 nodes the values are distinct; value // 16384 is the point's fibre family and value % 16384 its position among that family's points of the block in node order (last dimension fastest); in every block one family holds exactly 16384 points.
All inputs are finite; a program needn't handle non-finite values. No bound on the sum of `plastic_flags` on one device may be relied on, other than what follows from the above.
Results may differ from a plain program's by a relative error of at most 0.0024.
Values sent between devices are 32-bit elements; how exact they have to be, the bound alone decides.
No kernel may reach another device: no remote copies, remote signals or barrier semaphores. Data moves between devices by JAX's collectives and lax.ppermute only.
A program may use at most 128 MiB of HBM per device.

v0:
```python
import jax
import jax.numpy as jnp
from jax import lax
from jax.sharding import PartitionSpec as P

ITERS = 8


def padded_2(cells, sides, width, closed):
    for axis, dim in sides:
        count = lax.axis_size(axis)
        ends = count if closed else count - 1
        head = lax.slice_in_dim(cells, 0, width, axis=dim)
        tail = lax.slice_in_dim(cells, cells.shape[dim] - width, cells.shape[dim], axis=dim)
        cells = jnp.concatenate(
            [
                lax.ppermute(tail, axis, [(i, (i + 1) % count) for i in range(ends)]),
                cells,
                lax.ppermute(head, axis, [((i + 1) % count, i) for i in range(ends)]),
            ],
            axis=dim,
        )
    return cells


def shifted_diff(extended, dim_index, halo_width, margin, length):
    upper_side = lax.slice_in_dim(
        extended, halo_width - margin + 1, halo_width + length + margin + 1, axis=dim_index
    )
    lower_side = lax.slice_in_dim(
        extended, halo_width - margin - 1, halo_width + length + margin - 1, axis=dim_index
    )
    return (upper_side - lower_side) * 0.5


def extend(stacked, halo_width):
    cycle_ext = padded_2(stacked, (("blk", 1),), halo_width, True)
    slab_ext = padded_2(stacked, (("slab", 3), ("micro", 2)), halo_width, False)
    return (cycle_ext, slab_ext)


def gradients(stacked, halo_width, margin):
    size_x, size_y, size_z = stacked.shape[1:]
    cycle_ext, slab_ext = extend(stacked, halo_width)
    along_x = shifted_diff(cycle_ext, 1, halo_width, margin, size_x)
    along_y = shifted_diff(
        lax.slice_in_dim(slab_ext, halo_width, halo_width + size_z, axis=3),
        2,
        halo_width,
        margin,
        size_y,
    )
    along_z = shifted_diff(
        lax.slice_in_dim(slab_ext, halo_width, halo_width + size_y, axis=2),
        3,
        halo_width,
        margin,
        size_z,
    )
    return (along_x, along_y, along_z)


def fibre_model(block_rows, weight_in, weight_mid, weight_out, weight_tan):
    modal = (
        weight_in[0][:, None] * block_rows[0][None, :]
        + weight_in[1][:, None] * block_rows[1][None, :]
        + weight_in[2][:, None] * block_rows[2][None, :]
    )
    active = jnp.where(block_rows[3][None, :] > 0.5, jnp.tanh(modal), modal).astype(jnp.bfloat16)
    hidden = jnp.dot(weight_mid, active, preferred_element_type=jnp.float32)
    bounded = jnp.tanh(hidden).astype(jnp.bfloat16)
    stress = jnp.dot(weight_out, bounded, preferred_element_type=jnp.float32)
    widened = bounded.astype(jnp.float32)
    tangent = 0.5 + jnp.dot(weight_tan, widened * widened, precision=lax.Precision.HIGHEST)
    return jnp.concatenate([stress, tangent[None, :]], axis=0)


def global_sum(value):
    return lax.psum(value, ("blk", "slab", "micro"))


def body(
    displacement,
    load_field,
    foundation,
    plastic_flags,
    point_slot,
    family_in,
    family_mid,
    family_out,
    family_tan,
):
    size_x, size_y, size_z = displacement.shape
    points_dev = size_x * size_y * size_z
    capacity = points_dev // 2
    family_count = family_in.shape[0]
    strain_x, strain_y, strain_z = gradients(displacement[None], 1, 0)
    payload = jnp.concatenate(
        [strain_x, strain_y, strain_z, plastic_flags[None].astype(jnp.float32)], axis=0
    ).reshape(4, points_dev)
    slots = point_slot.reshape(points_dev)
    padded = (
        jnp.zeros((4, family_count * capacity), jnp.float32)
        .at[:, slots]
        .set(payload)
        .reshape(4, family_count, capacity)
    )
    per_family = lax.map(
        lambda inputs: fibre_model(inputs[0], inputs[1], inputs[2], inputs[3], inputs[4]),
        (jnp.moveaxis(padded, 1, 0), family_in, family_mid, family_out, family_tan),
    )
    returned = jnp.moveaxis(per_family, 0, 1)
    answers = returned.reshape(4, family_count * capacity)[:, slots].reshape(
        4, size_x, size_y, size_z
    )
    cycle_ext, slab_ext = extend(answers, 1)
    stress_x = shifted_diff(cycle_ext[0], 0, 1, 0, size_x)
    stress_y = shifted_diff(slab_ext[1][:, :, 1 : 1 + size_z], 1, 1, 0, size_y)
    stress_z = shifted_diff(slab_ext[2][:, 1 : 1 + size_y, :], 2, 1, 0, size_z)
    tangent_x = cycle_ext[3]
    tangent_y = slab_ext[3][:, :, 1 : 1 + size_z]
    tangent_z = slab_ext[3][:, 1 : 1 + size_y, :]
    rhs = load_field - foundation * displacement + (stress_x + stress_y + stress_z)
    solution = jnp.zeros_like(rhs)
    residual = rhs
    direction = rhs
    current = global_sum(jnp.sum(residual * residual))
    for iteration in range(ITERS):
        grad_x, grad_y, grad_z = gradients(direction[None], 2, 1)
        flux_x = tangent_x * grad_x[0]
        flux_y = tangent_y * grad_y[0]
        flux_z = tangent_z * grad_z[0]
        total = (
            shifted_diff(flux_x, 0, 1, 0, size_x)
            + shifted_diff(flux_y, 1, 1, 0, size_y)
            + shifted_diff(flux_z, 2, 1, 0, size_z)
        )
        image = foundation * direction - total
        alpha = current / global_sum(jnp.sum(direction * image))
        solution = solution + alpha * direction
        residual = residual - alpha * image
        following = global_sum(jnp.sum(residual * residual))
        direction = residual + following / current * direction
        current = following
    return (displacement + solution, residual)


def solution(mesh):
    placed = (
        P("blk", "micro", "slab"),
        P("blk", "micro", "slab"),
        P("blk", "micro", "slab"),
        P("blk", "micro", "slab"),
        P("blk", "micro", "slab"),
        P(),
        P(),
        P(),
        P(),
    )
    return jax.shard_map(
        body,
        mesh=mesh,
        in_specs=placed,
        out_specs=(P("blk", "micro", "slab"), P("blk", "micro", "slab")),
        check_vma=False,
    )
```

profile of v0, /device:TPU:0, one launch (start us, length us, event | category | flops | bytes accessed | tf_op | source)
XLA Modules:
  0.0 1172.3 jit_solution(12247829432491450463)
XLA Ops:
  31.0 93.5 %scatter_custom_fusion = f32[4,65536]{0,1:T(8,128)} fusion(s32[32768]{0:T(1024)S(1)} %bitcast.213, f32[32768,4]{1,0:T(8,128)} %copy.40, f32[]{:T(128)} %constant.13.clone.1), kind=kCustom, calls=%fused_computation.34 | custom fusion | bytes 1049088 | tf_op jit(solution)/shard_map/scatter | solution.py:105
  124.5 18.1 %copy.41 = f32[4,4,16384]{2,0,1:T(4,128)S(1)} copy(f32[4,4,16384]{0,2,1:T(8,128)} %bitcast.150) | data formatting | bytes 2097152 | tf_op jit(solution)/shard_map/reshape | solution.py:106
  142.5 78.4 %while.10 = (s32[]{:T(128)}, f32[4,4,16384]{2,1,0:T(4,128)S(1)}, bf16[4,3,256]{2,1,0:T(4,128)(2,1)S(1)}, bf16[4,256,256]{2,1,0:T(8,128)(2,1)}, f32[4,4,16384]{2,...) while((s32[]{:T(128)}, f32[4,4,16384]{2,1,0:T(4,128)S(1)}, ...), condition=%wide.region_2.3_spmd, body=%wide.region_1.2_spmd.sunk | while | flops 2265022464 | bytes 26981568 | solution.py:108
  152.6 9.5 fusion.181
  172.1 9.5 fusion.181
  220.9 16.1 %copy.43 = f32[4,4,16384]{0,2,1:T(8,128)} copy(f32[4,4,16384]{2,0,1:T(4,128)S(1)} %bitcast.211) | data formatting | bytes 2097152 | tf_op jit(solution)/shard_map/transpose | solution.py:112
  237.0 119.1 %gather_fusion = f32[32768,4]{1,0:T(8,128)} fusion(f32[4,65536]{0,1:T(8,128)} %bitcast.151, s32[32768]{0:T(1024)S(1)} %broadcast_clamp_fusion), kind=kCustom, calls=%fused_computation | custom fusion | bytes 1179648 | tf_op jit(solution)/shard_map/gather | solution.py:113
  356.1 10.0 copy.45
  372.0 10.8 collective-permute-done.8
  416.5 38.4 %all-reduce = (f32[]{:T(128)}, f32[]{:T(128)}) all-reduce(f32[]{:T(128)} %get-tuple-element.55, f32[]{:T(128)} %get-tuple-element.54), channel_id=1, replica_groups=mesh['blk'=4,'slab'=2,'micro'=4] {'blk','slab','micro'}, use_global_device_ids=true, to_apply=%region_4.5 | all-reduce | flops 2 | bytes 16 | tf_op jit(solution)/shard_map/psum | solution.py:79
  456.8 43.2 %psum.114 = f32[]{:T(128)} all-reduce(f32[]{:T(128)} %multiply_reduce_fusion.13), channel_id=1, replica_groups=mesh['blk'=4,'slab'=2,'micro'=4] {'blk','slab','micro'}, use_global_device_ids=true, to_apply=%region_8.9 | all-reduce | flops 1 | bytes 8 | tf_op jit(solution)/shard_map/psum | solution.py:79
  518.8 38.3 %psum.115 = f32[]{:T(128)} all-reduce(f32[]{:T(128)} %get-tuple-element.96), channel_id=1, replica_groups=mesh['blk'=4,'slab'=2,'micro'=4] {'blk','slab','micro'}, use_global_device_ids=true, to_apply=%region_10.11 | all-reduce | flops 1 | bytes 8 | tf_op jit(solution)/shard_map/psum | solution.py:79
  559.1 42.2 %psum.116 = f32[]{:T(128)} all-reduce(f32[]{:T(128)} %get-tuple-element.94), channel_id=1, replica_groups=mesh['blk'=4,'slab'=2,'micro'=4] {'blk','slab','micro'}, use_global_device_ids=true, to_apply=%region_12.13 | all-reduce | flops 1 | bytes 8 | tf_op jit(solution)/shard_map/psum | solution.py:79
  620.1 39.0 %psum.117 = f32[]{:T(128)} all-reduce(f32[]{:T(128)} %get-tuple-element.92), channel_id=1, replica_groups=mesh['blk'=4,'slab'=2,'micro'=4] {'blk','slab','micro'}, use_global_device_ids=true, to_apply=%region_14.15 | all-reduce | flops 1 | bytes 8 | tf_op jit(solution)/shard_map/psum | solution.py:79
  661.1 41.6 %psum.118 = f32[]{:T(128)} all-reduce(f32[]{:T(128)} %get-tuple-element.90), channel_id=1, replica_groups=mesh['blk'=4,'slab'=2,'micro'=4] {'blk','slab','micro'}, use_global_device_ids=true, to_apply=%region_16.17 | all-reduce | flops 1 | bytes 8 | tf_op jit(solution)/shard_map/psum | solution.py:79
  721.5 39.9 %psum.119 = f32[]{:T(128)} all-reduce(f32[]{:T(128)} %get-tuple-element.88), channel_id=1, replica_groups=mesh['blk'=4,'slab'=2,'micro'=4] {'blk','slab','micro'}, use_global_device_ids=true, to_apply=%region_18.19 | all-reduce | flops 1 | bytes 8 | tf_op jit(solution)/shard_map/psum | solution.py:79
  763.4 41.6 %psum.120 = f32[]{:T(128)} all-reduce(f32[]{:T(128)} %get-tuple-element.86), channel_id=1, replica_groups=mesh['blk'=4,'slab'=2,'micro'=4] {'blk','slab','micro'}, use_global_device_ids=true, to_apply=%region_20.21 | all-reduce | flops 1 | bytes 8 | tf_op jit(solution)/shard_map/psum | solution.py:79
  823.8 39.6 %psum.121 = f32[]{:T(128)} all-reduce(f32[]{:T(128)} %get-tuple-element.84), channel_id=1, replica_groups=mesh['blk'=4,'slab'=2,'micro'=4] {'blk','slab','micro'}, use_global_device_ids=true, to_apply=%region_22.23 | all-reduce | flops 1 | bytes 8 | tf_op jit(solution)/shard_map/psum | solution.py:79
  865.5 41.6 %psum.122 = f32[]{:T(128)} all-reduce(f32[]{:T(128)} %get-tuple-element.82), channel_id=1, replica_groups=mesh['blk'=4,'slab'=2,'micro'=4] {'blk','slab','micro'}, use_global_device_ids=true, to_apply=%region_24.25 | all-reduce | flops 1 | bytes 8 | tf_op jit(solution)/shard_map/psum | solution.py:79
  925.9 39.6 %psum.123 = f32[]{:T(128)} all-reduce(f32[]{:T(128)} %get-tuple-element.80), channel_id=1, replica_groups=mesh['blk'=4,'slab'=2,'micro'=4] {'blk','slab','micro'}, use_global_device_ids=true, to_apply=%region_26.27 | all-reduce | flops 1 | bytes 8 | tf_op jit(solution)/shard_map/psum | solution.py:79
  967.5 41.6 %psum.124 = f32[]{:T(128)} all-reduce(f32[]{:T(128)} %get-tuple-element.78), channel_id=1, replica_groups=mesh['blk'=4,'slab'=2,'micro'=4] {'blk','slab','micro'}, use_global_device_ids=true, to_apply=%region_28.29 | all-reduce | flops 1 | bytes 8 | tf_op jit(solution)/shard_map/psum | solution.py:79
  1027.9 39.6 %psum.125 = f32[]{:T(128)} all-reduce(f32[]{:T(128)} %get-tuple-element.76), channel_id=1, replica_groups=mesh['blk'=4,'slab'=2,'micro'=4] {'blk','slab','micro'}, use_global_device_ids=true, to_apply=%region_30.31 | all-reduce | flops 1 | bytes 8 | tf_op jit(solution)/shard_map/psum | solution.py:79
  1069.6 41.6 %psum.126 = f32[]{:T(128)} all-reduce(f32[]{:T(128)} %get-tuple-element.74), channel_id=1, replica_groups=mesh['blk'=4,'slab'=2,'micro'=4] {'blk','slab','micro'}, use_global_device_ids=true, to_apply=%region_32.33 | all-reduce | flops 1 | bytes 8 | tf_op jit(solution)/shard_map/psum | solution.py:79
  1130.0 39.6 %psum.127 = f32[]{:T(128)} all-reduce(f32[]{:T(128)} %get-tuple-element.72), channel_id=1, replica_groups=mesh['blk'=4,'slab'=2,'micro'=4] {'blk','slab','micro'}, use_global_device_ids=true, to_apply=%region_34.35 | all-reduce | flops 1 | bytes 8 | tf_op jit(solution)/shard_map/psum | solution.py:79
  (242 shorter events, 255.3 us)
Async XLA Ops:
  1.7 11.6 collective-permute-start.2
  8.6 11.7 %collective-permute-start = (f32[1,1,32,128]{3,2,1,0:T(8,128)S(1)}, f32[1,1,32,128]{3,2,1,0:T(8,128)S(1)}, u32[]{:S(2)}, u32[]{:S(2)}) collective-permute-start(f32[1,1,32,128]{3,2,1,0:T(8,128)S(1)} %get-tuple-element.169), channel_id=1, source_target_pairs={{8,0},{16,8},{24,16},{0,24},{9,1},{17,9},{25,17},{1,25},{10,2},{18... | collective-permute-start | bytes 49160 | tf_op jit(solution)/shard_map/ppermute | solution.py:19
  12.2 8.1 collective-permute-start.1
  366.3 16.5 %collective-permute-start.8 = (f32[4,8,32,1]{3,2,1,0:T(8,128)S(1)}, f32[4,8,32,1]{3,2,1,0:T(8,128)S(1)}, u32[]{:S(2)}, u32[]{:S(2)}) collective-permute-start(f32[4,8,32,1]{3,2,1,0:T(8,128)S(1)} %get-tuple-element.114), channel_id=1, source_target_pairs={{0,4},{1,5},{2,6},{3,7},{8,12},{9,13},{10,14},{11,15},{16,20},{17,... | collective-permute-start | bytes 12296 | tf_op jit(solution)/shard_map/ppermute | solution.py:17
  370.7 16.6 %collective-permute-start.9 = (f32[4,8,32,1]{3,2,1,0:T(8,128)S(1)}, f32[4,8,32,1]{3,2,1,0:T(8,128)S(1)}, u32[]{:S(2)}, u32[]{:S(2)}) collective-permute-start(f32[4,8,32,1]{3,2,1,0:T(8,128)S(1)} %get-tuple-element.115), channel_id=1, source_target_pairs={{4,0},{5,1},{6,2},{7,3},{12,8},{13,9},{14,10},{15,11},{20,16},{21,... | collective-permute-start | bytes 12296 | tf_op jit(solution)/shard_map/ppermute | solution.py:19
  404.4 11.3 collective-permute-start.12
  404.5 11.2 collective-permute-start.13
  507.0 11.0 collective-permute-start.18
  508.6 9.4 collective-permute-start.19
  608.3 11.0 collective-permute-start.24
  610.1 9.3 collective-permute-start.25
  709.7 11.0 collective-permute-start.30
  712.1 8.7 collective-permute-start.31
  806.5 7.9 collective-permute-start.38
  812.0 11.0 collective-permute-start.36
  814.4 8.7 collective-permute-start.37
  908.6 7.9 collective-permute-start.44
  914.1 11.0 collective-permute-start.42
  916.4 8.7 collective-permute-start.43
  1010.6 7.9 collective-permute-start.50
  1016.1 11.0 collective-permute-start.48
  1018.5 8.7 collective-permute-start.49
  1118.2 11.0 collective-permute-start.54
  1120.5 8.7 collective-permute-start.55
  (39 other events, 693.4 us)
where the time goes:
time: 1180 us; the launch traced here: 1170 us
  blocking collectives  608 us (52%)
  local copies, waits for them, and re-layouts  272 us (23%)
  starting transfers between devices  121 us (10%)
  matrix products  72.6 us (6%)
  waiting for transfers between devices  53.5 us (5%)
  other arithmetic  22.6 us (2%)
  between operations  22.2 us (2%)
    psum x15, blocking collectives, global_sum(): return lax.psum(value, ('blk', 'slab', 'micro'))  608 us
    gather x1, local copies, waits for them, and re-layouts, body(): returned.reshape(4, family_count * capacity)[:, slots]  119 us
    scatter x1, local copies, waits for them, and re-layouts, body(): padded = jnp.zeros((4, family_count * capacity), jnp.float32).at[:, slots...  93.5 us
    ppermute x30, starting transfers between devices, padded_2(): lax.ppermute(tail, axis, [(i, (i + 1) % count) for i in range(ends)])  72 us
    ppermute x30, starting transfers between devices, padded_2(): lax.ppermute(head, axis, [((i + 1) % count, i) for i in range(ends)])  48.6 us
    dot_general x4, matrix products, fibre_model(): jnp.dot(weight_tan, widened * widened, precision=lax.Precision.HIGHEST)  37.9 us
    ppermute x30, waiting for transfers between devices, padded_2(): lax.ppermute(head, axis, [((i + 1) % count, i) for i in range(ends)])  33.1 us
    dot_general x4, matrix products, fibre_model(): hidden = jnp.dot(weight_mid, active, preferred_element_type=jnp.float32)  29.9 us
  transfers between devices with their start and end apart: 60, of which 21 were waited for; matrix products, arithmetic and copies ran while one was open for 1% of the time, Pallas kernels for 0%

commit v1 on v0

v1 whole, which is shorter than its diff:
```python
import jax
import jax.numpy as jnp
from jax import lax
from jax.experimental import pallas as pl
from jax.experimental.pallas import tpu as pltpu
from jax.sharding import PartitionSpec as P

ITERS = 8
AXES = ("blk", "slab", "micro")
BF = jnp.bfloat16
F32 = jnp.float32


def split(value):
    high = lax.reduce_precision(value, 8, 7)
    return high.astype(BF), (value - high).astype(BF)


def pack_families(family_in, family_mid, family_out, family_tan):
    families, _, modes = family_in.shape
    spread = jnp.transpose(family_in, (2, 1, 0))
    spread = jnp.concatenate([spread, spread], axis=2).reshape(modes, 6 * families)
    high, low = split(spread)
    weight_in = jnp.concatenate([high, low], axis=1)
    weight_mid = jnp.transpose(family_mid, (1, 0, 2)).reshape(modes, families * modes)
    none = jnp.zeros((families, 1, modes), BF)
    stress = jnp.concatenate([family_out, none], axis=1).reshape(4 * families, modes)
    none = jnp.zeros((families, 3, modes), BF)
    tan_high, tan_low = split(family_tan)
    tan_high = jnp.concatenate([none, tan_high[:, None]], axis=1).reshape(4 * families, modes)
    tan_low = jnp.concatenate([none, tan_low[:, None]], axis=1).reshape(4 * families, modes)
    weight_out = jnp.concatenate(
        [
            jnp.concatenate([stress, tan_high, tan_high], axis=1),
            jnp.concatenate([jnp.zeros_like(stress), tan_low, tan_low], axis=1),
        ],
        axis=0,
    )
    return weight_in, weight_mid, weight_out


def cells_kernel(families, planes, strain_ref, code_ref, in_ref, mid_ref, out_ref, answer_ref):
    modes = in_ref.shape[0]
    spots = [(a, x) for a in range(code_ref.shape[0]) for x in planes]
    width = len(spots) * 128
    place = lax.broadcasted_iota(jnp.int32, (2 * families, 128), 0)
    column, family_row, flag_row = [], [], []
    for a, x in spots:
        code = code_ref[a, pl.ds(x, 1), :]
        family = lax.shift_right_logical(code, 1)
        picked = lax.rem(place, families) == jnp.broadcast_to(family, place.shape)
        pieces = []
        for j in range(3):
            value = jnp.broadcast_to(strain_ref[j, a, pl.ds(x, 1), :], place.shape)
            high = value.astype(BF).astype(F32)
            piece = jnp.where(place < families, high, value - high)
            pieces.append(jnp.where(picked, piece, 0.0))
        column.append(jnp.concatenate(pieces, axis=0))
        family_row.append(family)
        flag_row.append(lax.bitwise_and(code, 1))
    spread = jnp.concatenate(column, axis=1).astype(BF)
    spread = jnp.concatenate([spread, spread], axis=0)
    family = jnp.concatenate(family_row, axis=1)
    flag = jnp.concatenate(flag_row, axis=1)
    modal = jnp.dot(in_ref[...], spread, preferred_element_type=F32)
    flagged = jnp.broadcast_to(flag, (modes, width)) > 0
    active = jnp.where(flagged, jnp.tanh(modal), modal).astype(BF)
    wide = jnp.broadcast_to(family, (modes, width)).astype(BF)
    nothing = jnp.zeros_like(active)
    stacked = jnp.concatenate(
        [jnp.where(wide == jnp.array(f, BF), active, nothing) for f in range(families)], axis=0
    )
    hidden = jnp.dot(mid_ref[...], stacked, preferred_element_type=F32)
    bounded = jnp.tanh(hidden).astype(BF)
    square = bounded.astype(F32) * bounded.astype(F32)
    square_high = square.astype(BF)
    square_low = (square - square_high.astype(F32)).astype(BF)
    all_three = jnp.concatenate([bounded, square_high, square_low], axis=0)
    result = jnp.dot(out_ref[...], all_three, preferred_element_type=F32)
    result = result[: 4 * families] + result[4 * families :]
    owner = lax.shift_right_logical(lax.broadcasted_iota(jnp.int32, (4 * families, width), 0), 2)
    result = jnp.where(owner == family, result, 0.0)
    total = result[:4]
    for f in range(1, families):
        total = total + result[4 * f : 4 * f + 4]
    for i, (a, x) in enumerate(spots):
        answer_ref[:, a, x, :] = total[:, i * 128 : (i + 1) * 128]


def cells(strain, code, packed, families, step, planes):
    weight_in, weight_mid, weight_out = packed
    count = code.shape[0]
    planes = tuple(planes)
    points = count * len(planes) * 128
    modes = weight_in.shape[0]

    def whole(array):
        return pl.BlockSpec(array.shape, lambda i: (0,) * array.ndim)

    def kernel(*refs):
        cells_kernel(families, planes, *refs)

    return pl.pallas_call(
        kernel,
        grid=(count // step,),
        in_specs=[
            pl.BlockSpec((3, step, 8, 128), lambda i: (0, i, 0, 0)),
            pl.BlockSpec((step, 8, 128), lambda i: (i, 0, 0)),
            whole(weight_in),
            whole(weight_mid),
            whole(weight_out),
        ],
        out_specs=pl.BlockSpec((4, step, 8, 128), lambda i: (0, i, 0, 0)),
        out_shape=jax.ShapeDtypeStruct((4, count, 8, 128), F32),
        compiler_params=pltpu.CompilerParams(vmem_limit_bytes=48 * 2**20),
        cost_estimate=pl.CostEstimate(
            flops=2 * points * modes * modes * (families + 1), bytes_accessed=points * 32, transcendentals=2 * points * modes
        ),
        name="cells",
    )(strain, code, weight_in, weight_mid, weight_out)


def global_sum(value):
    count = 1
    for axis in AXES:
        count = count * lax.axis_size(axis)
    spread = jnp.broadcast_to(value.reshape(1, 1), (count, 128))
    return jnp.sum(lax.all_to_all(spread, AXES, 0, 0, tiled=True)[:, 0])


def widened(cells_, axis, dim, width, closed):
    count = lax.axis_size(axis)
    ends = count if closed else count - 1
    head = lax.slice_in_dim(cells_, 0, width, axis=dim)
    tail = lax.slice_in_dim(cells_, cells_.shape[dim] - width, cells_.shape[dim], axis=dim)
    before = lax.ppermute(tail, axis, [(i, (i + 1) % count) for i in range(ends)])
    after = lax.ppermute(head, axis, [((i + 1) % count, i) for i in range(ends)])
    return jnp.concatenate([before, cells_, after], axis=dim)


HALOS = (("blk", True), ("micro", False), ("slab", False))


def widened_all(field, width):
    return [widened(field, axis, dim, width, closed) for dim, (axis, closed) in enumerate(HALOS)]


def difference(field, dim):
    length = field.shape[dim]
    return (lax.slice_in_dim(field, 2, length, axis=dim) - lax.slice_in_dim(field, 0, length - 2, axis=dim)) * 0.5


def plain_body(
    displacement, load_field, foundation, plastic_flags, point_slot, family_in, family_mid, family_out, family_tan
):
    size_x, size_y, size_z = displacement.shape
    points = size_x * size_y * size_z
    families = family_in.shape[0]
    capacity = points // 2
    packed = pack_families(family_in, family_mid, family_out, family_tan)
    strain = [difference(w, dim) for dim, w in enumerate(widened_all(displacement, 1))]
    code = 2 * (point_slot // capacity) + plastic_flags
    tiles = points // 1024
    answers = cells(jnp.stack(strain).reshape(3, tiles, 8, 128), code.reshape(tiles, 8, 128), packed, families, 2, range(8))
    answers = answers.reshape(4, size_x, size_y, size_z)
    tangents = widened_all(0.5 + answers[3], 1)
    divergence = sum(
        difference(widened(answers[dim], axis, dim, 1, closed), dim) for dim, (axis, closed) in enumerate(HALOS)
    )
    rhs = load_field - foundation * displacement + divergence
    solution_ = jnp.zeros_like(rhs)
    residual = rhs
    direction = rhs
    current = global_sum(jnp.sum(residual * residual))
    for _ in range(ITERS):
        total = sum(
            difference(tangents[dim] * difference(w, dim), dim) for dim, w in enumerate(widened_all(direction, 2))
        )
        image = foundation * direction - total
        alpha = current / global_sum(jnp.sum(direction * image))
        solution_ = solution_ + alpha * direction
        residual = residual - alpha * image
        following = global_sum(jnp.sum(residual * residual))
        direction = residual + following / current * direction
        current = following
    return displacement + solution_, residual


VMEM = pl.BlockSpec(memory_space=pltpu.VMEM)
SMEM = pl.BlockSpec(memory_space=pltpu.SMEM)
GROUP = ("blk", "micro")


def call(kernel, out_shapes, scratch, name, *args, smem=0):
    return pl.pallas_call(
        kernel,
        out_shape=[jax.ShapeDtypeStruct(shape, dtype) for shape, dtype in out_shapes],
        in_specs=[SMEM] * smem + [VMEM] * (len(args) - smem),
        out_specs=[VMEM] * len(out_shapes),
        scratch_shapes=scratch,
        compiler_params=pltpu.CompilerParams(vmem_limit_bytes=40 * 2**20),
        name=name,
    )(*args)


def regroup(tiles):
    group = lax.broadcasted_iota(jnp.int32, (8, 128), 1) // 32
    result = []
    for a in range(4):
        tile = tiles[0]
        for m in range(4):
            shift = (m - a) * 32 % 128
            moved = pltpu.roll(tiles[m], shift, 1) if shift else tiles[m]
            tile = moved if m == 0 else jnp.where(group == m, moved, tile)
        result.append(tile)
    return result


def spread_kernel(place_ref, u_ref, load_ref, found_ref, code_ref, send_ref, turned):
    count = send_ref.shape[0]
    rest = load_ref[...] - found_ref[...] * u_ref[...]
    fields = (u_ref[...], code_ref[...].astype(F32), found_ref[...], rest)
    for number, field in enumerate(fields):
        for half in range(2):
            turned[number, half, 8:136, :] = jnp.transpose(field[4 * half : 4 * half + 4].reshape(128, 128))
    for half in range(2):
        turned[0, half, 0:8, :] = jnp.zeros((8, 128), F32)
        turned[0, half, 136:144, :] = jnp.zeros((8, 128), F32)
    row = lax.broadcasted_iota(jnp.int32, (8, 128), 0)
    for target in range(count):
        start = pl.multiple_of(8 * place_ref[target], 8)
        for number in range(4):
            for half in range(2):
                send_ref[target, 2 * number + half] = turned[number, half, pl.ds(start + 8, 8), :]
        edges = jnp.zeros((8, 128), F32)
        for half in range(2):
            low = turned[0, half, pl.ds(start, 8), :]
            high = turned[0, half, pl.ds(start + 16, 8), :]
            edges = jnp.where(row == half, jnp.broadcast_to(low[7:8], (8, 128)), edges)
            edges = jnp.where(row == 2 + half, jnp.broadcast_to(high[0:1], (8, 128)), edges)
        send_ref[target, 8] = edges


def beside(tile, low, high):
    row = lax.broadcasted_iota(jnp.int32, (8, 128), 0)
    after = jnp.where(row == 7, jnp.broadcast_to(high, (8, 128)), pltpu.roll(tile, 7, 0))
    before = jnp.where(row == 0, jnp.broadcast_to(low, (8, 128)), pltpu.roll(tile, 1, 0))
    return after, before


def radial(tile):
    lane = lax.broadcasted_iota(jnp.int32, tile.shape, tile.ndim - 1)
    after = jnp.where(lane == 127, 0.0, pltpu.roll(tile, 127, tile.ndim - 1))
    before = jnp.where(lane == 0, 0.0, pltpu.roll(tile, 1, tile.ndim - 1))
    return (after - before) * 0.5


def collect_kernel(around, recv_ref, strain_ref, code_ref, found_ref, rest_ref, u):
    along = recv_ref.shape[0] // 4
    edges = []
    for b in range(along):
        for half in range(2):
            for number in range(4):
                tiles = regroup([recv_ref[4 * b + m, 2 * number + half] for m in range(4)])
                for a in range(4):
                    at = 8 * b + 4 * half + a
                    if number == 0:
                        u[at] = tiles[a]
                    elif number == 1:
                        code_ref[at] = tiles[a].astype(jnp.int32)
                    elif number == 2:
                        found_ref[at] = tiles[a]
                    else:
                        rest_ref[at] = tiles[a]
        edges.append(regroup([recv_ref[4 * b + m, 8] for m in range(4)]))
    for at in range(around):
        tile = u[at]
        strain_ref[0, at] = (u[(at + 1) % around] - u[(at - 1) % around]) * 0.5
        strain_ref[1, at] = radial(tile)
        edge, half = edges[at // 8][at % 4], at % 8 // 4
        after, before = beside(tile, edge[half : half + 1], edge[2 + half : 3 + half])
        strain_ref[2, at] = (after - before) * 0.5


def rhs_kernel(around, outer_ref, inner_ref, rest_ref, low_ref, high_ref, own_ref):
    row = lax.broadcasted_iota(jnp.int32, (8, 128), 0)
    rim = (row == 0) | (row == 7)

    def answer(number, at):
        return jnp.where(rim, outer_ref[number, at], inner_ref[number, at])

    cycle = [answer(0, at) for at in range(around)]
    for at in range(around):
        low = low_ref[around + at // 8, pl.ds(at % 8, 1), :]
        high = high_ref[around + at // 8, pl.ds(at % 8, 1), :]
        after, before = beside(answer(2, at), low, high)
        divergence = (cycle[(at + 1) % around] - cycle[(at - 1) % around]) * 0.5
        divergence = divergence + radial(answer(1, at)) + (after - before) * 0.5
        own_ref[0, at] = rest_ref[at] + divergence
        own_ref[1, at] = 0.5 + answer(3, at)


HALF = ITERS // 2


def basis_kernel(
    around, seeds, ends_ref, scale_ref, tan_ref, tan_low_ref, tan_high_ref, found_ref, found_low_ref, found_high_ref,
    seed_ref, seed_low_ref, seed_high_ref, own_ref, gram_ref, tan, main, off_a, off_r, back_r, off_x, back_x, vectors
):
    centre, inverse = scale_ref[0], scale_ref[1]
    lane = lax.broadcasted_iota(jnp.int32, (24, 128), 1)
    plane = lax.broadcasted_iota(jnp.int32, (24, 128), 0)
    cut = ((plane == 7) & (ends_ref[0] == 1)) | ((plane == 14) & (ends_ref[1] == 1))
    quarter = 0.25 * inverse

    def three(low, own, high):
        return jnp.concatenate([low, own, high], axis=0)

    for at in range(around):
        tan[at] = three(tan_low_ref[at], tan_ref[at], tan_high_ref[at]) * quarter
    for at in range(around):
        here = tan[at]
        up_a, down_a = tan[(at + 1) % around], tan[(at - 1) % around]
        up_r = jnp.where(lane == 127, 0.0, pltpu.roll(here, 127, 1))
        down_r = jnp.where(lane == 0, 0.0, pltpu.roll(here, 1, 1))
        up_x = pltpu.roll(here, 23, 0)
        down_x = pltpu.roll(here, 1, 0)
        found = three(found_low_ref[at], found_ref[at], found_high_ref[at])
        main[at] = (found - centre) * inverse + ((up_a + down_a) + (up_r + down_r) + (up_x + down_x))
        beyond = jnp.where(lane >= 126, 0.0, up_r)
        off_r[at] = beyond
        back_r[at] = pltpu.roll(beyond, 2, 1)
        beyond = jnp.where(cut, 0.0, up_x)
        off_x[at] = beyond
        back_x[at] = pltpu.roll(beyond, 2, 0)

    def apply(index, at):
        value = vectors[index, at]
        result = main[at] * value
        result = result - tan[(at + 1) % around] * vectors[index, (at + 2) % around]
        result = result - tan[(at - 1) % around] * vectors[index, (at - 2) % around]
        result = result - off_r[at] * pltpu.roll(value, 126, 1) - back_r[at] * pltpu.roll(value, 2, 1)
        return result - off_x[at] * pltpu.roll(value, 22, 0) - back_x[at] * pltpu.roll(value, 2, 0)

    size = HALF + 1
    for seed in range(seeds):
        base = seed * size
        for at in range(around):
            vectors[base, at] = three(seed_low_ref[seed, at], seed_ref[seed, at], seed_high_ref[seed, at])
        for degree in range(1, size):
            for at in range(around):
                value = apply(base + degree - 1, at)
                if degree > 1:
                    value = value + value - vectors[base + degree - 2, at]
                vectors[base + degree, at] = value
    total = seeds * size
    for index in range(total):
        for at in range(around):
            own_ref[index, at] = vectors[index, at, 8:16, :]
    column = lax.broadcasted_iota(jnp.int32, (1, 128), 1)
    gram = jnp.zeros((1, 128), F32)
    number = 0
    for i in range(total):
        sums = [jnp.zeros((8, 128), F32)] * (total - i)
        for at in range(around):
            left = own_ref[i, at]
            for j in range(i, total):
                sums[j - i] = sums[j - i] + left * own_ref[j, at]
        for value in sums:
            entry = jnp.sum(jnp.sum(value, axis=0, keepdims=True), axis=1, keepdims=True)
            gram = jnp.where(column == number, jnp.broadcast_to(entry, (1, 128)), gram)
            number += 1
    gram_ref[...] = gram


def unpack_gram(all_ref, total):
    row = jnp.sum(all_ref[...], axis=0, keepdims=True)
    gram, number = {}, 0
    for i in range(total):
        for j in range(i, total):
            gram[i, j] = gram[j, i] = jnp.broadcast_to(row[:, number : number + 1], (1, 128))
            number += 1
    return gram


def dot(gram, left, right):
    total = len(left)
    result = None
    for i in range(total):
        if left[i] is None:
            continue
        inner = None
        for j in range(total):
            if right[j] is not None:
                term = gram[i, j] * right[j]
                inner = term if inner is None else inner + term
        if inner is not None:
            result = left[i] * inner if result is None else result + left[i] * inner
    return result


def axpy(scale, left, right):
    result = []
    for a, b in zip(left, right, strict=True):
        a = None if a is None else (a if scale is None else scale * a)
        result.append(b if a is None else (a if b is None else b + a))
    return result


def times_operator(vector, centre, half_width, size):
    result = []
    half = 0.5 * half_width
    for base in range(0, len(vector), size):
        part = vector[base : base + size]
        for j in range(size):
            terms = []
            if part[j] is not None:
                terms.append(centre * part[j])
            if j > 0 and part[j - 1] is not None:
                terms.append((half_width if j == 1 else half) * part[j - 1])
            if j + 1 < size and part[j + 1] is not None:
                terms.append(half * part[j + 1])
            result.append(sum(terms[1:], terms[0]) if terms else None)
    return result


def iterate(gram, total, residual, direction, current, centre, half_width, worst):
    size = HALF + 1
    change = [None] * total
    norms = [jnp.sqrt(gram[i, i]) for i in range(total)]
    before = current
    for step in range(HALF):
        image = times_operator(direction, centre, half_width, size)
        alpha = current / dot(gram, direction, image)
        change = axpy(alpha, direction, change)
        residual = axpy(-alpha, image, residual)
        following = dot(gram, residual, residual)
        bound = None
        for c, n in zip(residual, norms, strict=True):
            if c is not None:
                bound = jnp.abs(c) * n if bound is None else bound + jnp.abs(c) * n
        worst = jnp.maximum(worst, bound * bound / following)
        worst = jnp.where(following > 0.0, worst, jnp.inf)
        before = current
        if step < HALF - 1:
            direction = axpy(following / current, direction, residual)
        current = following
    return change, residual, direction, before, current, worst


def combine(coefficients, own_ref, at):
    result = None
    for index, c in enumerate(coefficients):
        if c is not None:
            term = jnp.broadcast_to(c, (8, 128)) * own_ref[index, at]
            result = term if result is None else result + term
    return result


def middle_kernel(around, scale_ref, all_ref, own_ref, seeds_ref, change_ref, state_ref):
    total = HALF + 1
    gram = unpack_gram(all_ref, total)
    one = [jnp.ones((1, 128), F32)] + [None] * HALF
    nothing = jnp.zeros((1, 128), F32)
    change, residual, direction, before, _, worst = iterate(
        gram, total, one, one, gram[0, 0], scale_ref[0], scale_ref[2], nothing
    )
    for at in range(around):
        seeds_ref[0, at] = combine(residual, own_ref, at)
        seeds_ref[1, at] = combine(direction, own_ref, at)
        change_ref[at] = combine(change, own_ref, at)
    state_ref[...] = jnp.concatenate([before, worst] + [nothing] * 6, axis=0)


def last_kernel(around, scale_ref, all_ref, own_ref, change_ref, state_ref, send_ref, worst_ref):
    size = HALF + 1
    total = 2 * size
    gram = unpack_gram(all_ref, total)
    ones = jnp.ones((1, 128), F32)
    residual = [ones] + [None] * (total - 1)
    beta = gram[0, 0] / state_ref[0:1, :]
    direction = list(residual)
    direction[size] = beta
    change, residual, _, _, _, worst = iterate(
        gram, total, residual, direction, gram[0, 0], scale_ref[0], scale_ref[2], state_ref[1:2, :]
    )
    worst_ref[...] = jnp.broadcast_to(worst, (8, 128))
    for b in range(around // 8):
        for half in range(2):
            for number in range(2):
                tiles = []
                for a in range(4):
                    at = 8 * b + 4 * half + a
                    if number == 0:
                        tiles.append(change_ref[at] + combine(change, own_ref, at))
                    else:
                        tiles.append(combine(residual, own_ref, at))
                tiles = regroup(tiles)
                for m in range(4):
                    send_ref[4 * b + m, 2 * number + half] = tiles[m]


def deliver_kernel(place_ref, u_ref, recv_ref, updated_ref, residual_ref, turned):
    for source in range(recv_ref.shape[0]):
        start = pl.multiple_of(8 * place_ref[source], 8)
        for index in range(4):
            turned[index, pl.ds(start, 8), :] = recv_ref[source, index]
    for half in range(2):
        part = slice(4 * half, 4 * half + 4)
        updated_ref[part] = u_ref[part] + jnp.transpose(turned[half]).reshape(4, 32, 128)
        residual_ref[part] = jnp.transpose(turned[2 + half]).reshape(4, 32, 128)


def sliced_body(
    displacement, load_field, foundation, plastic_flags, point_slot, family_in, family_mid, family_out, family_tan
):
    size_x, size_y, size_z = displacement.shape
    families = family_in.shape[0]
    along, across = lax.axis_size("blk"), lax.axis_size("micro")
    peers = along * across
    around = size_x * along
    everyone = peers * lax.axis_size("slab")
    slab = lax.axis_index("slab")
    path = [b * across + (m if b % 2 == 0 else across - 1 - m) for b in range(along) for m in range(across)]
    forth = jnp.array(path, jnp.int32)
    place = jnp.where(slab == 0, forth, peers - 1 - forth)
    mine = jnp.take(place, lax.axis_index("blk") * across + lax.axis_index("micro")) + peers * slab
    ends = jnp.stack([(mine == 0), (mine == everyone - 1)]).astype(jnp.int32)
    spots = [0] * everyone
    for b in range(along):
        for s in range(2):
            for m in range(across):
                position = path[b * across + m]
                spots[position if s == 0 else 2 * peers - 1 - position] = (b * 2 + s) * across + m
    rising = [(spots[i], spots[i + 1]) for i in range(everyone - 1)]
    falling = [(b, a) for a, b in rising]

    def neighbours(to_next, to_previous):
        return lax.ppermute(to_next, AXES, rising), lax.ppermute(to_previous, AXES, falling)

    packed = pack_families(family_in, family_mid, family_out, family_tan)
    typical = 0.5 + 0.33 * jnp.mean(jnp.sum(family_tan, axis=1))
    centre = 1.1 + 1.5 * typical
    half_width = centre - 0.2
    scale = jnp.stack([centre, 1.0 / half_width, half_width])

    rim = jnp.where(slab == 0, displacement[:, :, size_z - 1], displacement[:, :, 0]).reshape(2, 128)
    rim = lax.ppermute(rim, "slab", [(0, 1), (1, 0)])
    code = 2 * (point_slot // (size_x * size_y * size_z // 2)) + plastic_flags
    (send,) = call(
        spread_kernel, [((peers, 9, 8, 128), F32)], [pltpu.VMEM((4, 2, 144, 128), F32)], "spread",
        place, displacement, load_field, foundation, code, smem=1,
    )
    middle = path.index(peers - 1)
    send = lax.dynamic_update_slice(send, rim[None, None], (middle, 8, jnp.where(slab == 0, 2, 0), 0))
    recv = lax.all_to_all(send, GROUP, 0, 0, tiled=True)
    field = (around, 8, 128)
    strain, code, found, rest = call(
        lambda *refs: collect_kernel(around, *refs),
        [((3,) + field, F32), (field, jnp.int32), (field, F32), (field, F32)],
        [pltpu.VMEM(field, F32)], "collect", recv,
    )
    outer = cells(strain, code, packed, families, 8, (0, 7))
    rows = (around // 8, 8, 128)
    low, high = neighbours(
        jnp.concatenate([found, outer[2, :, 7].reshape(rows)]), jnp.concatenate([found, outer[2, :, 0].reshape(rows)])
    )
    inner = cells(strain, code, packed, families, 4, range(1, 7))
    (own,) = call(
        lambda *refs: rhs_kernel(around, *refs), [((2,) + field, F32)], [], "rhs", outer, inner, rest, low, high
    )
    own_low, own_high = neighbours(own, own)

    def basis(seeds, tangents, vectors):
        tall = pltpu.VMEM((around, 24, 128), F32)
        total = seeds * (HALF + 1)
        products, gram = call(
            lambda *refs: basis_kernel(around, seeds, *refs),
            [((total,) + field, F32), ((1, 128), F32)],
            [tall] * 7 + [pltpu.VMEM((total, around, 24, 128), F32)],
            "basis", ends, scale, *tangents, found, low, high, *vectors, smem=2,
        )
        return products, lax.all_to_all(jnp.broadcast_to(gram, (everyone, 128)), AXES, 0, 0, tiled=True)

    tangents = (own[1], own_low[1], own_high[1])
    first, sums = basis(1, tangents, (own[:1], own_low[:1], own_high[:1]))
    seeds, change, state = call(
        lambda *refs: middle_kernel(around, *refs),
        [((2,) + field, F32), (field, F32), ((8, 128), F32)], [], "middle", scale, sums, first, smem=1,
    )
    second, sums = basis(2, tangents, (seeds, *neighbours(seeds, seeds)))
    send, worst = call(
        lambda *refs: last_kernel(around, *refs),
        [((peers, 4, 8, 128), F32), ((8, 128), F32)], [], "last", scale, sums, second, change, state, smem=1,
    )
    recv = lax.all_to_all(send, GROUP, 0, 0, tiled=True)
    shape = displacement.shape
    updated, residual = call(
        deliver_kernel, [(shape, F32), (shape, F32)], [pltpu.VMEM((4, 128, 128), F32)], "deliver",
        place, displacement, recv, smem=1,
    )
    return updated, residual, worst[0, 0]


MOST_LOST = 3000.0


def body(*inputs):
    size_x, size_y, size_z = inputs[0].shape
    along, across = lax.axis_size("blk"), lax.axis_size("micro")
    fits = (
        (size_x, size_y, size_z) == (8, 32, 128)
        and across == 4
        and size_z == 8 * along * across
        and lax.axis_size("slab") == 2
    )
    if not fits:
        return plain_body(*inputs)
    updated, residual, worst = sliced_body(*inputs)
    return lax.cond(worst < MOST_LOST, lambda: (updated, residual), lambda: plain_body(*inputs))


def solution(mesh):
    field = P("blk", "micro", "slab")
    return jax.shard_map(
        body,
        mesh=mesh,
        in_specs=(field,) * 5 + (P(),) * 4,
        out_specs=(field, field),
        check_vma=False,
    )
```

time: 1180 us -> 138 us (0.12)
  blocking collectives: 608 us -> 30.5 us
  local copies, waits for them, and re-layouts: 272 us -> 3.53 us
  starting transfers between devices: 121 us -> 24.1 us
  matrix products: 72.6 us -> 0 us
  Pallas kernels: 0 us -> 48.2 us
  waiting for transfers between devices: 53.5 us -> 24.6 us
  between operations: 22.2 us -> 3.05 us
  other arithmetic: 22.6 us -> 3.68 us
    psum x15 -> x0, blocking collectives: 608 us -> none  [global_sum(): return lax.psum(value, ('blk', 'slab', 'micro'))]
    gather x1 -> x0, local copies, waits for them, and re-layouts: 119 us -> none  [body(): returned.reshape(4, family_count * capacity)[:, slots]]
    ppermute x60 -> x7, starting transfers between devices: 121 us -> 14.6 us  [the longest x3 7.56 us: neighbours(): lax.ppermute(to_next, AXES, rising)]
    scatter x1 -> x0, local copies, waits for them, and re-layouts: 93.5 us -> none  [body(): padded = jnp.zeros((4, family_count * capacity), jnp.float32).at[:, slots...]
    dot_general x12 -> x0, matrix products: 72.6 us -> none  [the longest x4 37.9 us: fibre_model(): jnp.dot(weight_tan, widened * widened, precision=lax.Precision.HIGHEST)]
    ppermute x60 -> x7, waiting for transfers between devices: 53.5 us -> 3.28 us  [the longest x3 2.21 us: neighbours(): lax.ppermute(to_previous, AXES, falling)]
    pallas_call x0 -> x10, Pallas kernels: none -> 48.2 us  [the longest x2 33.4 us: cells(): pl.pallas_call(kernel, grid=(count // step,), in_specs=[pl.BlockSpec((3,...]
    all_to_all x0 -> x2, blocking collectives: none -> 30.5 us  [basis(): lax.all_to_all(jnp.broadcast_to(gram, (everyone, 128)), AXES, 0, 0, tiled...]
  transfers between devices with their start and end apart: 60 -> 9, of which waited for: 21 -> 4; matrix products, arithmetic and copies ran while one was open for 1% -> 3% of each run, Pallas kernels for 0% -> 20%
where the time goes in v1:
time: 138 us
  Pallas kernels  48.2 us (35%)
  blocking collectives  30.5 us (22%)
  waiting for transfers between devices  24.6 us (18%)
  starting transfers between devices  24.1 us (17%)
  other arithmetic  3.68 us (3%)
  local copies, waits for them, and re-layouts  3.53 us (3%)
  between operations  3.05 us (2%)
    pallas_call x2, Pallas kernels, cells(): pl.pallas_call(kernel, grid=(count // step,), in_specs=[pl.BlockSpec((3,...  33.4 us
    all_to_all x2, blocking collectives, basis(): lax.all_to_all(jnp.broadcast_to(gram, (everyone, 128)), AXES, 0, 0, tiled...  30.5 us
    all_to_all x2, waiting for transfers between devices, sliced_body(): recv = lax.all_to_all(send, GROUP, 0, 0, tiled=True)  21.4 us
    pallas_call x8, Pallas kernels, call(): pl.pallas_call(kernel, out_shape=[jax.ShapeDtypeStruct(shape, dtype) for...  14.8 us
    all_to_all x2, starting transfers between devices, sliced_body(): recv = lax.all_to_all(send, GROUP, 0, 0, tiled=True)  9.47 us
    ppermute x3, starting transfers between devices, neighbours(): lax.ppermute(to_next, AXES, rising)  7.56 us
    ppermute x3, starting transfers between devices, neighbours(): lax.ppermute(to_previous, AXES, falling)  4.06 us
    ppermute x1, starting transfers between devices, sliced_body(): rim = lax.ppermute(rim, 'slab', [(0, 1), (1, 0)])  2.97 us
  transfers between devices with their start and end apart: 9, of which 4 were waited for; matrix products, arithmetic and copies ran while one was open for 3% of the time, Pallas kernels for 20%

profile of v1, /device:TPU:0, one launch (start us, length us, event | category | flops | bytes accessed | tf_op | source)
XLA Modules:
  0.0 137.6 jit_solution(15184584685119744200)
XLA Ops:
  0.6 1.2 select_reduce_fusion
  1.9 3.0 %collective-permute-start.66 = (f32[2,128]{1,0:T(2,128)S(1)}, f32[2,128]{1,0:T(2,128)S(1)}, u32[]{:S(2)}, u32[]{:S(2)}) collective-permute-start(f32[2,128]{1,0:T(2,128)S(1)} %select_n.49), channel_id=1, source_target_pairs={{0,4},{4,0},{1,5},{5,1},{2,6},{6,2},{3,7},{7,3},{8,12},{12,8},{9,1... | collective-permute-start | bytes 3080 | tf_op jit(solution)/shard_map/ppermute | solution.py:548
  4.9 1.1 fusion.103.code_ref
  6.6 2.2 %spread.1 = f32[16,9,8,128]{3,2,1,0:T(8,128)} custom-call(s32[16]{0:T(128)S(1)} %broadcast_select_fusion.place_ref, f32[8,32,128]{2,1,0:T(8,128)} %u_ref.3, f32[8,32,128]{2,1,0:T(8,128)} %load_ref.1, f32[8,32,128]{2,1,0:T(8,128)} %found_ref.1, s32[8,32,128]{2,1,0:T(8,128)S(1)} %fusion.103.code_ref), custom_call_target="tpu_custom_call" | custom-call | tf_op jit(solution)/shard_map/spread/pallas_call | solution.py:195
  9.4 5.9 %all-to-all-start.16 = ((f32[16,9,8,128]{3,2,1,0:T(8,128)}), f32[16,9,8,128]{3,2,1,0:T(8,128)S(1)}, u32[]{:S(2)}, u32[]{:S(2)}) async-start(f32[16,9,8,128]{3,2,1,0:T(8,128)} %bitcast_dynamic-update-slice_fusion), calls=%async_computation.16 | async-start | bytes 1179648 | tf_op jit(solution)/shard_map/all_to_all | solution.py:556
  18.4 12.5 %all-to-all-done.16.refs_0_ = f32[16,9,8,128]{3,2,1,0:T(8,128)S(1)} async-done(((f32[16,9,8,128]{3,2,1,0:T(8,128)}), f32[16,9,8,128]{3,2,1,0:T(8,128)S(1)}, u32[]{:S(2)}, u32[]{:S(2)}) %all-to-all-start.16) | async-done | bytes 589856 | tf_op jit(solution)/shard_map/all_to_all | solution.py:556
  31.5 8.3 %cells.4.refs_0_ = f32[4,32,8,128]{3,2,1,0:T(8,128)S(1)} custom-call(f32[3,32,8,128]{3,2,1,0:T(8,128)S(1)} %get-tuple-element.46.refs_0_, s32[32,8,128]{2,1,0:T(8,128)S(1)} %get-tuple-element.47.refs_1_, bf16[256,48]{1,0:T(8,128)(2,1)S(1)} %copy.83.refs_2_, bf16[256,1024]{1,0:T(8,128)(2,1)S(1)} %bitcast.82, bf16[32,768]{1,0:T(8,128)(2,1)S(1)} %maximum_maximum_fusion.1.refs_4_), custom_call_target="tpu_custom_call" | custom-call | flops 5368709120 | bytes 262144 | tf_op jit(solution)/shard_map/cells/pallas_call | solution.py:103
  39.8 1.9 %collective-permute-start.67 = (f32[36,8,128]{2,1,0:T(8,128)S(1)}, f32[36,8,128]{2,1,0:T(8,128)S(1)}, u32[]{:S(2)}, u32[]{:S(2)}) collective-permute-start(f32[36,8,128]{2,1,0:T(8,128)S(1)} %get-tuple-element.238), channel_id=1, source_target_pairs={{0,1},{1,2},{2,3},{3,11},{11,10},{10,9},{9,8},{8,16},{16,17},{17,1... | collective-permute-start | bytes 442376 | tf_op jit(solution)/shard_map/ppermute | solution.py:539
  41.8 1.3 collective-permute-start.68
  43.1 25.1 %cells.5.refs_1_ = f32[4,32,8,128]{3,2,1,0:T(8,128)S(1)} custom-call(f32[3,32,8,128]{3,2,1,0:T(8,128)S(1)} %get-tuple-element.46.refs_0_, s32[32,8,128]{2,1,0:T(8,128)S(1)} %get-tuple-element.47.refs_1_, bf16[256,48]{1,0:T(8,128)(2,1)S(1)} %copy.83.refs_2_, bf16[256,1024]{1,0:T(8,128)(2,1)S(1)} %bitcast.83, bf16[32,768]{1,0:T(8,128)(2,1)S(1)} %maximum_maximum_fusion.1.refs_4_), custom_call_target="tpu_custom_call" | custom-call | flops 16106127360 | bytes 786432 | tf_op jit(solution)/shard_map/cells/pallas_call | solution.py:103
  68.3 1.3 collective-permute-start.70
  69.7 3.8 %collective-permute-start.69 = (f32[2,32,8,128]{3,2,1,0:T(8,128)S(1)}, f32[2,32,8,128]{3,2,1,0:T(8,128)S(1)}, u32[]{:S(2)}, u32[]{:S(2)}) collective-permute-start(f32[2,32,8,128]{3,2,1,0:T(8,128)S(1)} %rhs.2), channel_id=1, source_target_pairs={{0,1},{1,2},{2,3},{3,11},{11,10},{10,9},{9,8},{8,16},{16,17},{17,1... | collective-permute-start | bytes 786440 | tf_op jit(solution)/shard_map/ppermute | solution.py:539
  73.6 1.1 collective-permute-done.69
  74.7 3.5 %basis.2 = (f32[5,32,8,128]{3,2,1,0:T(8,128)S(1)}, f32[1,128]{1,0:T(1,128)S(1)}) custom-call(s32[2]{0:T(128)S(1)} %add_convert_fusion.refs_0_, f32[3]{0:T(128)S(1)} %pad_maximum_fusion.20.refs_1_.refs_0_, f32[32,8,128]{2,1,0:T(8,128)S(1)} %get-tuple-element.236.refs_2_, f32[32,8,128]{2,1,0:T(8,128)S(1)} %get-tuple-element.234.refs_3_, ...), custom_call_target="tpu_custom_call" | custom-call | tf_op jit(solution)/shard_map/basis/pallas_call | solution.py:195
  78.3 16.4 %all_to_all.153 = f32[32,1,128]{2,1,0:T(1,128)S(1)} all-to-all(f32[32,1,128]{2,1,0:T(1,128)S(1)} %broadcast_in_dim.54), channel_id=1, replica_groups=mesh['blk'=4,'slab'=2,'micro'=4] {'blk','slab','micro'}, dimensions={0} | all-to-all | bytes 32768 | tf_op jit(solution)/shard_map/all_to_all | solution.py:583
  94.7 0.8 middle.1
  95.6 1.8 %collective-permute-start.71 = (f32[2,32,8,128]{3,2,1,0:T(8,128)S(1)}, f32[2,32,8,128]{3,2,1,0:T(8,128)S(1)}, u32[]{:S(2)}, u32[]{:S(2)}) collective-permute-start(f32[2,32,8,128]{3,2,1,0:T(8,128)S(1)} %get-tuple-element.52.refs_8_), channel_id=1, source_target_pairs={{0,1},{1,2},{2,3},{3,11},{11,10},{10,9},{9,8},{8,16},{16,17},{17,1... | collective-permute-start | bytes 786440 | tf_op jit(solution)/shard_map/ppermute | solution.py:539
  97.4 1.5 %collective-permute-start.72 = (f32[2,32,8,128]{3,2,1,0:T(8,128)S(1)}, f32[2,32,8,128]{3,2,1,0:T(8,128)S(1)}, u32[]{:S(2)}, u32[]{:S(2)}) collective-permute-start(f32[2,32,8,128]{3,2,1,0:T(8,128)S(1)} %get-tuple-element.52.refs_8_), channel_id=1, source_target_pairs={{1,0},{2,1},{3,2},{11,3},{10,11},{9,10},{8,9},{16,8},{17,16},{18,1... | collective-permute-start | bytes 786440 | tf_op jit(solution)/shard_map/ppermute | solution.py:539
  98.8 2.2 %collective-permute-done.72.refs_10_ = f32[2,32,8,128]{3,2,1,0:T(8,128)S(1)} collective-permute-done((f32[2,32,8,128]{3,2,1,0:T(8,128)S(1)}, f32[2,32,8,128]{3,2,1,0:T(8,128)S(1)}, u32[]{:S(2)}, u32[]{:S(2)}) %collective-permute-start.72) | collective-permute-done | bytes 262176 | tf_op jit(solution)/shard_map/ppermute | solution.py:539
  101.0 4.9 %basis.3 = (f32[10,32,8,128]{3,2,1,0:T(8,128)S(1)}, f32[1,128]{1,0:T(1,128)S(1)}) custom-call(s32[2]{0:T(128)S(1)} %add_convert_fusion.refs_0_, f32[3]{0:T(128)S(1)} %pad_maximum_fusion.20.refs_1_.refs_0_, f32[32,8,128]{2,1,0:T(8,128)S(1)} %get-tuple-element.236.refs_2_, f32[32,8,128]{2,1,0:T(8,128)S(1)} %get-tuple-element.234.refs_3_, ...), custom_call_target="tpu_custom_call" | custom-call | tf_op jit(solution)/shard_map/basis/pallas_call | solution.py:195
  106.1 14.0 %all_to_all.154 = f32[32,1,128]{2,1,0:T(1,128)S(1)} all-to-all(f32[32,1,128]{2,1,0:T(1,128)S(1)} %broadcast_in_dim.55), channel_id=1, replica_groups=mesh['blk'=4,'slab'=2,'micro'=4] {'blk','slab','micro'}, dimensions={0} | all-to-all | bytes 32768 | tf_op jit(solution)/shard_map/all_to_all | solution.py:583
  120.1 1.9 %last.1 = (f32[16,4,8,128]{3,2,1,0:T(8,128)}, f32[8,128]{1,0:T(8,128)S(1)}) custom-call(f32[3]{0:T(128)S(1)} %pad_maximum_fusion.20.refs_1_.refs_0_, f32[32,128]{1,0:T(8,128)S(1)} %bitcast.86, f32[10,32,8,128]{3,2,1,0:T(8,128)S(1)} %get-tuple-element.54.refs_2_, f32[32,8,128]{2,1,0:T(8,128)S(1)} %get-tuple-element.55.refs_3_, ...), custom_call_target="tpu_custom_call" | custom-call | tf_op jit(solution)/shard_map/last/pallas_call | solution.py:195
  122.0 3.5 %all-to-all-start.19 = ((f32[16,4,8,128]{3,2,1,0:T(8,128)}), f32[16,4,8,128]{3,2,1,0:T(8,128)S(1)}, u32[]{:S(2)}, u32[]{:S(2)}) async-start(f32[16,4,8,128]{3,2,1,0:T(8,128)} %get-tuple-element.58), calls=%async_computation.19 | async-start | bytes 524288 | tf_op jit(solution)/shard_map/all_to_all | solution.py:596
  126.7 8.8 %all-to-all-done.19.recv_ref = f32[16,4,8,128]{3,2,1,0:T(8,128)S(1)} async-done(((f32[16,4,8,128]{3,2,1,0:T(8,128)}), f32[16,4,8,128]{3,2,1,0:T(8,128)S(1)}, u32[]{:S(2)}, u32[]{:S(2)}) %all-to-all-start.19) | async-done | bytes 262176 | tf_op jit(solution)/shard_map/all_to_all | solution.py:596
  (61 shorter events, 6.4 us)
Async XLA Ops:
  1.9 14.1 %copy-start.8 = (f32[4,256]{1,0:T(4,128)S(1)}, f32[4,256]{1,0:T(4,128)}, u32[]{:S(2)}) copy-start(f32[4,256]{1,0:T(4,128)} %param.20) | copy-start | bytes 12292
  1.9 14.8 %copy-start.7 = (bf16[4,3,256]{2,0,1:T(4,128)(2,1)S(1)}, bf16[4,3,256]{2,0,1:T(4,128)(2,1)}, u32[]{:S(2)}) copy-start(bf16[4,3,256]{2,0,1:T(4,128)(2,1)} %param.19) | copy-start | bytes 18436
  1.9 6.9 %collective-permute-start.66 = (f32[2,128]{1,0:T(2,128)S(1)}, f32[2,128]{1,0:T(2,128)S(1)}, u32[]{:S(2)}, u32[]{:S(2)}) collective-permute-start(f32[2,128]{1,0:T(2,128)S(1)} %select_n.49), channel_id=1, source_target_pairs={{0,4},{4,0},{1,5},{5,1},{2,6},{6,2},{3,7},{7,3},{8,12},{12,8},{9,1... | collective-permute-start | bytes 3080 | tf_op jit(solution)/shard_map/ppermute | solution.py:548
  5.9 10.8 %copy-start.6 = (f32[4,3,256]{2,0,1:T(4,128)S(1)}, f32[4,3,256]{2,0,1:T(4,128)}, u32[]{:S(2)}) copy-start(f32[4,3,256]{2,0,1:T(4,128)} %param.17) | copy-start | bytes 36868
  6.6 10.3 %copy-start.2 = (bf16[4,256,256]{2,1,0:T(8,128)(2,1)S(1)}, bf16[4,256,256]{2,1,0:T(8,128)(2,1)}, u32[]{:S(2)}) copy-start(bf16[4,256,256]{2,1,0:T(8,128)(2,1)} %param.18) | copy-start | bytes 1572868
  9.4 21.5 %all-to-all-start.16 = ((f32[16,9,8,128]{3,2,1,0:T(8,128)}), f32[16,9,8,128]{3,2,1,0:T(8,128)S(1)}, u32[]{:S(2)}, u32[]{:S(2)}) async-start(f32[16,9,8,128]{3,2,1,0:T(8,128)} %bitcast_dynamic-update-slice_fusion), calls=%async_computation.16 | async-start | bytes 1179648 | tf_op jit(solution)/shard_map/all_to_all | solution.py:556
  39.8 28.3 %collective-permute-start.67 = (f32[36,8,128]{2,1,0:T(8,128)S(1)}, f32[36,8,128]{2,1,0:T(8,128)S(1)}, u32[]{:S(2)}, u32[]{:S(2)}) collective-permute-start(f32[36,8,128]{2,1,0:T(8,128)S(1)} %get-tuple-element.238), channel_id=1, source_target_pairs={{0,1},{1,2},{2,3},{3,11},{11,10},{10,9},{9,8},{8,16},{16,17},{17,1... | collective-permute-start | bytes 442376 | tf_op jit(solution)/shard_map/ppermute | solution.py:539
  41.8 26.4 %collective-permute-start.68 = (f32[36,8,128]{2,1,0:T(8,128)S(1)}, f32[36,8,128]{2,1,0:T(8,128)S(1)}, u32[]{:S(2)}, u32[]{:S(2)}) collective-permute-start(f32[36,8,128]{2,1,0:T(8,128)S(1)} %get-tuple-element.237), channel_id=1, source_target_pairs={{1,0},{2,1},{3,2},{11,3},{10,11},{9,10},{8,9},{16,8},{17,16},{18,1... | collective-permute-start | bytes 442376 | tf_op jit(solution)/shard_map/ppermute | solution.py:539
  68.3 5.3 %collective-permute-start.70 = (f32[2,32,8,128]{3,2,1,0:T(8,128)S(1)}, f32[2,32,8,128]{3,2,1,0:T(8,128)S(1)}, u32[]{:S(2)}, u32[]{:S(2)}) collective-permute-start(f32[2,32,8,128]{3,2,1,0:T(8,128)S(1)} %rhs.2), channel_id=1, source_target_pairs={{1,0},{2,1},{3,2},{11,3},{10,11},{9,10},{8,9},{16,8},{17,16},{18,1... | collective-permute-start | bytes 786440 | tf_op jit(solution)/shard_map/ppermute | solution.py:539
  69.7 5.0 %collective-permute-start.69 = (f32[2,32,8,128]{3,2,1,0:T(8,128)S(1)}, f32[2,32,8,128]{3,2,1,0:T(8,128)S(1)}, u32[]{:S(2)}, u32[]{:S(2)}) collective-permute-start(f32[2,32,8,128]{3,2,1,0:T(8,128)S(1)} %rhs.2), channel_id=1, source_target_pairs={{0,1},{1,2},{2,3},{3,11},{11,10},{10,9},{9,8},{8,16},{16,17},{17,1... | collective-permute-start | bytes 786440 | tf_op jit(solution)/shard_map/ppermute | solution.py:539
  95.6 3.3 %collective-permute-start.71 = (f32[2,32,8,128]{3,2,1,0:T(8,128)S(1)}, f32[2,32,8,128]{3,2,1,0:T(8,128)S(1)}, u32[]{:S(2)}, u32[]{:S(2)}) collective-permute-start(f32[2,32,8,128]{3,2,1,0:T(8,128)S(1)} %get-tuple-element.52.refs_8_), channel_id=1, source_target_pairs={{0,1},{1,2},{2,3},{3,11},{11,10},{10,9},{9,8},{8,16},{16,17},{17,1... | collective-permute-start | bytes 786440 | tf_op jit(solution)/shard_map/ppermute | solution.py:539
  97.4 3.7 %collective-permute-start.72 = (f32[2,32,8,128]{3,2,1,0:T(8,128)S(1)}, f32[2,32,8,128]{3,2,1,0:T(8,128)S(1)}, u32[]{:S(2)}, u32[]{:S(2)}) collective-permute-start(f32[2,32,8,128]{3,2,1,0:T(8,128)S(1)} %get-tuple-element.52.refs_8_), channel_id=1, source_target_pairs={{1,0},{2,1},{3,2},{11,3},{10,11},{9,10},{8,9},{16,8},{17,16},{18,1... | collective-permute-start | bytes 786440 | tf_op jit(solution)/shard_map/ppermute | solution.py:539
  106.0 29.5 %copy-start.1 = (f32[8,32,128]{2,1,0:T(8,128)S(1)}, f32[8,32,128]{2,1,0:T(8,128)}, u32[]{:S(2)}) copy-start(f32[8,32,128]{2,1,0:T(8,128)} %u_ref.3) | copy-start | bytes 393220
  106.0 30.2 %copy-start = (f32[8,32,128]{2,1,0:T(8,128)S(1)}, f32[8,32,128]{2,1,0:T(8,128)}, u32[]{:S(2)}) copy-start(f32[8,32,128]{2,1,0:T(8,128)} %found_ref.1) | copy-start | bytes 393220
  106.0 30.2 %copy-start.3 = (s32[8,32,128]{2,1,0:T(8,128)S(1)}, s32[8,32,128]{2,1,0:T(8,128)}, u32[]{:S(2)}) copy-start(s32[8,32,128]{2,1,0:T(8,128)} %param.15) | copy-start | bytes 393220
  106.0 30.2 %copy-start.4 = (s32[8,32,128]{2,1,0:T(8,128)S(1)}, s32[8,32,128]{2,1,0:T(8,128)}, u32[]{:S(2)}) copy-start(s32[8,32,128]{2,1,0:T(8,128)} %param.16) | copy-start | bytes 393220
  106.0 30.2 %copy-start.5 = (f32[8,32,128]{2,1,0:T(8,128)S(1)}, f32[8,32,128]{2,1,0:T(8,128)}, u32[]{:S(2)}) copy-start(f32[8,32,128]{2,1,0:T(8,128)} %load_ref.1) | copy-start | bytes 393220
  122.0 13.5 %all-to-all-start.19 = ((f32[16,4,8,128]{3,2,1,0:T(8,128)}), f32[16,4,8,128]{3,2,1,0:T(8,128)S(1)}, u32[]{:S(2)}, u32[]{:S(2)}) async-start(f32[16,4,8,128]{3,2,1,0:T(8,128)} %get-tuple-element.58), calls=%async_computation.19 | async-start | bytes 524288 | tf_op jit(solution)/shard_map/all_to_all | solution.py:596
  136.3 0.7 copy-start.9
  136.9 0.7 copy-start.10

commit v2 on v1

--- a/solution.py
+++ b/solution.py
@@ -39,7 +39,8 @@
     return weight_in, weight_mid, weight_out
 
 
-def cells_kernel(families, planes, strain_ref, code_ref, in_ref, mid_ref, out_ref, answer_ref):
+def cells_kernel(families, planes, strain_ref, code_ref, in_ref, mid_ref, out_ref, *refs):
+    *edges, answer_ref = refs
     modes = in_ref.shape[0]
     spots = [(a, x) for a in range(code_ref.shape[0]) for x in planes]
     width = len(spots) * 128
@@ -51,7 +52,11 @@
         picked = lax.rem(place, families) == jnp.broadcast_to(family, place.shape)
         pieces = []
         for j in range(3):
-            value = jnp.broadcast_to(strain_ref[j, a, pl.ds(x, 1), :], place.shape)
+            value = strain_ref[j, a, pl.ds(x, 1), :]
+            if edges and j == 2:
+                part = edges[0 if x == 0 else 1][0, pl.ds(a, 1), :] * 0.5
+                value = value - part if x == 0 else value + part
+            value = jnp.broadcast_to(value, place.shape)
             high = value.astype(BF).astype(F32)
             piece = jnp.where(place < families, high, value - high)
             pieces.append(jnp.where(picked, piece, 0.0))
@@ -87,7 +92,7 @@
         answer_ref[:, a, x, :] = total[:, i * 128 : (i + 1) * 128]
 
 
-def cells(strain, code, packed, families, step, planes):
+def cells(strain, code, packed, families, step, planes, *edges):
     weight_in, weight_mid, weight_out = packed
     count = code.shape[0]
     planes = tuple(planes)
@@ -109,7 +114,8 @@
             whole(weight_in),
             whole(weight_mid),
             whole(weight_out),
-        ],
+        ]
+        + [pl.BlockSpec((1, 8, 128), lambda i: (count + i, 0, 0)) for _ in edges],
         out_specs=pl.BlockSpec((4, step, 8, 128), lambda i: (0, i, 0, 0)),
         out_shape=jax.ShapeDtypeStruct((4, count, 8, 128), F32),
         compiler_params=pltpu.CompilerParams(vmem_limit_bytes=48 * 2**20),
@@ -117,7 +123,7 @@
             flops=2 * points * modes * modes * (families + 1), bytes_accessed=points * 32, transcendentals=2 * points * modes
         ),
         name="cells",
-    )(strain, code, weight_in, weight_mid, weight_out)
+    )(strain, code, weight_in, weight_mid, weight_out, *edges)
 
 
 def global_sum(value):
@@ -216,29 +222,26 @@
     return result
 
 
-def spread_kernel(place_ref, u_ref, load_ref, found_ref, code_ref, send_ref, turned):
-    count = send_ref.shape[0]
+def place(slab, position, peers):
+    return position + slab * (peers - 1 - 2 * position)
+
+
+def spread_kernel(path, capacity, u_ref, load_ref, found_ref, slot_ref, flag_ref, send_ref, turned):
+    peers = len(path)
+    slab = lax.axis_index("slab")
+    code = jnp.zeros(slot_ref.shape, jnp.int32)
+    for family in range(1, 4):
+        code = code + jnp.where(slot_ref[...] >= family * capacity, 2, 0)
     rest = load_ref[...] - found_ref[...] * u_ref[...]
-    fields = (u_ref[...], code_ref[...].astype(F32), found_ref[...], rest)
+    fields = (u_ref[...], (code + flag_ref[...]).astype(F32), found_ref[...], rest)
     for number, field in enumerate(fields):
         for half in range(2):
-            turned[number, half, 8:136, :] = jnp.transpose(field[4 * half : 4 * half + 4].reshape(128, 128))
-    for half in range(2):
-        turned[0, half, 0:8, :] = jnp.zeros((8, 128), F32)
-        turned[0, half, 136:144, :] = jnp.zeros((8, 128), F32)
-    row = lax.broadcasted_iota(jnp.int32, (8, 128), 0)
-    for target in range(count):
-        start = pl.multiple_of(8 * place_ref[target], 8)
+            turned[number, half] = jnp.transpose(field[4 * half : 4 * half + 4].reshape(128, 128))
+    for target in range(peers):
+        start = pl.multiple_of(8 * place(slab, path[target], peers), 8)
         for number in range(4):
             for half in range(2):
-                send_ref[target, 2 * number + half] = turned[number, half, pl.ds(start + 8, 8), :]
-        edges = jnp.zeros((8, 128), F32)
-        for half in range(2):
-            low = turned[0, half, pl.ds(start, 8), :]
-            high = turned[0, half, pl.ds(start + 16, 8), :]
-            edges = jnp.where(row == half, jnp.broadcast_to(low[7:8], (8, 128)), edges)
-            edges = jnp.where(row == 2 + half, jnp.broadcast_to(high[0:1], (8, 128)), edges)
-        send_ref[target, 8] = edges
+                send_ref[target, 2 * number + half] = turned[number, half, pl.ds(start, 8), :]
 
 
 def beside(tile, low, high):
@@ -255,10 +258,8 @@
     return (after - before) * 0.5
 
 
-def collect_kernel(around, recv_ref, strain_ref, code_ref, found_ref, rest_ref, u):
-    along = recv_ref.shape[0] // 4
-    edges = []
-    for b in range(along):
+def collect_kernel(around, recv_ref, strain_ref, code_ref, found_ref, rest_ref, next_ref, previous_ref, u):
+    for b in range(around // 8):
         for half in range(2):
             for number in range(4):
                 tiles = regroup([recv_ref[4 * b + m, 2 * number + half] for m in range(4)])
@@ -270,29 +271,33 @@
                         code_ref[at] = tiles[a].astype(jnp.int32)
                     elif number == 2:
                         found_ref[at] = tiles[a]
+                        next_ref[at] = tiles[a]
+                        previous_ref[at] = tiles[a]
                     else:
                         rest_ref[at] = tiles[a]
-        edges.append(regroup([recv_ref[4 * b + m, 8] for m in range(4)]))
+    nothing = jnp.zeros((1, 128), F32)
     for at in range(around):
         tile = u[at]
         strain_ref[0, at] = (u[(at + 1) % around] - u[(at - 1) % around]) * 0.5
         strain_ref[1, at] = radial(tile)
-        edge, half = edges[at // 8][at % 4], at % 8 // 4
-        after, before = beside(tile, edge[half : half + 1], edge[2 + half : 3 + half])
+        after, before = beside(tile, nothing, nothing)
         strain_ref[2, at] = (after - before) * 0.5
-
-
-def rhs_kernel(around, outer_ref, inner_ref, rest_ref, low_ref, high_ref, own_ref):
+        next_ref[around + at // 8, pl.ds(at % 8, 1), :] = tile[7:8]
+        previous_ref[around + at // 8, pl.ds(at % 8, 1), :] = tile[0:1]
+
+
+def rhs_kernel(around, first_ref, outer_ref, second_ref, rest_ref, low_ref, high_ref, own_ref):
     row = lax.broadcasted_iota(jnp.int32, (8, 128), 0)
     rim = (row == 0) | (row == 7)
 
     def answer(number, at):
-        return jnp.where(rim, outer_ref[number, at], inner_ref[number, at])
+        inner = jnp.where(row < 4, first_ref[number, at], second_ref[number, at])
+        return jnp.where(rim, outer_ref[number, at], inner)
 
     cycle = [answer(0, at) for at in range(around)]
     for at in range(around):
-        low = low_ref[around + at // 8, pl.ds(at % 8, 1), :]
-        high = high_ref[around + at // 8, pl.ds(at % 8, 1), :]
+        low = low_ref[at // 8, pl.ds(at % 8, 1), :]
+        high = high_ref[at // 8, pl.ds(at % 8, 1), :]
         after, before = beside(answer(2, at), low, high)
         divergence = (cycle[(at + 1) % around] - cycle[(at - 1) % around]) * 0.5
         divergence = divergence + radial(answer(1, at)) + (after - before) * 0.5
@@ -304,9 +309,14 @@
 
 
 def basis_kernel(
-    around, seeds, ends_ref, scale_ref, tan_ref, tan_low_ref, tan_high_ref, found_ref, found_low_ref, found_high_ref,
-    seed_ref, seed_low_ref, seed_high_ref, own_ref, gram_ref, tan, main, off_a, off_r, back_r, off_x, back_x, vectors
+    around, last, ends_ref, scale_ref, tan_ref, tan_low_ref, tan_high_ref, found_ref, found_low_ref, found_high_ref,
+    seed_ref, seed_low_ref, seed_high_ref, *refs
 ):
+    if last:
+        earlier_ref, own_ref, gram_ref, *scratch = refs
+    else:
+        own_ref, *scratch = refs
+    tan, main, off_r, back_r, off_x, back_x, vectors = scratch
     centre, inverse = scale_ref[0], scale_ref[1]
     lane = lax.broadcasted_iota(jnp.int32, (24, 128), 1)
     plane = lax.broadcasted_iota(jnp.int32, (24, 128), 0)
@@ -342,30 +352,34 @@
         result = result - off_r[at] * pltpu.roll(value, 126, 1) - back_r[at] * pltpu.roll(value, 2, 1)
         return result - off_x[at] * pltpu.roll(value, 22, 0) - back_x[at] * pltpu.roll(value, 2, 0)
 
-    size = HALF + 1
-    for seed in range(seeds):
-        base = seed * size
+    for at in range(around):
+        vectors[0, at] = three(seed_low_ref[at], seed_ref[at], seed_high_ref[at])
+    for degree in range(1, HALF + 1):
         for at in range(around):
-            vectors[base, at] = three(seed_low_ref[seed, at], seed_ref[seed, at], seed_high_ref[seed, at])
-        for degree in range(1, size):
-            for at in range(around):
-                value = apply(base + degree - 1, at)
-                if degree > 1:
-                    value = value + value - vectors[base + degree - 2, at]
-                vectors[base + degree, at] = value
-    total = seeds * size
-    for index in range(total):
+            value = apply(degree - 1, at)
+            if degree > 1:
+                value = value + value - vectors[degree - 2, at]
+            vectors[degree, at] = value
+    skipped = 1 if last else 0
+    for index in range(skipped, HALF + 1):
         for at in range(around):
-            own_ref[index, at] = vectors[index, at, 8:16, :]
+            own_ref[index - skipped, at] = vectors[index, at, 8:16, :]
+    if not last:
+        return
+    total = 2 * HALF + 1
     column = lax.broadcasted_iota(jnp.int32, (1, 128), 1)
     gram = jnp.zeros((1, 128), F32)
     number = 0
+
+    def own(index, at):
+        return earlier_ref[index, at] if index <= HALF else own_ref[index - HALF - 1, at]
+
     for i in range(total):
         sums = [jnp.zeros((8, 128), F32)] * (total - i)
         for at in range(around):
-            left = own_ref[i, at]
+            left = own(i, at)
             for j in range(i, total):
-                sums[j - i] = sums[j - i] + left * own_ref[j, at]
+                sums[j - i] = sums[j - i] + left * own(j, at)
         for value in sums:
             entry = jnp.sum(jnp.sum(value, axis=0, keepdims=True), axis=1, keepdims=True)
             gram = jnp.where(column == number, jnp.broadcast_to(entry, (1, 128)), gram)
@@ -407,30 +421,35 @@
     return result
 
 
-def times_operator(vector, centre, half_width, size):
-    result = []
+def times_operator(vector, centre, half_width):
+    total = len(vector)
+    result = [None] * total
     half = 0.5 * half_width
-    for base in range(0, len(vector), size):
-        part = vector[base : base + size]
-        for j in range(size):
-            terms = []
-            if part[j] is not None:
-                terms.append(centre * part[j])
-            if j > 0 and part[j - 1] is not None:
-                terms.append((half_width if j == 1 else half) * part[j - 1])
-            if j + 1 < size and part[j + 1] is not None:
-                terms.append(half * part[j + 1])
-            result.append(sum(terms[1:], terms[0]) if terms else None)
+
+    def add(index, term):
+        result[index] = term if result[index] is None else result[index] + term
+
+    for j, c in enumerate(vector):
+        if c is None:
+            continue
+        add(j, centre * c)
+        if j in (0, HALF):
+            add(j + 1, half_width * c)
+        else:
+            add(j + 1, half * c)
+            add(j - 1, half * c)
     return result
 
 
-def iterate(gram, total, residual, direction, current, centre, half_width, worst):
-    size = HALF + 1
+def iterate(gram, total, centre, half_width):
+    residual = [jnp.ones((1, 128), F32)] + [None] * (total - 1)
+    direction = residual
     change = [None] * total
     norms = [jnp.sqrt(gram[i, i]) for i in range(total)]
-    before = current
-    for step in range(HALF):
-        image = times_operator(direction, centre, half_width, size)
+    current = gram[0, 0]
+    worst = jnp.zeros((1, 128), F32)
+    for step in range(ITERS):
+        image = times_operator(direction, centre, half_width)
         alpha = current / dot(gram, direction, image)
         change = axpy(alpha, direction, change)
         residual = axpy(-alpha, image, residual)
@@ -441,68 +460,39 @@
                 bound = jnp.abs(c) * n if bound is None else bound + jnp.abs(c) * n
         worst = jnp.maximum(worst, bound * bound / following)
         worst = jnp.where(following > 0.0, worst, jnp.inf)
-        before = current
-        if step < HALF - 1:
+        if step < ITERS - 1:
             direction = axpy(following / current, direction, residual)
         current = following
-    return change, residual, direction, before, current, worst
-
-
-def combine(coefficients, own_ref, at):
+    return change, residual, worst
+
+
+def combine(coefficients, early_ref, late_ref, at):
     result = None
     for index, c in enumerate(coefficients):
         if c is not None:
-            term = jnp.broadcast_to(c, (8, 128)) * own_ref[index, at]
-            result = term if result is None else result + term
+            vector = early_ref[index, at] if index <= HALF else late_ref[index - HALF - 1, at]
+            result = c * vector if result is None else result + c * vector
     return result
 
 
-def middle_kernel(around, scale_ref, all_ref, own_ref, seeds_ref, change_ref, state_ref):
-    total = HALF + 1
-    gram = unpack_gram(all_ref, total)
-    one = [jnp.ones((1, 128), F32)] + [None] * HALF
-    nothing = jnp.zeros((1, 128), F32)
-    change, residual, direction, before, _, worst = iterate(
-        gram, total, one, one, gram[0, 0], scale_ref[0], scale_ref[2], nothing
-    )
-    for at in range(around):
-        seeds_ref[0, at] = combine(residual, own_ref, at)
-        seeds_ref[1, at] = combine(direction, own_ref, at)
-        change_ref[at] = combine(change, own_ref, at)
-    state_ref[...] = jnp.concatenate([before, worst] + [nothing] * 6, axis=0)
-
-
-def last_kernel(around, scale_ref, all_ref, own_ref, change_ref, state_ref, send_ref, worst_ref):
-    size = HALF + 1
-    total = 2 * size
-    gram = unpack_gram(all_ref, total)
-    ones = jnp.ones((1, 128), F32)
-    residual = [ones] + [None] * (total - 1)
-    beta = gram[0, 0] / state_ref[0:1, :]
-    direction = list(residual)
-    direction[size] = beta
-    change, residual, _, _, _, worst = iterate(
-        gram, total, residual, direction, gram[0, 0], scale_ref[0], scale_ref[2], state_ref[1:2, :]
-    )
+def last_kernel(around, scale_ref, all_ref, early_ref, late_ref, send_ref, worst_ref):
+    total = 2 * HALF + 1
+    change, residual, worst = iterate(unpack_gram(all_ref, total), total, scale_ref[0], scale_ref[2])
     worst_ref[...] = jnp.broadcast_to(worst, (8, 128))
+    pairs = [[None if c is None else jnp.broadcast_to(c, (8, 128)) for c in part] for part in (change, residual)]
     for b in range(around // 8):
         for half in range(2):
             for number in range(2):
-                tiles = []
-                for a in range(4):
-                    at = 8 * b + 4 * half + a
-                    if number == 0:
-                        tiles.append(change_ref[at] + combine(change, own_ref, at))
-                    else:
-                        tiles.append(combine(residual, own_ref, at))
+                tiles = [combine(pairs[number], early_ref, late_ref, 8 * b + 4 * half + a) for a in range(4)]
                 tiles = regroup(tiles)
                 for m in range(4):
                     send_ref[4 * b + m, 2 * number + half] = tiles[m]
 
 
-def deliver_kernel(place_ref, u_ref, recv_ref, updated_ref, residual_ref, turned):
+def deliver_kernel(path, u_ref, recv_ref, updated_ref, residual_ref, turned):
+    slab = lax.axis_index("slab")
     for source in range(recv_ref.shape[0]):
-        start = pl.multiple_of(8 * place_ref[source], 8)
+        start = pl.multiple_of(8 * place(slab, path[source], len(path)), 8)
         for index in range(4):
             turned[index, pl.ds(start, 8), :] = recv_ref[source, index]
     for half in range(2):
@@ -522,16 +512,14 @@
     everyone = peers * lax.axis_size("slab")
     slab = lax.axis_index("slab")
     path = [b * across + (m if b % 2 == 0 else across - 1 - m) for b in range(along) for m in range(across)]
-    forth = jnp.array(path, jnp.int32)
-    place = jnp.where(slab == 0, forth, peers - 1 - forth)
-    mine = jnp.take(place, lax.axis_index("blk") * across + lax.axis_index("micro")) + peers * slab
+    forth = jnp.array(path, jnp.int32)[lax.axis_index("blk") * across + lax.axis_index("micro")]
+    mine = place(slab, forth, peers) + peers * slab
     ends = jnp.stack([(mine == 0), (mine == everyone - 1)]).astype(jnp.int32)
     spots = [0] * everyone
     for b in range(along):
         for s in range(2):
             for m in range(across):
-                position = path[b * across + m]
-                spots[position if s == 0 else 2 * peers - 1 - position] = (b * 2 + s) * across + m
+                spots[place(s, path[b * across + m], peers) + peers * s] = (b * 2 + s) * across + m
     rising = [(spots[i], spots[i + 1]) for i in range(everyone - 1)]
     falling = [(b, a) for a, b in rising]
 
@@ -540,69 +528,62 @@
 
     packed = pack_families(family_in, family_mid, family_out, family_tan)
     typical = 0.5 + 0.33 * jnp.mean(jnp.sum(family_tan, axis=1))
-    centre = 1.1 + 1.5 * typical
-    half_width = centre - 0.2
+    centre = 1.1 + 1.4 * typical
+    half_width = centre - 0.4
     scale = jnp.stack([centre, 1.0 / half_width, half_width])
 
-    rim = jnp.where(slab == 0, displacement[:, :, size_z - 1], displacement[:, :, 0]).reshape(2, 128)
-    rim = lax.ppermute(rim, "slab", [(0, 1), (1, 0)])
-    code = 2 * (point_slot // (size_x * size_y * size_z // 2)) + plastic_flags
+    capacity = size_x * size_y * size_z // 2
     (send,) = call(
-        spread_kernel, [((peers, 9, 8, 128), F32)], [pltpu.VMEM((4, 2, 144, 128), F32)], "spread",
-        place, displacement, load_field, foundation, code, smem=1,
-    )
-    middle = path.index(peers - 1)
-    send = lax.dynamic_update_slice(send, rim[None, None], (middle, 8, jnp.where(slab == 0, 2, 0), 0))
+        lambda *refs: spread_kernel(path, capacity, *refs),
+        [((peers, 8, 8, 128), F32)], [pltpu.VMEM((4, 2, 128, 128), F32)], "spread",
+        displacement, load_field, foundation, point_slot, plastic_flags,
+    )
     recv = lax.all_to_all(send, GROUP, 0, 0, tiled=True)
     field = (around, 8, 128)
-    strain, code, found, rest = call(
+    edge = (around // 8, 8, 128)
+    message = (around + around // 8, 8, 128)
+    strain, code, found, rest, to_next, to_previous = call(
         lambda *refs: collect_kernel(around, *refs),
-        [((3,) + field, F32), (field, jnp.int32), (field, F32), (field, F32)],
+        [((3,) + field, F32), (field, jnp.int32), (field, F32), (field, F32), (message, F32), (message, F32)],
         [pltpu.VMEM(field, F32)], "collect", recv,
     )
-    outer = cells(strain, code, packed, families, 8, (0, 7))
-    rows = (around // 8, 8, 128)
-    low, high = neighbours(
-        jnp.concatenate([found, outer[2, :, 7].reshape(rows)]), jnp.concatenate([found, outer[2, :, 0].reshape(rows)])
-    )
-    inner = cells(strain, code, packed, families, 4, range(1, 7))
+    low, high = neighbours(to_next, to_previous)
+    first = cells(strain, code, packed, families, 8, (1, 2, 3))
+    outer = cells(strain, code, packed, families, 8, (0, 7), low, high)
+    edge_low, edge_high = neighbours(outer[2, :, 7].reshape(edge), outer[2, :, 0].reshape(edge))
+    second = cells(strain, code, packed, families, 8, (4, 5, 6))
     (own,) = call(
-        lambda *refs: rhs_kernel(around, *refs), [((2,) + field, F32)], [], "rhs", outer, inner, rest, low, high
+        lambda *refs: rhs_kernel(around, *refs), [((2,) + field, F32)], [], "rhs",
+        first, outer, second, rest, edge_low, edge_high,
     )
     own_low, own_high = neighbours(own, own)
 
-    def basis(seeds, tangents, vectors):
-        tall = pltpu.VMEM((around, 24, 128), F32)
-        total = seeds * (HALF + 1)
-        products, gram = call(
-            lambda *refs: basis_kernel(around, seeds, *refs),
-            [((total,) + field, F32), ((1, 128), F32)],
-            [tall] * 7 + [pltpu.VMEM((total, around, 24, 128), F32)],
-            "basis", ends, scale, *tangents, found, low, high, *vectors, smem=2,
+    def basis(last, outputs, *vectors):
+        return call(
+            lambda *refs: basis_kernel(around, last, *refs), outputs,
+            [pltpu.VMEM((around, 24, 128), F32)] * 6 + [pltpu.VMEM((HALF + 1, around, 24, 128), F32)],
+            "basis", ends, scale, own[1], own_low[1], own_high[1], found, low, high, *vectors, smem=2,
         )
-        return products, lax.all_to_all(jnp.broadcast_to(gram, (everyone, 128)), AXES, 0, 0, tiled=True)
-
-    tangents = (own[1], own_low[1], own_high[1])
-    first, sums = basis(1, tangents, (own[:1], own_low[:1], own_high[:1]))
-    seeds, change, state = call(
-        lambda *refs: middle_kernel(around, *refs),
-        [((2,) + field, F32), (field, F32), ((8, 128), F32)], [], "middle", scale, sums, first, smem=1,
-    )
-    second, sums = basis(2, tangents, (seeds, *neighbours(seeds, seeds)))
+
+    (early,) = basis(False, [((HALF + 1,) + field, F32)], own[0], own_low[0], own_high[0])
+    late, gram = basis(
+        True, [((HALF,) + field, F32), ((1, 128), F32)], early[HALF], *neighbours(early[HALF], early[HALF]), early
+    )
+    sums = lax.all_to_all(jnp.broadcast_to(gram, (everyone, 128)), AXES, 0, 0, tiled=True)
     send, worst = call(
         lambda *refs: last_kernel(around, *refs),
-        [((peers, 4, 8, 128), F32), ((8, 128), F32)], [], "last", scale, sums, second, change, state, smem=1,
+        [((peers, 4, 8, 128), F32), ((8, 128), F32)], [], "last", scale, sums, early, late, smem=1,
     )
     recv = lax.all_to_all(send, GROUP, 0, 0, tiled=True)
     shape = displacement.shape
     updated, residual = call(
-        deliver_kernel, [(shape, F32), (shape, F32)], [pltpu.VMEM((4, 128, 128), F32)], "deliver",
-        place, displacement, recv, smem=1,
+        lambda *refs: deliver_kernel(path, *refs),
+        [(shape, F32), (shape, F32)], [pltpu.VMEM((4, 128, 128), F32)], "deliver", displacement, recv,
     )
     return updated, residual, worst[0, 0]
 
 
-MOST_LOST = 3000.0
+MOST_LOST = 1.0e5
 
 
 def body(*inputs):
@@ -613,6 +594,7 @@
         and across == 4
         and size_z == 8 * along * across
         and lax.axis_size("slab") == 2
+        and inputs[5].shape[0] == 4
     )
     if not fits:
         return plain_body(*inputs)

time: 138 us -> 126 us (0.913)
  blocking collectives: 30.5 us -> 15.1 us
  starting transfers between devices: 24.1 us -> 32.4 us
  other arithmetic: 3.68 us -> 0.78 us
  Pallas kernels: 48.2 us -> 45.7 us
  waiting for transfers between devices: 24.6 us -> 22.7 us
    all_to_all x2 -> x1, blocking collectives: 30.5 us -> 15.1 us  [sliced_body(): lax.all_to_all(jnp.broadcast_to(gram, (everyone, 128)), AXES, 0, 0, tiled...]
    ppermute x3 -> x4, starting transfers between devices: 7.56 us -> 15.9 us  [neighbours(): lax.ppermute(to_next, AXES, rising)]
    all_to_all x2, waiting for transfers between devices: 21.4 us -> 17.6 us  [sliced_body(): recv = lax.all_to_all(send, GROUP, 0, 0, tiled=True)]
    ppermute x1 -> x0, starting transfers between devices: 2.97 us -> none  [sliced_body(): rim = lax.ppermute(rim, 'slab', [(0, 1), (1, 0)])]
    ppermute x3 -> x4, waiting for transfers between devices: 2.21 us -> 5.05 us  [neighbours(): lax.ppermute(to_previous, AXES, falling)]
    pallas_call x8 -> x7, Pallas kernels: 14.8 us -> 12.3 us  [call(): pl.pallas_call(kernel, out_shape=[jax.ShapeDtypeStruct(shape, dtype) for...]
    unnamed x25 -> x27, local copies, waits for them, and re-layouts: 1.36 us -> 3.34 us
    select_n x2 -> x0, other arithmetic: 1.83 us -> none  [the longest x1 1.16 us: sliced_body(): jnp.where(slab == 0, displacement[:, :, size_z - 1], displacement[:, :, 0])]
  transfers between devices with their start and end apart: 9 -> 10, of which waited for: 4 -> 4; matrix products, arithmetic and copies ran while one was open for 3% -> 2% of each run, Pallas kernels for 20% -> 20%
where the time goes in v2:
time: 126 us; the launch traced here: 125 us
  Pallas kernels  45.7 us (36%)
  starting transfers between devices  32.4 us (26%)
  waiting for transfers between devices  22.7 us (18%)
  blocking collectives  15.1 us (12%)
  local copies, waits for them, and re-layouts  4.78 us (4%)
  between operations  3.72 us (3%)
    pallas_call x3, Pallas kernels, cells(): pl.pallas_call(kernel, grid=(count // step,), in_specs=[pl.BlockSpec((3,...  33.4 us
    all_to_all x2, waiting for transfers between devices, sliced_body(): recv = lax.all_to_all(send, GROUP, 0, 0, tiled=True)  17.6 us
    ppermute x4, starting transfers between devices, neighbours(): lax.ppermute(to_next, AXES, rising)  15.9 us
    all_to_all x1, blocking collectives, sliced_body(): lax.all_to_all(jnp.broadcast_to(gram, (everyone, 128)), AXES, 0, 0, tiled...  15.1 us
    pallas_call x7, Pallas kernels, call(): pl.pallas_call(kernel, out_shape=[jax.ShapeDtypeStruct(shape, dtype) for...  12.3 us
    all_to_all x2, starting transfers between devices, sliced_body(): recv = lax.all_to_all(send, GROUP, 0, 0, tiled=True)  11.2 us
    ppermute x4, starting transfers between devices, neighbours(): lax.ppermute(to_previous, AXES, falling)  5.34 us
    ppermute x4, waiting for transfers between devices, neighbours(): lax.ppermute(to_previous, AXES, falling)  5.05 us
  transfers between devices with their start and end apart: 10, of which 4 were waited for; matrix products, arithmetic and copies ran while one was open for 2% of the time, Pallas kernels for 20%

profile of v2, /device:TPU:0, one launch (start us, length us, event | category | flops | bytes accessed | tf_op | source)
XLA Modules:
  0.0 125.2 jit_solution(13325426946072027085)
XLA Ops:
  0.6 2.2 %spread.1 = f32[16,8,8,128]{3,2,1,0:T(8,128)} custom-call(f32[8,32,128]{2,1,0:T(8,128)} %refs_0_.3, f32[8,32,128]{2,1,0:T(8,128)} %refs_1_.1, f32[8,32,128]{2,1,0:T(8,128)} %refs_2_.1, s32[8,32,128]{2,1,0:T(8,128)} %refs_3_.1, s32[8,32,128]{2,1,0:T(8,128)} %refs_4_.1), custom_call_target="tpu_custom_call" | custom-call | tf_op jit(solution)/shard_map/spread/pallas_call | solution.py:201
  2.9 7.5 %all-to-all-start.16 = ((f32[16,8,8,128]{3,2,1,0:T(8,128)}), f32[16,8,8,128]{3,2,1,0:T(8,128)S(1)}, u32[]{:S(2)}, u32[]{:S(2)}) async-start(f32[16,8,8,128]{3,2,1,0:T(8,128)} %spread.1), calls=%async_computation.16 | async-start | bytes 1048576 | tf_op jit(solution)/shard_map/all_to_all | solution.py:541
  10.4 0.7 copy-done.8
  15.2 0.7 copy-done.7
  16.1 8.8 %all-to-all-done.16.refs_0_ = f32[16,8,8,128]{3,2,1,0:T(8,128)S(1)} async-done(((f32[16,8,8,128]{3,2,1,0:T(8,128)}), f32[16,8,8,128]{3,2,1,0:T(8,128)S(1)}, u32[]{:S(2)}, u32[]{:S(2)}) %all-to-all-start.16) | async-done | bytes 524320 | tf_op jit(solution)/shard_map/all_to_all | solution.py:541
  25.4 1.9 %collective-permute-start.66 = (f32[36,8,128]{2,1,0:T(8,128)S(1)}, f32[36,8,128]{2,1,0:T(8,128)S(1)}, u32[]{:S(2)}, u32[]{:S(2)}) collective-permute-start(f32[36,8,128]{2,1,0:T(8,128)S(1)} %get-tuple-element.45), channel_id=1, source_target_pairs={{0,1},{1,2},{2,3},{3,11},{11,10},{10,9},{9,8},{8,16},{16,17},{17,1... | collective-permute-start | bytes 442376 | tf_op jit(solution)/shard_map/ppermute | solution.py:527
  27.3 1.3 %collective-permute-start.67 = (f32[36,8,128]{2,1,0:T(8,128)S(1)}, f32[36,8,128]{2,1,0:T(8,128)S(1)}, u32[]{:S(2)}, u32[]{:S(2)}) collective-permute-start(f32[36,8,128]{2,1,0:T(8,128)S(1)} %get-tuple-element.46), channel_id=1, source_target_pairs={{1,0},{2,1},{3,2},{11,3},{10,11},{9,10},{8,9},{16,8},{17,16},{18,1... | collective-permute-start | bytes 442376 | tf_op jit(solution)/shard_map/ppermute | solution.py:527
  28.6 12.6 %cells.5.refs_0_ = f32[4,32,8,128]{3,2,1,0:T(8,128)S(1)} custom-call(f32[3,32,8,128]{3,2,1,0:T(8,128)S(1)} %get-tuple-element.43.refs_0_, s32[32,8,128]{2,1,0:T(8,128)S(1)} %get-tuple-element.44.refs_1_, bf16[256,48]{1,0:T(8,128)(2,1)S(1)} %copy.85.refs_2_, bf16[256,1024]{1,0:T(8,128)(2,1)S(1)} %bitcast.85, bf16[32,768]{1,0:T(8,128)(2,1)S(1)} %maximum_maximum_fusion.1.refs_4_), custom_call_target="tpu_custom_call" | custom-call | flops 8053063680 | bytes 393216 | tf_op jit(solution)/shard_map/cells/pallas_call | solution.py:108
  41.2 8.3 %cells.6.refs_1_ = f32[4,32,8,128]{3,2,1,0:T(8,128)S(1)} custom-call(f32[3,32,8,128]{3,2,1,0:T(8,128)S(1)} %get-tuple-element.43.refs_0_, s32[32,8,128]{2,1,0:T(8,128)S(1)} %get-tuple-element.44.refs_1_, bf16[256,48]{1,0:T(8,128)(2,1)S(1)} %copy.85.refs_2_, bf16[256,1024]{1,0:T(8,128)(2,1)S(1)} %bitcast.86, ...), custom_call_target="tpu_custom_call" | custom-call | flops 5368709120 | bytes 262144 | tf_op jit(solution)/shard_map/cells/pallas_call | solution.py:108
  49.6 3.0 %collective-permute-start.68 = (f32[4,8,128]{2,1,0:T(8,128)S(1)}, f32[4,8,128]{2,1,0:T(8,128)S(1)}, u32[]{:S(2)}, u32[]{:S(2)}) collective-permute-start(f32[4,8,128]{2,1,0:T(8,128)S(1)} %bitcast.140), channel_id=1, source_target_pairs={{0,1},{1,2},{2,3},{3,11},{11,10},{10,9},{9,8},{8,16},{16,17},{17,1... | collective-permute-start | bytes 49160 | tf_op jit(solution)/shard_map/ppermute | solution.py:527
  52.6 1.3 %collective-permute-start.69 = (f32[4,8,128]{2,1,0:T(8,128)S(1)}, f32[4,8,128]{2,1,0:T(8,128)S(1)}, u32[]{:S(2)}, u32[]{:S(2)}) collective-permute-start(f32[4,8,128]{2,1,0:T(8,128)S(1)} %bitcast.139), channel_id=1, source_target_pairs={{1,0},{2,1},{3,2},{11,3},{10,11},{9,10},{8,9},{16,8},{17,16},{18,1... | collective-permute-start | bytes 49160 | tf_op jit(solution)/shard_map/ppermute | solution.py:527
  53.9 12.6 %cells.7.refs_2_ = f32[4,32,8,128]{3,2,1,0:T(8,128)S(1)} custom-call(f32[3,32,8,128]{3,2,1,0:T(8,128)S(1)} %get-tuple-element.43.refs_0_, s32[32,8,128]{2,1,0:T(8,128)S(1)} %get-tuple-element.44.refs_1_, bf16[256,48]{1,0:T(8,128)(2,1)S(1)} %copy.85.refs_2_, bf16[256,1024]{1,0:T(8,128)(2,1)S(1)} %bitcast.87, bf16[32,768]{1,0:T(8,128)(2,1)S(1)} %maximum_maximum_fusion.1.refs_4_), custom_call_target="tpu_custom_call" | custom-call | flops 8053063680 | bytes 393216 | tf_op jit(solution)/shard_map/cells/pallas_call | solution.py:108
  66.7 4.3 %collective-permute-start.70 = (f32[2,32,8,128]{3,2,1,0:T(8,128)S(1)}, f32[2,32,8,128]{3,2,1,0:T(8,128)S(1)}, u32[]{:S(2)}, u32[]{:S(2)}) collective-permute-start(f32[2,32,8,128]{3,2,1,0:T(8,128)S(1)} %rhs.1), channel_id=1, source_target_pairs={{0,1},{1,2},{2,3},{3,11},{11,10},{10,9},{9,8},{8,16},{16,17},{17,1... | collective-permute-start | bytes 786440 | tf_op jit(solution)/shard_map/ppermute | solution.py:527
  71.0 1.3 %collective-permute-start.71 = (f32[2,32,8,128]{3,2,1,0:T(8,128)S(1)}, f32[2,32,8,128]{3,2,1,0:T(8,128)S(1)}, u32[]{:S(2)}, u32[]{:S(2)}) collective-permute-start(f32[2,32,8,128]{3,2,1,0:T(8,128)S(1)} %rhs.1), channel_id=1, source_target_pairs={{1,0},{2,1},{3,2},{11,3},{10,11},{9,10},{8,9},{16,8},{17,16},{18,1... | collective-permute-start | bytes 786440 | tf_op jit(solution)/shard_map/ppermute | solution.py:527
  72.4 3.3 %collective-permute-done.71 = f32[2,32,8,128]{3,2,1,0:T(8,128)S(1)} collective-permute-done((f32[2,32,8,128]{3,2,1,0:T(8,128)S(1)}, f32[2,32,8,128]{3,2,1,0:T(8,128)S(1)}, u32[]{:S(2)}, u32[]{:S(2)}) %collective-permute-start.71) | collective-permute-done | bytes 262176 | tf_op jit(solution)/shard_map/ppermute | solution.py:527
  75.7 3.3 %basis.2.refs_11_.refs_2_ = f32[5,32,8,128]{3,2,1,0:T(8,128)S(1)} custom-call(s32[2]{0:T(128)S(1)} %add_convert_fusion.refs_0_, f32[3]{0:T(128)S(1)} %pad_maximum_fusion.18.refs_1_.refs_0_, f32[32,8,128]{2,1,0:T(8,128)S(1)} %get-tuple-element.219.refs_2_, f32[32,8,128]{2,1,0:T(8,128)S(1)} %get-tuple-element.217.refs_3_, ...), custom_call_target="tpu_custom_call" | custom-call | tf_op jit(solution)/shard_map/basis/pallas_call | solution.py:201
  79.0 6.7 %collective-permute-start.72 = (f32[32,8,128]{2,1,0:T(8,128)S(1)}, f32[32,8,128]{2,1,0:T(8,128)S(1)}, u32[]{:S(2)}, u32[]{:S(2)}) collective-permute-start(f32[32,8,128]{2,1,0:T(8,128)S(1)} %slice_bitcast_fusion.4.refs_8_), channel_id=1, source_target_pairs={{0,1},{1,2},{2,3},{3,11},{11,10},{10,9},{9,8},{8,16},{16,17},{17,1... | collective-permute-start | bytes 393224 | tf_op jit(solution)/shard_map/ppermute | solution.py:527
  85.7 1.5 %collective-permute-start.73 = (f32[32,8,128]{2,1,0:T(8,128)S(1)}, f32[32,8,128]{2,1,0:T(8,128)S(1)}, u32[]{:S(2)}, u32[]{:S(2)}) collective-permute-start(f32[32,8,128]{2,1,0:T(8,128)S(1)} %slice_bitcast_fusion.4.refs_8_), channel_id=1, source_target_pairs={{1,0},{2,1},{3,2},{11,3},{10,11},{9,10},{8,9},{16,8},{17,16},{18,1... | collective-permute-start | bytes 393224 | tf_op jit(solution)/shard_map/ppermute | solution.py:527
  87.2 1.8 %collective-permute-done.73.refs_10_ = f32[32,8,128]{2,1,0:T(8,128)S(1)} collective-permute-done((f32[32,8,128]{2,1,0:T(8,128)S(1)}, f32[32,8,128]{2,1,0:T(8,128)S(1)}, u32[]{:S(2)}, u32[]{:S(2)}) %collective-permute-start.73) | collective-permute-done | bytes 131104 | tf_op jit(solution)/shard_map/ppermute | solution.py:527
  89.0 4.0 %basis.3 = (f32[4,32,8,128]{3,2,1,0:T(8,128)S(1)}, f32[1,128]{1,0:T(1,128)S(1)}) custom-call(s32[2]{0:T(128)S(1)} %add_convert_fusion.refs_0_, f32[3]{0:T(128)S(1)} %pad_maximum_fusion.18.refs_1_.refs_0_, f32[32,8,128]{2,1,0:T(8,128)S(1)} %get-tuple-element.219.refs_2_, f32[32,8,128]{2,1,0:T(8,128)S(1)} %get-tuple-element.217.refs_3_, ...), custom_call_target="tpu_custom_call" | custom-call | tf_op jit(solution)/shard_map/basis/pallas_call | solution.py:201
  92.9 15.1 %all_to_all.145 = f32[32,1,128]{2,1,0:T(1,128)S(1)} all-to-all(f32[32,1,128]{2,1,0:T(1,128)S(1)} %broadcast_in_dim.44), channel_id=1, replica_groups=mesh['blk'=4,'slab'=2,'micro'=4] {'blk','slab','micro'}, dimensions={0} | all-to-all | bytes 32768 | tf_op jit(solution)/shard_map/all_to_all | solution.py:572
  108.0 2.0 %last.1 = (f32[16,4,8,128]{3,2,1,0:T(8,128)}, f32[8,128]{1,0:T(8,128)S(1)}) custom-call(f32[3]{0:T(128)S(1)} %pad_maximum_fusion.18.refs_1_.refs_0_, f32[32,128]{1,0:T(8,128)S(1)} %bitcast.90, f32[5,32,8,128]{3,2,1,0:T(8,128)S(1)} %basis.2.refs_11_.refs_2_, f32[4,32,8,128]{3,2,1,0:T(8,128)S(1)} %get-tuple-element.50.refs_3_), custom_call_target="tpu_custom_call" | custom-call | tf_op jit(solution)/shard_map/last/pallas_call | solution.py:201
  110.0 3.7 %all-to-all-start.18 = ((f32[16,4,8,128]{3,2,1,0:T(8,128)}), f32[16,4,8,128]{3,2,1,0:T(8,128)S(1)}, u32[]{:S(2)}, u32[]{:S(2)}) async-start(f32[16,4,8,128]{3,2,1,0:T(8,128)} %get-tuple-element.52), calls=%async_computation.18 | async-start | bytes 524288 | tf_op jit(solution)/shard_map/all_to_all | solution.py:577
  114.9 8.8 %all-to-all-done.18.refs_1_ = f32[16,4,8,128]{3,2,1,0:T(8,128)S(1)} async-done(((f32[16,4,8,128]{3,2,1,0:T(8,128)}), f32[16,4,8,128]{3,2,1,0:T(8,128)S(1)}, u32[]{:S(2)}, u32[]{:S(2)}) %all-to-all-start.18) | async-done | bytes 262176 | tf_op jit(solution)/shard_map/all_to_all | solution.py:577
  (58 shorter events, 5.1 us)
Async XLA Ops:
  2.9 12.2 %copy-start.2 = (bf16[4,256,256]{2,1,0:T(8,128)(2,1)S(1)}, bf16[4,256,256]{2,1,0:T(8,128)(2,1)}, u32[]{:S(2)}) copy-start(bf16[4,256,256]{2,1,0:T(8,128)(2,1)} %param.18) | copy-start | bytes 1572868
  2.9 22.0 %all-to-all-start.16 = ((f32[16,8,8,128]{3,2,1,0:T(8,128)}), f32[16,8,8,128]{3,2,1,0:T(8,128)S(1)}, u32[]{:S(2)}, u32[]{:S(2)}) async-start(f32[16,8,8,128]{3,2,1,0:T(8,128)} %spread.1), calls=%async_computation.16 | async-start | bytes 1048576 | tf_op jit(solution)/shard_map/all_to_all | solution.py:541
  10.4 0.7 copy-start.8
  12.3 0.7 copy-start.11
  12.4 2.5 %copy-start.6 = (f32[4,3,256]{2,0,1:T(4,128)S(1)}, f32[4,3,256]{2,0,1:T(4,128)}, u32[]{:S(2)}) copy-start(f32[4,3,256]{2,0,1:T(4,128)} %param.17) | copy-start | bytes 36868
  15.2 0.7 copy-start.7
  25.4 15.8 %collective-permute-start.66 = (f32[36,8,128]{2,1,0:T(8,128)S(1)}, f32[36,8,128]{2,1,0:T(8,128)S(1)}, u32[]{:S(2)}, u32[]{:S(2)}) collective-permute-start(f32[36,8,128]{2,1,0:T(8,128)S(1)} %get-tuple-element.45), channel_id=1, source_target_pairs={{0,1},{1,2},{2,3},{3,11},{11,10},{10,9},{9,8},{8,16},{16,17},{17,1... | collective-permute-start | bytes 442376 | tf_op jit(solution)/shard_map/ppermute | solution.py:527
  27.3 13.9 %collective-permute-start.67 = (f32[36,8,128]{2,1,0:T(8,128)S(1)}, f32[36,8,128]{2,1,0:T(8,128)S(1)}, u32[]{:S(2)}, u32[]{:S(2)}) collective-permute-start(f32[36,8,128]{2,1,0:T(8,128)S(1)} %get-tuple-element.46), channel_id=1, source_target_pairs={{1,0},{2,1},{3,2},{11,3},{10,11},{9,10},{8,9},{16,8},{17,16},{18,1... | collective-permute-start | bytes 442376 | tf_op jit(solution)/shard_map/ppermute | solution.py:527
  49.6 16.9 %collective-permute-start.68 = (f32[4,8,128]{2,1,0:T(8,128)S(1)}, f32[4,8,128]{2,1,0:T(8,128)S(1)}, u32[]{:S(2)}, u32[]{:S(2)}) collective-permute-start(f32[4,8,128]{2,1,0:T(8,128)S(1)} %bitcast.140), channel_id=1, source_target_pairs={{0,1},{1,2},{2,3},{3,11},{11,10},{10,9},{9,8},{8,16},{16,17},{17,1... | collective-permute-start | bytes 49160 | tf_op jit(solution)/shard_map/ppermute | solution.py:527
  52.6 13.9 %collective-permute-start.69 = (f32[4,8,128]{2,1,0:T(8,128)S(1)}, f32[4,8,128]{2,1,0:T(8,128)S(1)}, u32[]{:S(2)}, u32[]{:S(2)}) collective-permute-start(f32[4,8,128]{2,1,0:T(8,128)S(1)} %bitcast.139), channel_id=1, source_target_pairs={{1,0},{2,1},{3,2},{11,3},{10,11},{9,10},{8,9},{16,8},{17,16},{18,1... | collective-permute-start | bytes 49160 | tf_op jit(solution)/shard_map/ppermute | solution.py:527
  66.7 5.7 %collective-permute-start.70 = (f32[2,32,8,128]{3,2,1,0:T(8,128)S(1)}, f32[2,32,8,128]{3,2,1,0:T(8,128)S(1)}, u32[]{:S(2)}, u32[]{:S(2)}) collective-permute-start(f32[2,32,8,128]{3,2,1,0:T(8,128)S(1)} %rhs.1), channel_id=1, source_target_pairs={{0,1},{1,2},{2,3},{3,11},{11,10},{10,9},{9,8},{8,16},{16,17},{17,1... | collective-permute-start | bytes 786440 | tf_op jit(solution)/shard_map/ppermute | solution.py:527
  71.0 4.6 %collective-permute-start.71 = (f32[2,32,8,128]{3,2,1,0:T(8,128)S(1)}, f32[2,32,8,128]{3,2,1,0:T(8,128)S(1)}, u32[]{:S(2)}, u32[]{:S(2)}) collective-permute-start(f32[2,32,8,128]{3,2,1,0:T(8,128)S(1)} %rhs.1), channel_id=1, source_target_pairs={{1,0},{2,1},{3,2},{11,3},{10,11},{9,10},{8,9},{16,8},{17,16},{18,1... | collective-permute-start | bytes 786440 | tf_op jit(solution)/shard_map/ppermute | solution.py:527
  79.0 8.2 %collective-permute-start.72 = (f32[32,8,128]{2,1,0:T(8,128)S(1)}, f32[32,8,128]{2,1,0:T(8,128)S(1)}, u32[]{:S(2)}, u32[]{:S(2)}) collective-permute-start(f32[32,8,128]{2,1,0:T(8,128)S(1)} %slice_bitcast_fusion.4.refs_8_), channel_id=1, source_target_pairs={{0,1},{1,2},{2,3},{3,11},{11,10},{10,9},{9,8},{8,16},{16,17},{17,1... | collective-permute-start | bytes 393224 | tf_op jit(solution)/shard_map/ppermute | solution.py:527
  85.7 3.2 %collective-permute-start.73 = (f32[32,8,128]{2,1,0:T(8,128)S(1)}, f32[32,8,128]{2,1,0:T(8,128)S(1)}, u32[]{:S(2)}, u32[]{:S(2)}) collective-permute-start(f32[32,8,128]{2,1,0:T(8,128)S(1)} %slice_bitcast_fusion.4.refs_8_), channel_id=1, source_target_pairs={{1,0},{2,1},{3,2},{11,3},{10,11},{9,10},{8,9},{16,8},{17,16},{18,1... | collective-permute-start | bytes 393224 | tf_op jit(solution)/shard_map/ppermute | solution.py:527
  108.0 15.8 %copy-start.5 = (s32[8,32,128]{2,1,0:T(8,128)S(1)}, s32[8,32,128]{2,1,0:T(8,128)}, u32[]{:S(2)}) copy-start(s32[8,32,128]{2,1,0:T(8,128)} %refs_4_.1) | copy-start | bytes 393220
  110.0 13.7 %copy-start.1 = (f32[8,32,128]{2,1,0:T(8,128)S(1)}, f32[8,32,128]{2,1,0:T(8,128)}, u32[]{:S(2)}) copy-start(f32[8,32,128]{2,1,0:T(8,128)} %refs_0_.3) | copy-start | bytes 393220
  110.0 13.7 %all-to-all-start.18 = ((f32[16,4,8,128]{3,2,1,0:T(8,128)}), f32[16,4,8,128]{3,2,1,0:T(8,128)S(1)}, u32[]{:S(2)}, u32[]{:S(2)}) async-start(f32[16,4,8,128]{3,2,1,0:T(8,128)} %get-tuple-element.52), calls=%async_computation.18 | async-start | bytes 524288 | tf_op jit(solution)/shard_map/all_to_all | solution.py:577
  114.8 9.0 %copy-start = (f32[8,32,128]{2,1,0:T(8,128)S(1)}, f32[8,32,128]{2,1,0:T(8,128)}, u32[]{:S(2)}) copy-start(f32[8,32,128]{2,1,0:T(8,128)} %refs_2_.1) | copy-start | bytes 393220
  114.8 9.0 %copy-start.3 = (f32[8,32,128]{2,1,0:T(8,128)S(1)}, f32[8,32,128]{2,1,0:T(8,128)}, u32[]{:S(2)}) copy-start(f32[8,32,128]{2,1,0:T(8,128)} %refs_1_.1) | copy-start | bytes 393220
  114.8 9.0 %copy-start.4 = (s32[8,32,128]{2,1,0:T(8,128)S(1)}, s32[8,32,128]{2,1,0:T(8,128)}, u32[]{:S(2)}) copy-start(s32[8,32,128]{2,1,0:T(8,128)} %refs_3_.1) | copy-start | bytes 393220
  123.9 0.7 copy-start.9
  124.5 0.7 copy-start.10

commit v3 on v2

--- a/solution.py
+++ b/solution.py
@@ -31,8 +31,8 @@
     tan_low = jnp.concatenate([none, tan_low[:, None]], axis=1).reshape(4 * families, modes)
     weight_out = jnp.concatenate(
         [
-            jnp.concatenate([stress, tan_high, tan_high], axis=1),
-            jnp.concatenate([jnp.zeros_like(stress), tan_low, tan_low], axis=1),
+            jnp.concatenate([stress, tan_high], axis=1),
+            jnp.concatenate([jnp.zeros_like(stress), tan_low], axis=1),
         ],
         axis=0,
     )
@@ -54,8 +54,10 @@
         for j in range(3):
             value = strain_ref[j, a, pl.ds(x, 1), :]
             if edges and j == 2:
-                part = edges[0 if x == 0 else 1][0, pl.ds(a, 1), :] * 0.5
-                value = value - part if x == 0 else value + part
+                even, chip_ref, far_ref = edges
+                chip, far = chip_ref[0, pl.ds(a, 1), :], far_ref[0, pl.ds(a, 1), :]
+                beyond = jnp.where(even[...] == (1 if x == 7 else 0), chip, far) * 0.5
+                value = value - beyond if x == 0 else value + beyond
             value = jnp.broadcast_to(value, place.shape)
             high = value.astype(BF).astype(F32)
             piece = jnp.where(place < families, high, value - high)
@@ -77,11 +79,8 @@
     )
     hidden = jnp.dot(mid_ref[...], stacked, preferred_element_type=F32)
     bounded = jnp.tanh(hidden).astype(BF)
-    square = bounded.astype(F32) * bounded.astype(F32)
-    square_high = square.astype(BF)
-    square_low = (square - square_high.astype(F32)).astype(BF)
-    all_three = jnp.concatenate([bounded, square_high, square_low], axis=0)
-    result = jnp.dot(out_ref[...], all_three, preferred_element_type=F32)
+    both = jnp.concatenate([bounded, bounded * bounded], axis=0)
+    result = jnp.dot(out_ref[...], both, preferred_element_type=F32)
     result = result[: 4 * families] + result[4 * families :]
     owner = lax.shift_right_logical(lax.broadcasted_iota(jnp.int32, (4 * families, width), 0), 2)
     result = jnp.where(owner == family, result, 0.0)
@@ -115,7 +114,8 @@
             whole(weight_mid),
             whole(weight_out),
         ]
-        + [pl.BlockSpec((1, 8, 128), lambda i: (count + i, 0, 0)) for _ in edges],
+        + [pl.BlockSpec((1, 128), lambda i: (0, 0)) for _ in edges[:1]]
+        + [pl.BlockSpec((1, 8, 128), lambda i: (count + i, 0, 0)) for _ in edges[1:]],
         out_specs=pl.BlockSpec((4, step, 8, 128), lambda i: (0, i, 0, 0)),
         out_shape=jax.ShapeDtypeStruct((4, count, 8, 128), F32),
         compiler_params=pltpu.CompilerParams(vmem_limit_bytes=48 * 2**20),
@@ -193,15 +193,14 @@
 
 
 VMEM = pl.BlockSpec(memory_space=pltpu.VMEM)
-SMEM = pl.BlockSpec(memory_space=pltpu.SMEM)
 GROUP = ("blk", "micro")
 
 
-def call(kernel, out_shapes, scratch, name, *args, smem=0):
+def call(kernel, out_shapes, scratch, name, *args):
     return pl.pallas_call(
         kernel,
         out_shape=[jax.ShapeDtypeStruct(shape, dtype) for shape, dtype in out_shapes],
-        in_specs=[SMEM] * smem + [VMEM] * (len(args) - smem),
+        in_specs=[VMEM] * len(args),
         out_specs=[VMEM] * len(out_shapes),
         scratch_shapes=scratch,
         compiler_params=pltpu.CompilerParams(vmem_limit_bytes=40 * 2**20),
@@ -224,6 +223,13 @@
 
 def place(slab, position, peers):
     return position + slab * (peers - 1 - 2 * position)
+
+
+def whereabouts(peers):
+    across = lax.axis_size("micro")
+    b, m, slab = lax.axis_index("blk"), lax.axis_index("micro"), lax.axis_index("slab")
+    position = place(slab, b * across + jnp.where(b % 2 == 0, m, across - 1 - m), peers)
+    return (slab == 0) & (position == 0), (slab == 1) & (position == peers - 1), position % 2 == 0
 
 
 def spread_kernel(path, capacity, u_ref, load_ref, found_ref, slot_ref, flag_ref, send_ref, turned):
@@ -258,7 +264,8 @@
     return (after - before) * 0.5
 
 
-def collect_kernel(around, recv_ref, strain_ref, code_ref, found_ref, rest_ref, next_ref, previous_ref, u):
+def collect_kernel(around, recv_ref, strain_ref, code_ref, found_ref, rest_ref, chip_ref, far_ref, u):
+    _, _, even = whereabouts(recv_ref.shape[0])
     for b in range(around // 8):
         for half in range(2):
             for number in range(4):
@@ -271,8 +278,8 @@
                         code_ref[at] = tiles[a].astype(jnp.int32)
                     elif number == 2:
                         found_ref[at] = tiles[a]
-                        next_ref[at] = tiles[a]
-                        previous_ref[at] = tiles[a]
+                        chip_ref[at] = tiles[a]
+                        far_ref[at] = tiles[a]
                     else:
                         rest_ref[at] = tiles[a]
     nothing = jnp.zeros((1, 128), F32)
@@ -282,11 +289,19 @@
         strain_ref[1, at] = radial(tile)
         after, before = beside(tile, nothing, nothing)
         strain_ref[2, at] = (after - before) * 0.5
-        next_ref[around + at // 8, pl.ds(at % 8, 1), :] = tile[7:8]
-        previous_ref[around + at // 8, pl.ds(at % 8, 1), :] = tile[0:1]
-
-
-def rhs_kernel(around, first_ref, outer_ref, second_ref, rest_ref, low_ref, high_ref, own_ref):
+        chip_ref[around + at // 8, pl.ds(at % 8, 1), :] = tile[7:8]
+        far_ref[around + at // 8, pl.ds(at % 8, 1), :] = tile[0:1]
+    for index in range(around, around + around // 8):
+        bottom, top = far_ref[index], chip_ref[index]
+        chip_ref[index] = jnp.where(even, top, bottom)
+        far_ref[index] = jnp.where(even, bottom, top)
+
+
+def rhs_kernel(around, peers, first_ref, outer_ref, second_ref, rest_ref, chip_ref, far_ref, own_ref, low_ref, high_ref):
+    _, _, even = whereabouts(peers)
+    for index in range(around // 8):
+        low_ref[index] = jnp.where(even, far_ref[index], chip_ref[index])
+        high_ref[index] = jnp.where(even, chip_ref[index], far_ref[index])
     row = lax.broadcasted_iota(jnp.int32, (8, 128), 0)
     rim = (row == 0) | (row == 7)
 
@@ -306,28 +321,30 @@
 
 
 HALF = ITERS // 2
+MOST_LOST = 1.0e5
 
 
 def basis_kernel(
-    around, last, ends_ref, scale_ref, tan_ref, tan_low_ref, tan_high_ref, found_ref, found_low_ref, found_high_ref,
-    seed_ref, seed_low_ref, seed_high_ref, *refs
+    around, peers, last, scale_ref, tan_ref, tan_chip_ref, tan_far_ref, found_ref, found_chip_ref, found_far_ref,
+    seed_ref, seed_chip_ref, seed_far_ref, *refs
 ):
     if last:
         earlier_ref, own_ref, gram_ref, *scratch = refs
     else:
         own_ref, *scratch = refs
     tan, main, off_r, back_r, off_x, back_x, vectors = scratch
-    centre, inverse = scale_ref[0], scale_ref[1]
+    centre, inverse = scale_ref[0:1, :], scale_ref[1:2, :]
+    is_first, is_last, even = whereabouts(peers)
     lane = lax.broadcasted_iota(jnp.int32, (24, 128), 1)
     plane = lax.broadcasted_iota(jnp.int32, (24, 128), 0)
-    cut = ((plane == 7) & (ends_ref[0] == 1)) | ((plane == 14) & (ends_ref[1] == 1))
+    cut = ((plane == 7) & is_first) | ((plane == 14) & is_last)
     quarter = 0.25 * inverse
 
-    def three(low, own, high):
-        return jnp.concatenate([low, own, high], axis=0)
+    def three(own, chip, far):
+        return jnp.concatenate([jnp.where(even, far, chip), own, jnp.where(even, chip, far)], axis=0)
 
     for at in range(around):
-        tan[at] = three(tan_low_ref[at], tan_ref[at], tan_high_ref[at]) * quarter
+        tan[at] = three(tan_ref[at], tan_chip_ref[at], tan_far_ref[at]) * quarter
     for at in range(around):
         here = tan[at]
         up_a, down_a = tan[(at + 1) % around], tan[(at - 1) % around]
@@ -335,7 +352,7 @@
         down_r = jnp.where(lane == 0, 0.0, pltpu.roll(here, 1, 1))
         up_x = pltpu.roll(here, 23, 0)
         down_x = pltpu.roll(here, 1, 0)
-        found = three(found_low_ref[at], found_ref[at], found_high_ref[at])
+        found = three(found_ref[at], found_chip_ref[at], found_far_ref[at])
         main[at] = (found - centre) * inverse + ((up_a + down_a) + (up_r + down_r) + (up_x + down_x))
         beyond = jnp.where(lane >= 126, 0.0, up_r)
         off_r[at] = beyond
@@ -353,7 +370,7 @@
         return result - off_x[at] * pltpu.roll(value, 22, 0) - back_x[at] * pltpu.roll(value, 2, 0)
 
     for at in range(around):
-        vectors[0, at] = three(seed_low_ref[at], seed_ref[at], seed_high_ref[at])
+        vectors[0, at] = three(seed_ref[at], seed_chip_ref[at], seed_far_ref[at])
     for degree in range(1, HALF + 1):
         for at in range(around):
             value = apply(degree - 1, at)
@@ -384,7 +401,7 @@
             entry = jnp.sum(jnp.sum(value, axis=0, keepdims=True), axis=1, keepdims=True)
             gram = jnp.where(column == number, jnp.broadcast_to(entry, (1, 128)), gram)
             number += 1
-    gram_ref[...] = gram
+    gram_ref[...] = jnp.broadcast_to(gram, gram_ref.shape)
 
 
 def unpack_gram(all_ref, total):
@@ -477,7 +494,7 @@
 
 def last_kernel(around, scale_ref, all_ref, early_ref, late_ref, send_ref, worst_ref):
     total = 2 * HALF + 1
-    change, residual, worst = iterate(unpack_gram(all_ref, total), total, scale_ref[0], scale_ref[2])
+    change, residual, worst = iterate(unpack_gram(all_ref, total), total, scale_ref[0:1, :], scale_ref[2:3, :])
     worst_ref[...] = jnp.broadcast_to(worst, (8, 128))
     pairs = [[None if c is None else jnp.broadcast_to(c, (8, 128)) for c in part] for part in (change, residual)]
     for b in range(around // 8):
@@ -489,16 +506,21 @@
                     send_ref[4 * b + m, 2 * number + half] = tiles[m]
 
 
-def deliver_kernel(path, u_ref, recv_ref, updated_ref, residual_ref, turned):
+def deliver_kernel(path, u_ref, recv_ref, worst_ref, instead_updated_ref, instead_residual_ref, *refs):
+    updated_ref, residual_ref, turned = refs
     slab = lax.axis_index("slab")
     for source in range(recv_ref.shape[0]):
         start = pl.multiple_of(8 * place(slab, path[source], len(path)), 8)
         for index in range(4):
             turned[index, pl.ds(start, 8), :] = recv_ref[source, index]
+    good = jnp.broadcast_to(worst_ref[0:1, :] < MOST_LOST, (32, 128))
     for half in range(2):
-        part = slice(4 * half, 4 * half + 4)
-        updated_ref[part] = u_ref[part] + jnp.transpose(turned[half]).reshape(4, 32, 128)
-        residual_ref[part] = jnp.transpose(turned[2 + half]).reshape(4, 32, 128)
+        change = jnp.transpose(turned[half]).reshape(4, 32, 128)
+        residual = jnp.transpose(turned[2 + half]).reshape(4, 32, 128)
+        for i in range(4):
+            at = 4 * half + i
+            updated_ref[at] = jnp.where(good, u_ref[at] + change[i], instead_updated_ref[at])
+            residual_ref[at] = jnp.where(good, residual[i], instead_residual_ref[at])
 
 
 def sliced_body(
@@ -510,27 +532,26 @@
     peers = along * across
     around = size_x * along
     everyone = peers * lax.axis_size("slab")
-    slab = lax.axis_index("slab")
     path = [b * across + (m if b % 2 == 0 else across - 1 - m) for b in range(along) for m in range(across)]
-    forth = jnp.array(path, jnp.int32)[lax.axis_index("blk") * across + lax.axis_index("micro")]
-    mine = place(slab, forth, peers) + peers * slab
-    ends = jnp.stack([(mine == 0), (mine == everyone - 1)]).astype(jnp.int32)
+    _, _, even = whereabouts(peers)
     spots = [0] * everyone
     for b in range(along):
         for s in range(2):
             for m in range(across):
                 spots[place(s, path[b * across + m], peers) + peers * s] = (b * 2 + s) * across + m
-    rising = [(spots[i], spots[i + 1]) for i in range(everyone - 1)]
-    falling = [(b, a) for a, b in rising]
-
-    def neighbours(to_next, to_previous):
-        return lax.ppermute(to_next, AXES, rising), lax.ppermute(to_previous, AXES, falling)
+
+    def swap(first, value):
+        pairs = [(spots[i], spots[i + 1]) for i in range(first, everyone - 1, 2)]
+        return lax.ppermute(value, AXES, pairs + [(b, a) for a, b in pairs])
+
+    def neighbours(to_chip, to_far):
+        return swap(0, to_chip), swap(1, to_far)
 
     packed = pack_families(family_in, family_mid, family_out, family_tan)
     typical = 0.5 + 0.33 * jnp.mean(jnp.sum(family_tan, axis=1))
     centre = 1.1 + 1.4 * typical
     half_width = centre - 0.4
-    scale = jnp.stack([centre, 1.0 / half_width, half_width])
+    scale = jnp.broadcast_to(jnp.stack([centre, 1.0 / half_width, half_width] + [centre] * 5)[:, None], (8, 128))
 
     capacity = size_x * size_y * size_z // 2
     (send,) = call(
@@ -542,48 +563,50 @@
     field = (around, 8, 128)
     edge = (around // 8, 8, 128)
     message = (around + around // 8, 8, 128)
-    strain, code, found, rest, to_next, to_previous = call(
+    strain, code, found, rest, to_chip, to_far = call(
         lambda *refs: collect_kernel(around, *refs),
         [((3,) + field, F32), (field, jnp.int32), (field, F32), (field, F32), (message, F32), (message, F32)],
         [pltpu.VMEM(field, F32)], "collect", recv,
     )
-    low, high = neighbours(to_next, to_previous)
+    chip, far = neighbours(to_chip, to_far)
     first = cells(strain, code, packed, families, 8, (1, 2, 3))
-    outer = cells(strain, code, packed, families, 8, (0, 7), low, high)
-    edge_low, edge_high = neighbours(outer[2, :, 7].reshape(edge), outer[2, :, 0].reshape(edge))
+    outer = cells(strain, code, packed, families, 8, (0, 7), jnp.broadcast_to(even.astype(jnp.int32), (1, 128)), chip, far)
+    top, bottom = outer[2, :, 7].reshape(edge), outer[2, :, 0].reshape(edge)
+    edge_chip, edge_far = neighbours(jnp.where(even, top, bottom), jnp.where(even, bottom, top))
     second = cells(strain, code, packed, families, 8, (4, 5, 6))
     (own,) = call(
-        lambda *refs: rhs_kernel(around, *refs), [((2,) + field, F32)], [], "rhs",
-        first, outer, second, rest, edge_low, edge_high,
-    )
-    own_low, own_high = neighbours(own, own)
+        lambda *refs: rhs_kernel(around, peers, *refs), [((2,) + field, F32)], [pltpu.VMEM(edge, F32)] * 2, "rhs",
+        first, outer, second, rest, edge_chip, edge_far,
+    )
+    own_chip, own_far = neighbours(own, own)
 
     def basis(last, outputs, *vectors):
         return call(
-            lambda *refs: basis_kernel(around, last, *refs), outputs,
+            lambda *refs: basis_kernel(around, peers, last, *refs), outputs,
             [pltpu.VMEM((around, 24, 128), F32)] * 6 + [pltpu.VMEM((HALF + 1, around, 24, 128), F32)],
-            "basis", ends, scale, own[1], own_low[1], own_high[1], found, low, high, *vectors, smem=2,
+            "basis", scale, own[1], own_chip[1], own_far[1], found, chip, far, *vectors,
         )
 
-    (early,) = basis(False, [((HALF + 1,) + field, F32)], own[0], own_low[0], own_high[0])
+    (early,) = basis(False, [((HALF + 1,) + field, F32)], own[0], own_chip[0], own_far[0])
     late, gram = basis(
-        True, [((HALF,) + field, F32), ((1, 128), F32)], early[HALF], *neighbours(early[HALF], early[HALF]), early
-    )
-    sums = lax.all_to_all(jnp.broadcast_to(gram, (everyone, 128)), AXES, 0, 0, tiled=True)
+        True, [((HALF,) + field, F32), ((everyone, 128), F32)], early[HALF], *neighbours(early[HALF], early[HALF]), early
+    )
+    sums = lax.all_to_all(gram, AXES, 0, 0, tiled=True)
     send, worst = call(
         lambda *refs: last_kernel(around, *refs),
-        [((peers, 4, 8, 128), F32), ((8, 128), F32)], [], "last", scale, sums, early, late, smem=1,
+        [((peers, 4, 8, 128), F32), ((8, 128), F32)], [], "last", scale, sums, early, late,
     )
     recv = lax.all_to_all(send, GROUP, 0, 0, tiled=True)
+    inputs = (
+        displacement, load_field, foundation, plastic_flags, point_slot, family_in, family_mid, family_out, family_tan
+    )
+    good, recv = lax.optimization_barrier((worst[0, 0] < MOST_LOST, recv))
+    instead = lax.cond(good, lambda: (jnp.zeros_like(displacement),) * 2, lambda: plain_body(*inputs))
     shape = displacement.shape
-    updated, residual = call(
-        lambda *refs: deliver_kernel(path, *refs),
-        [(shape, F32), (shape, F32)], [pltpu.VMEM((4, 128, 128), F32)], "deliver", displacement, recv,
-    )
-    return updated, residual, worst[0, 0]
-
-
-MOST_LOST = 1.0e5
+    return call(
+        lambda *refs: deliver_kernel(path, *refs), [(shape, F32), (shape, F32)], [pltpu.VMEM((4, 128, 128), F32)],
+        "deliver", displacement, recv, worst, *instead,
+    )
 
 
 def body(*inputs):
@@ -598,8 +621,7 @@
     )
     if not fits:
         return plain_body(*inputs)
-    updated, residual, worst = sliced_body(*inputs)
-    return lax.cond(worst < MOST_LOST, lambda: (updated, residual), lambda: plain_body(*inputs))
+    return tuple(sliced_body(*inputs))
 
 
 def solution(mesh):

time: 126 us -> 111 us (0.88)
  starting transfers between devices: 32.4 us -> 26.4 us
  Pallas kernels: 45.7 us -> 41.4 us
  waiting for transfers between devices: 22.7 us -> 20.5 us
  local copies, waits for them, and re-layouts: 4.78 us -> 3.02 us
  blocking collectives: 15.1 us -> 16.5 us
  between operations: 3.72 us -> 2.34 us
    ppermute x8, starting transfers between devices: 21.3 us -> 15.2 us  [swap(): return lax.ppermute(value, AXES, pairs + [(b, a) for a, b in pairs])]
    ppermute x8, waiting for transfers between devices: 5.06 us -> 0.16 us  [swap(): return lax.ppermute(value, AXES, pairs + [(b, a) for a, b in pairs])]
    pallas_call x3, Pallas kernels: 33.4 us -> 30.3 us  [cells(): pl.pallas_call(kernel, grid=(count // step,), in_specs=[pl.BlockSpec((3,...]
    all_to_all x2, waiting for transfers between devices: 17.6 us -> 20.3 us  [sliced_body(): recv = lax.all_to_all(send, GROUP, 0, 0, tiled=True)]
    all_to_all x1, blocking collectives: 15.1 us -> 16.5 us  [sliced_body(): sums = lax.all_to_all(gram, AXES, 0, 0, tiled=True)]
    unnamed x27 -> x21, local copies, waits for them, and re-layouts: 3.34 us -> 2.02 us
  transfers between devices with their start and end apart: 10 -> 10, of which waited for: 4 -> 3; matrix products, arithmetic and copies ran while one was open for 2% -> 1% of each run, Pallas kernels for 20% -> 21%
where the time goes in v3:
time: 111 us
  Pallas kernels  41.4 us (37%)
  starting transfers between devices  26.4 us (24%)
  waiting for transfers between devices  20.5 us (18%)
  blocking collectives  16.5 us (15%)
  local copies, waits for them, and re-layouts  3.02 us (3%)
  between operations  2.34 us (2%)
    pallas_call x3, Pallas kernels, cells(): pl.pallas_call(kernel, grid=(count // step,), in_specs=[pl.BlockSpec((3,...  30.3 us
    all_to_all x2, waiting for transfers between devices, sliced_body(): recv = lax.all_to_all(send, GROUP, 0, 0, tiled=True)  20.3 us
    all_to_all x1, blocking collectives, sliced_body(): sums = lax.all_to_all(gram, AXES, 0, 0, tiled=True)  16.5 us
    ppermute x8, starting transfers between devices, swap(): return lax.ppermute(value, AXES, pairs + [(b, a) for a, b in pairs])  15.2 us
    all_to_all x2, starting transfers between devices, sliced_body(): recv = lax.all_to_all(send, GROUP, 0, 0, tiled=True)  11.2 us
    pallas_call x7, Pallas kernels, call(): pl.pallas_call(kernel, out_shape=[jax.ShapeDtypeStruct(shape, dtype) for...  11.1 us
  transfers between devices with their start and end apart: 10, of which 3 were waited for; matrix products, arithmetic and copies ran while one was open for 1% of the time, Pallas kernels for 21%

profile of v3, /device:TPU:0, one launch (start us, length us, event | category | flops | bytes accessed | tf_op | source)
XLA Modules:
  0.0 110.8 jit_solution(6140028383819669577)
XLA Ops:
  0.6 2.2 %spread.1 = f32[16,8,8,128]{3,2,1,0:T(8,128)} custom-call(f32[8,32,128]{2,1,0:T(8,128)} %refs_0_.3, f32[8,32,128]{2,1,0:T(8,128)} %refs_1_.1, f32[8,32,128]{2,1,0:T(8,128)} %refs_2_.1, s32[8,32,128]{2,1,0:T(8,128)} %refs_3_.1, s32[8,32,128]{2,1,0:T(8,128)} %refs_4_.1), custom_call_target="tpu_custom_call" | custom-call | tf_op jit(solution)/shard_map/spread/pallas_call | solution.py:200
  2.9 7.5 %all-to-all-start.16 = ((f32[16,8,8,128]{3,2,1,0:T(8,128)}), f32[16,8,8,128]{3,2,1,0:T(8,128)S(1)}, u32[]{:S(2)}, u32[]{:S(2)}) async-start(f32[16,8,8,128]{3,2,1,0:T(8,128)} %spread.1), calls=%async_computation.16 | async-start | bytes 1048576 | tf_op jit(solution)/shard_map/all_to_all | solution.py:562
  10.4 0.7 copy-done.6
  11.3 0.6 copy-done.8
  12.0 0.6 fusion.108
  12.7 0.7 copy-done.7
  13.4 11.5 %all-to-all-done.16.refs_0_ = f32[16,8,8,128]{3,2,1,0:T(8,128)S(1)} async-done(((f32[16,8,8,128]{3,2,1,0:T(8,128)}), f32[16,8,8,128]{3,2,1,0:T(8,128)S(1)}, u32[]{:S(2)}, u32[]{:S(2)}) %all-to-all-start.16) | async-done | bytes 524320 | tf_op jit(solution)/shard_map/all_to_all | solution.py:562
  25.5 0.7 collective-permute-start.67
  26.2 11.4 %cells.5.refs_0_ = f32[4,32,8,128]{3,2,1,0:T(8,128)S(1)} custom-call(f32[3,32,8,128]{3,2,1,0:T(8,128)S(1)} %get-tuple-element.43.refs_0_, s32[32,8,128]{2,1,0:T(8,128)S(1)} %get-tuple-element.44.refs_1_, bf16[256,48]{1,0:T(8,128)(2,1)S(1)} %copy.82.refs_2_, bf16[256,1024]{1,0:T(8,128)(2,1)S(1)} %bitcast.84, bf16[32,512]{1,0:T(8,128)(2,1)S(1)} %fusion.104.refs_4_), custom_call_target="tpu_custom_call" | custom-call | flops 8053063680 | bytes 393216 | tf_op jit(solution)/shard_map/cells/pallas_call | solution.py:107
  37.6 7.5 %cells.6.refs_1_ = f32[4,32,8,128]{3,2,1,0:T(8,128)S(1)} custom-call(f32[3,32,8,128]{3,2,1,0:T(8,128)S(1)} %get-tuple-element.43.refs_0_, s32[32,8,128]{2,1,0:T(8,128)S(1)} %get-tuple-element.44.refs_1_, bf16[256,48]{1,0:T(8,128)(2,1)S(1)} %copy.82.refs_2_, bf16[256,1024]{1,0:T(8,128)(2,1)S(1)} %bitcast.85, bf16[32,512]{1,0:T(8,128)(2,1)S(1)} %fusion.104.refs_4_, ...), custom_call_target="tpu_custom_call" | custom-call | flops 5368709120 | bytes 262144 | tf_op jit(solution)/shard_map/cells/pallas_call | solution.py:107
  45.1 2.6 %collective-permute-start.68 = (f32[4,8,128]{2,1,0:T(8,128)S(1)}, f32[4,8,128]{2,1,0:T(8,128)S(1)}, u32[]{:S(2)}, u32[]{:S(2)}) collective-permute-start(f32[4,8,128]{2,1,0:T(8,128)S(1)} %bitcast.139), channel_id=1, source_target_pairs={{0,1},{2,3},{11,10},{9,8},{16,17},{18,19},{27,26},{25,24},{28,29},... | collective-permute-start | bytes 49160 | tf_op jit(solution)/shard_map/ppermute | solution.py:545
  47.7 0.7 collective-permute-start.69
  48.4 11.4 %cells.7.refs_2_ = f32[4,32,8,128]{3,2,1,0:T(8,128)S(1)} custom-call(f32[3,32,8,128]{3,2,1,0:T(8,128)S(1)} %get-tuple-element.43.refs_0_, s32[32,8,128]{2,1,0:T(8,128)S(1)} %get-tuple-element.44.refs_1_, bf16[256,48]{1,0:T(8,128)(2,1)S(1)} %copy.82.refs_2_, bf16[256,1024]{1,0:T(8,128)(2,1)S(1)} %bitcast.86, bf16[32,512]{1,0:T(8,128)(2,1)S(1)} %fusion.104.refs_4_), custom_call_target="tpu_custom_call" | custom-call | flops 8053063680 | bytes 393216 | tf_op jit(solution)/shard_map/cells/pallas_call | solution.py:107
  60.0 2.7 %collective-permute-start.70 = (f32[2,32,8,128]{3,2,1,0:T(8,128)S(1)}, f32[2,32,8,128]{3,2,1,0:T(8,128)S(1)}, u32[]{:S(2)}, u32[]{:S(2)}) collective-permute-start(f32[2,32,8,128]{3,2,1,0:T(8,128)S(1)} %rhs.1), channel_id=1, source_target_pairs={{0,1},{2,3},{11,10},{9,8},{16,17},{18,19},{27,26},{25,24},{28,29},... | collective-permute-start | bytes 786440 | tf_op jit(solution)/shard_map/ppermute | solution.py:545
  63.5 0.7 collective-permute-start.71
  64.3 2.6 %basis.2.refs_10_.refs_2_ = f32[5,32,8,128]{3,2,1,0:T(8,128)S(1)} custom-call(f32[8,128]{1,0:T(8,128)S(1)} %broadcast_in_dim.44.refs_0_, f32[32,8,128]{2,1,0:T(8,128)S(1)} %get-tuple-element.219.refs_1_, f32[32,8,128]{2,1,0:T(8,128)S(1)} %get-tuple-element.217.refs_2_, f32[32,8,128]{2,1,0:T(8,128)S(1)} %get-tuple-element.215.refs_3_, ...), custom_call_target="tpu_custom_call" | custom-call | tf_op jit(solution)/shard_map/basis/pallas_call | solution.py:200
  67.0 7.0 %collective-permute-start.72 = (f32[32,8,128]{2,1,0:T(8,128)S(1)}, f32[32,8,128]{2,1,0:T(8,128)S(1)}, u32[]{:S(2)}, u32[]{:S(2)}) collective-permute-start(f32[32,8,128]{2,1,0:T(8,128)S(1)} %slice_bitcast_fusion.4.refs_7_), channel_id=1, source_target_pairs={{0,1},{2,3},{11,10},{9,8},{16,17},{18,19},{27,26},{25,24},{28,29},... | collective-permute-start | bytes 393224 | tf_op jit(solution)/shard_map/ppermute | solution.py:545
  74.0 0.8 collective-permute-start.73
  75.0 3.2 %basis.3 = (f32[4,32,8,128]{3,2,1,0:T(8,128)S(1)}, f32[32,128]{1,0:T(8,128)S(1)}) custom-call(f32[8,128]{1,0:T(8,128)S(1)} %broadcast_in_dim.44.refs_0_, f32[32,8,128]{2,1,0:T(8,128)S(1)} %get-tuple-element.219.refs_1_, f32[32,8,128]{2,1,0:T(8,128)S(1)} %get-tuple-element.217.refs_2_, f32[32,8,128]{2,1,0:T(8,128)S(1)} %get-tuple-element.215.refs_3_, ...), custom_call_target="tpu_custom_call" | custom-call | tf_op jit(solution)/shard_map/basis/pallas_call | solution.py:200
  78.2 16.5 %all_to_all.148 = f32[32,1,128]{2,1,0:T(1,128)S(1)} all-to-all(f32[32,1,128]{2,1,0:T(1,128)S(1)} %bitcast.90), channel_id=1, replica_groups=mesh['blk'=4,'slab'=2,'micro'=4] {'blk','slab','micro'}, dimensions={0} | all-to-all | bytes 32768 | tf_op jit(solution)/shard_map/all_to_all | solution.py:594
  94.8 1.4 %last.1 = (f32[16,4,8,128]{3,2,1,0:T(8,128)}, f32[8,128]{1,0:T(8,128)S(1)}) custom-call(f32[8,128]{1,0:T(8,128)S(1)} %broadcast_in_dim.44.refs_0_, f32[32,128]{1,0:T(8,128)S(1)} %bitcast.89, f32[5,32,8,128]{3,2,1,0:T(8,128)S(1)} %basis.2.refs_10_.refs_2_, f32[4,32,8,128]{3,2,1,0:T(8,128)S(1)} %get-tuple-element.50.refs_3_), custom_call_target="tpu_custom_call" | custom-call | tf_op jit(solution)/shard_map/last/pallas_call | solution.py:200
  96.2 3.7 %all-to-all-start.18 = ((f32[16,4,8,128]{3,2,1,0:T(8,128)}), f32[16,4,8,128]{3,2,1,0:T(8,128)S(1)}, u32[]{:S(2)}, u32[]{:S(2)}) async-start(f32[16,4,8,128]{3,2,1,0:T(8,128)} %get-tuple-element.52), calls=%async_computation.18 | async-start | bytes 524288 | tf_op jit(solution)/shard_map/all_to_all | solution.py:599
  101.0 8.8 %all-to-all-done.18.refs_1_ = f32[16,4,8,128]{3,2,1,0:T(8,128)S(1)} async-done(((f32[16,4,8,128]{3,2,1,0:T(8,128)}), f32[16,4,8,128]{3,2,1,0:T(8,128)S(1)}, u32[]{:S(2)}, u32[]{:S(2)}) %all-to-all-start.18) | async-done | bytes 262176 | tf_op jit(solution)/shard_map/all_to_all | solution.py:599
  109.9 0.9 deliver.1
  (52 shorter events, 2.1 us)
Async XLA Ops:
  2.9 8.4 %copy-start.2 = (bf16[4,256,256]{2,1,0:T(8,128)(2,1)S(1)}, bf16[4,256,256]{2,1,0:T(8,128)(2,1)}, u32[]{:S(2)}) copy-start(bf16[4,256,256]{2,1,0:T(8,128)(2,1)} %param.17) | copy-start | bytes 1572868
  2.9 22.0 %all-to-all-start.16 = ((f32[16,8,8,128]{3,2,1,0:T(8,128)}), f32[16,8,8,128]{3,2,1,0:T(8,128)S(1)}, u32[]{:S(2)}, u32[]{:S(2)}) async-start(f32[16,8,8,128]{3,2,1,0:T(8,128)} %spread.1), calls=%async_computation.16 | async-start | bytes 1048576 | tf_op jit(solution)/shard_map/all_to_all | solution.py:562
  10.4 0.7 copy-start.6
  11.3 0.7 copy-start.8
  12.6 0.7 copy-start.7
  25.4 12.2 %collective-permute-start.66 = (f32[36,8,128]{2,1,0:T(8,128)S(1)}, f32[36,8,128]{2,1,0:T(8,128)S(1)}, u32[]{:S(2)}, u32[]{:S(2)}) collective-permute-start(f32[36,8,128]{2,1,0:T(8,128)S(1)} %get-tuple-element.45), channel_id=1, source_target_pairs={{0,1},{2,3},{11,10},{9,8},{16,17},{18,19},{27,26},{25,24},{28,29},... | collective-permute-start | bytes 442376 | tf_op jit(solution)/shard_map/ppermute | solution.py:545
  25.5 12.1 %collective-permute-start.67 = (f32[36,8,128]{2,1,0:T(8,128)S(1)}, f32[36,8,128]{2,1,0:T(8,128)S(1)}, u32[]{:S(2)}, u32[]{:S(2)}) collective-permute-start(f32[36,8,128]{2,1,0:T(8,128)S(1)} %get-tuple-element.46), channel_id=1, source_target_pairs={{1,2},{3,11},{10,9},{8,16},{17,18},{19,27},{26,25},{24,28},{29,30}... | collective-permute-start | bytes 442376 | tf_op jit(solution)/shard_map/ppermute | solution.py:545
  45.1 14.6 %collective-permute-start.68 = (f32[4,8,128]{2,1,0:T(8,128)S(1)}, f32[4,8,128]{2,1,0:T(8,128)S(1)}, u32[]{:S(2)}, u32[]{:S(2)}) collective-permute-start(f32[4,8,128]{2,1,0:T(8,128)S(1)} %bitcast.139), channel_id=1, source_target_pairs={{0,1},{2,3},{11,10},{9,8},{16,17},{18,19},{27,26},{25,24},{28,29},... | collective-permute-start | bytes 49160 | tf_op jit(solution)/shard_map/ppermute | solution.py:545
  47.7 12.1 %collective-permute-start.69 = (f32[4,8,128]{2,1,0:T(8,128)S(1)}, f32[4,8,128]{2,1,0:T(8,128)S(1)}, u32[]{:S(2)}, u32[]{:S(2)}) collective-permute-start(f32[4,8,128]{2,1,0:T(8,128)S(1)} %bitcast.138), channel_id=1, source_target_pairs={{1,2},{3,11},{10,9},{8,16},{17,18},{19,27},{26,25},{24,28},{29,30}... | collective-permute-start | bytes 49160 | tf_op jit(solution)/shard_map/ppermute | solution.py:545
  60.0 4.2 %collective-permute-start.70 = (f32[2,32,8,128]{3,2,1,0:T(8,128)S(1)}, f32[2,32,8,128]{3,2,1,0:T(8,128)S(1)}, u32[]{:S(2)}, u32[]{:S(2)}) collective-permute-start(f32[2,32,8,128]{3,2,1,0:T(8,128)S(1)} %rhs.1), channel_id=1, source_target_pairs={{0,1},{2,3},{11,10},{9,8},{16,17},{18,19},{27,26},{25,24},{28,29},... | collective-permute-start | bytes 786440 | tf_op jit(solution)/shard_map/ppermute | solution.py:545
  63.5 0.7 collective-permute-start.71
  67.0 8.0 %collective-permute-start.72 = (f32[32,8,128]{2,1,0:T(8,128)S(1)}, f32[32,8,128]{2,1,0:T(8,128)S(1)}, u32[]{:S(2)}, u32[]{:S(2)}) collective-permute-start(f32[32,8,128]{2,1,0:T(8,128)S(1)} %slice_bitcast_fusion.4.refs_7_), channel_id=1, source_target_pairs={{0,1},{2,3},{11,10},{9,8},{16,17},{18,19},{27,26},{25,24},{28,29},... | collective-permute-start | bytes 393224 | tf_op jit(solution)/shard_map/ppermute | solution.py:545
  74.0 1.0 collective-permute-start.73
  94.8 15.1 %copy-start.5 = (s32[8,32,128]{2,1,0:T(8,128)S(1)}, s32[8,32,128]{2,1,0:T(8,128)}, u32[]{:S(2)}) copy-start(s32[8,32,128]{2,1,0:T(8,128)} %refs_4_.1) | copy-start | bytes 393220
  96.2 13.7 %copy-start = (f32[8,32,128]{2,1,0:T(8,128)S(1)}, f32[8,32,128]{2,1,0:T(8,128)}, u32[]{:S(2)}) copy-start(f32[8,32,128]{2,1,0:T(8,128)} %refs_2_.1) | copy-start | bytes 393220
  96.2 13.7 %copy-start.1 = (f32[8,32,128]{2,1,0:T(8,128)S(1)}, f32[8,32,128]{2,1,0:T(8,128)}, u32[]{:S(2)}) copy-start(f32[8,32,128]{2,1,0:T(8,128)} %refs_0_.3) | copy-start | bytes 393220
  96.2 13.7 %copy-start.3 = (f32[8,32,128]{2,1,0:T(8,128)S(1)}, f32[8,32,128]{2,1,0:T(8,128)}, u32[]{:S(2)}) copy-start(f32[8,32,128]{2,1,0:T(8,128)} %refs_1_.1) | copy-start | bytes 393220
  96.2 13.7 %copy-start.4 = (s32[8,32,128]{2,1,0:T(8,128)S(1)}, s32[8,32,128]{2,1,0:T(8,128)}, u32[]{:S(2)}) copy-start(s32[8,32,128]{2,1,0:T(8,128)} %refs_3_.1) | copy-start | bytes 393220
  96.2 13.7 %all-to-all-start.18 = ((f32[16,4,8,128]{3,2,1,0:T(8,128)}), f32[16,4,8,128]{3,2,1,0:T(8,128)S(1)}, u32[]{:S(2)}, u32[]{:S(2)}) async-start(f32[16,4,8,128]{3,2,1,0:T(8,128)} %get-tuple-element.52), calls=%async_computation.18 | async-start | bytes 524288 | tf_op jit(solution)/shard_map/all_to_all | solution.py:599

commit v4 on v3

--- a/solution.py
+++ b/solution.py
@@ -196,12 +196,13 @@
 GROUP = ("blk", "micro")
 
 
-def call(kernel, out_shapes, scratch, name, *args):
+def call(kernel, out_shapes, scratch, name, *args, grid=(), ins=None, outs=None):
     return pl.pallas_call(
         kernel,
         out_shape=[jax.ShapeDtypeStruct(shape, dtype) for shape, dtype in out_shapes],
-        in_specs=[VMEM] * len(args),
-        out_specs=[VMEM] * len(out_shapes),
+        grid=grid,
+        in_specs=ins or [VMEM] * len(args),
+        out_specs=outs or [VMEM] * len(out_shapes),
         scratch_shapes=scratch,
         compiler_params=pltpu.CompilerParams(vmem_limit_bytes=40 * 2**20),
         name=name,
@@ -235,19 +236,16 @@
 def spread_kernel(path, capacity, u_ref, load_ref, found_ref, slot_ref, flag_ref, send_ref, turned):
     peers = len(path)
     slab = lax.axis_index("slab")
-    code = jnp.zeros(slot_ref.shape, jnp.int32)
+    code = flag_ref[...]
     for family in range(1, 4):
         code = code + jnp.where(slot_ref[...] >= family * capacity, 2, 0)
     rest = load_ref[...] - found_ref[...] * u_ref[...]
-    fields = (u_ref[...], (code + flag_ref[...]).astype(F32), found_ref[...], rest)
-    for number, field in enumerate(fields):
-        for half in range(2):
-            turned[number, half] = jnp.transpose(field[4 * half : 4 * half + 4].reshape(128, 128))
+    for number, value in enumerate((u_ref[...], code.astype(F32), found_ref[...], rest)):
+        turned[number] = jnp.transpose(value.reshape(128, 128))
     for target in range(peers):
         start = pl.multiple_of(8 * place(slab, path[target], peers), 8)
         for number in range(4):
-            for half in range(2):
-                send_ref[target, 2 * number + half] = turned[number, half, pl.ds(start, 8), :]
+            send_ref[target, 0, number] = turned[number, pl.ds(start, 8), :]
 
 
 def beside(tile, low, high):
@@ -264,12 +262,16 @@
     return (after - before) * 0.5
 
 
-def collect_kernel(around, recv_ref, strain_ref, code_ref, found_ref, rest_ref, chip_ref, far_ref, u):
+def collect_kernel(around, tan_ref, recv_ref, strain_ref, code_ref, found_ref, rest_ref, chip_ref, far_ref, scale_ref, u):
     _, _, even = whereabouts(recv_ref.shape[0])
+    typical = jnp.sum(jnp.sum(tan_ref[...], axis=1, keepdims=True), axis=0, keepdims=True) / tan_ref.shape[0]
+    centre = jnp.broadcast_to(1.1 + 1.4 * (0.5 + 0.33 * typical), (8, 128))
+    row = lax.broadcasted_iota(jnp.int32, (8, 128), 0)
+    scale_ref[...] = jnp.where(row == 0, centre, jnp.where(row == 1, 1.0 / (centre - 0.4), centre - 0.4))
     for b in range(around // 8):
         for half in range(2):
             for number in range(4):
-                tiles = regroup([recv_ref[4 * b + m, 2 * number + half] for m in range(4)])
+                tiles = regroup([recv_ref[4 * b + m, half, number] for m in range(4)])
                 for a in range(4):
                     at = 8 * b + 4 * half + a
                     if number == 0:
@@ -329,9 +331,9 @@
     seed_ref, seed_chip_ref, seed_far_ref, *refs
 ):
     if last:
-        earlier_ref, own_ref, gram_ref, *scratch = refs
+        earlier_ref, previous_ref, own_ref, sums_ref, *scratch = refs
     else:
-        own_ref, *scratch = refs
+        own_ref, sums_ref, *scratch = refs
     tan, main, off_r, back_r, off_x, back_x, vectors = scratch
     centre, inverse = scale_ref[0:1, :], scale_ref[1:2, :]
     is_first, is_last, even = whereabouts(peers)
@@ -377,40 +379,43 @@
             if degree > 1:
                 value = value + value - vectors[degree - 2, at]
             vectors[degree, at] = value
-    skipped = 1 if last else 0
-    for index in range(skipped, HALF + 1):
-        for at in range(around):
-            own_ref[index - skipped, at] = vectors[index, at, 8:16, :]
-    if not last:
-        return
-    total = 2 * HALF + 1
+    pairs = []
+    if last:
+        for degree in range(1, HALF + 1):
+            for at in range(around):
+                value = vectors[degree, at, 8:16, :]
+                own_ref[degree - 1, at] = value + value - earlier_ref[HALF - degree, at]
+            before = earlier_ref.at[HALF] if degree == 1 else own_ref.at[degree - 2]
+            pairs += [(before, own_ref.at[degree - 1]), (own_ref.at[degree - 1], own_ref.at[degree - 1])]
+    else:
+        for degree in range(HALF + 1):
+            for at in range(around):
+                own_ref[degree, at] = vectors[degree, at, 8:16, :]
+            if degree:
+                pairs.append((own_ref.at[degree - 1], own_ref.at[degree]))
+            pairs.append((own_ref.at[degree], own_ref.at[degree]))
     column = lax.broadcasted_iota(jnp.int32, (1, 128), 1)
-    gram = jnp.zeros((1, 128), F32)
-    number = 0
-
-    def own(index, at):
-        return earlier_ref[index, at] if index <= HALF else own_ref[index - HALF - 1, at]
-
-    for i in range(total):
-        sums = [jnp.zeros((8, 128), F32)] * (total - i)
-        for at in range(around):
-            left = own(i, at)
-            for j in range(i, total):
-                sums[j - i] = sums[j - i] + left * own(j, at)
-        for value in sums:
-            entry = jnp.sum(jnp.sum(value, axis=0, keepdims=True), axis=1, keepdims=True)
-            gram = jnp.where(column == number, jnp.broadcast_to(entry, (1, 128)), gram)
-            number += 1
-    gram_ref[...] = jnp.broadcast_to(gram, gram_ref.shape)
+    sums = previous_ref[0:1, :] if last else jnp.zeros((1, 128), F32)
+    for number, (left, right) in enumerate(pairs):
+        parts = [left[at] * right[at] for at in range(around)]
+        while len(parts) > 1:
+            parts = [a + b for a, b in zip(parts[::2], parts[1::2], strict=True)]
+        entry = jnp.sum(jnp.sum(parts[0], axis=0, keepdims=True), axis=1, keepdims=True)
+        place_of = number + (2 * HALF + 1 if last else 0)
+        sums = jnp.where(column == place_of, jnp.broadcast_to(entry, (1, 128)), sums)
+    sums_ref[...] = jnp.broadcast_to(sums, sums_ref.shape)
 
 
 def unpack_gram(all_ref, total):
     row = jnp.sum(all_ref[...], axis=0, keepdims=True)
-    gram, number = {}, 0
+    moments = []
+    for number in range(2 * total - 1):
+        entry = jnp.broadcast_to(row[:, number : number + 1], (1, 128))
+        moments.append(entry if number < 2 else entry + entry - moments[number % 2])
+    gram = {}
     for i in range(total):
         for j in range(i, total):
-            gram[i, j] = gram[j, i] = jnp.broadcast_to(row[:, number : number + 1], (1, 128))
-            number += 1
+            gram[i, j] = gram[j, i] = 0.5 * (moments[i + j] + moments[j - i])
     return gram
 
 
@@ -450,10 +455,8 @@
         if c is None:
             continue
         add(j, centre * c)
-        if j in (0, HALF):
-            add(j + 1, half_width * c)
-        else:
-            add(j + 1, half * c)
+        add(j + 1, (half if j else half_width) * c)
+        if j:
             add(j - 1, half * c)
     return result
 
@@ -503,7 +506,7 @@
                 tiles = [combine(pairs[number], early_ref, late_ref, 8 * b + 4 * half + a) for a in range(4)]
                 tiles = regroup(tiles)
                 for m in range(4):
-                    send_ref[4 * b + m, 2 * number + half] = tiles[m]
+                    send_ref[4 * b + m, half, number] = tiles[m]
 
 
 def deliver_kernel(path, u_ref, recv_ref, worst_ref, instead_updated_ref, instead_residual_ref, *refs):
@@ -511,16 +514,14 @@
     slab = lax.axis_index("slab")
     for source in range(recv_ref.shape[0]):
         start = pl.multiple_of(8 * place(slab, path[source], len(path)), 8)
-        for index in range(4):
-            turned[index, pl.ds(start, 8), :] = recv_ref[source, index]
+        for index in range(2):
+            turned[index, pl.ds(start, 8), :] = recv_ref[source, 0, index]
     good = jnp.broadcast_to(worst_ref[0:1, :] < MOST_LOST, (32, 128))
-    for half in range(2):
-        change = jnp.transpose(turned[half]).reshape(4, 32, 128)
-        residual = jnp.transpose(turned[2 + half]).reshape(4, 32, 128)
-        for i in range(4):
-            at = 4 * half + i
-            updated_ref[at] = jnp.where(good, u_ref[at] + change[i], instead_updated_ref[at])
-            residual_ref[at] = jnp.where(good, residual[i], instead_residual_ref[at])
+    change = jnp.transpose(turned[0]).reshape(4, 32, 128)
+    residual = jnp.transpose(turned[1]).reshape(4, 32, 128)
+    for i in range(4):
+        updated_ref[i] = jnp.where(good, u_ref[i] + change[i], instead_updated_ref[i])
+        residual_ref[i] = jnp.where(good, residual[i], instead_residual_ref[i])
 
 
 def sliced_body(
@@ -545,28 +546,26 @@
         return lax.ppermute(value, AXES, pairs + [(b, a) for a, b in pairs])
 
     def neighbours(to_chip, to_far):
-        return swap(0, to_chip), swap(1, to_far)
+        far = swap(1, to_far)
+        return swap(0, to_chip), far
 
     packed = pack_families(family_in, family_mid, family_out, family_tan)
-    typical = 0.5 + 0.33 * jnp.mean(jnp.sum(family_tan, axis=1))
-    centre = 1.1 + 1.4 * typical
-    half_width = centre - 0.4
-    scale = jnp.broadcast_to(jnp.stack([centre, 1.0 / half_width, half_width] + [centre] * 5)[:, None], (8, 128))
-
     capacity = size_x * size_y * size_z // 2
+    halves = pl.BlockSpec((4, 32, 128), lambda i: (i, 0, 0))
     (send,) = call(
         lambda *refs: spread_kernel(path, capacity, *refs),
-        [((peers, 8, 8, 128), F32)], [pltpu.VMEM((4, 2, 128, 128), F32)], "spread",
+        [((peers, 2, 4, 8, 128), F32)], [pltpu.VMEM((4, 128, 128), F32)], "spread",
         displacement, load_field, foundation, point_slot, plastic_flags,
+        grid=(2,), ins=[halves] * 5, outs=[pl.BlockSpec((peers, 1, 4, 8, 128), lambda i: (0, i, 0, 0, 0))],
     )
     recv = lax.all_to_all(send, GROUP, 0, 0, tiled=True)
     field = (around, 8, 128)
     edge = (around // 8, 8, 128)
     message = (around + around // 8, 8, 128)
-    strain, code, found, rest, to_chip, to_far = call(
+    strain, code, found, rest, to_chip, to_far, scale = call(
         lambda *refs: collect_kernel(around, *refs),
-        [((3,) + field, F32), (field, jnp.int32), (field, F32), (field, F32), (message, F32), (message, F32)],
-        [pltpu.VMEM(field, F32)], "collect", recv,
+        [((3,) + field, F32), (field, jnp.int32), (field, F32), (field, F32), (message, F32), (message, F32), ((8, 128), F32)],
+        [pltpu.VMEM(field, F32)], "collect", family_tan, recv,
     )
     chip, far = neighbours(to_chip, to_far)
     first = cells(strain, code, packed, families, 8, (1, 2, 3))
@@ -587,14 +586,14 @@
             "basis", scale, own[1], own_chip[1], own_far[1], found, chip, far, *vectors,
         )
 
-    (early,) = basis(False, [((HALF + 1,) + field, F32)], own[0], own_chip[0], own_far[0])
-    late, gram = basis(
-        True, [((HALF,) + field, F32), ((everyone, 128), F32)], early[HALF], *neighbours(early[HALF], early[HALF]), early
-    )
-    sums = lax.all_to_all(gram, AXES, 0, 0, tiled=True)
+    early, sums = basis(False, [((HALF + 1,) + field, F32), ((8, 128), F32)], own[0], own_chip[0], own_far[0])
+    late, sums = basis(
+        True, [((HALF,) + field, F32), ((everyone, 128), F32)], early[HALF], *neighbours(early[HALF], early[HALF]), early, sums
+    )
+    sums = lax.all_to_all(sums, AXES, 0, 0, tiled=True)
     send, worst = call(
         lambda *refs: last_kernel(around, *refs),
-        [((peers, 4, 8, 128), F32), ((8, 128), F32)], [], "last", scale, sums, early, late,
+        [((peers, 2, 2, 8, 128), F32), ((8, 128), F32)], [], "last", scale, sums, early, late,
     )
     recv = lax.all_to_all(send, GROUP, 0, 0, tiled=True)
     inputs = (
@@ -604,8 +603,15 @@
     instead = lax.cond(good, lambda: (jnp.zeros_like(displacement),) * 2, lambda: plain_body(*inputs))
     shape = displacement.shape
     return call(
-        lambda *refs: deliver_kernel(path, *refs), [(shape, F32), (shape, F32)], [pltpu.VMEM((4, 128, 128), F32)],
-        "deliver", displacement, recv, worst, *instead,
+        lambda *refs: deliver_kernel(path, *refs), [(shape, F32), (shape, F32)], [pltpu.VMEM((2, 128, 128), F32)],
+        "deliver", displacement, recv, worst, *instead, grid=(2,), outs=[halves] * 2,
+        ins=[
+            halves,
+            pl.BlockSpec((peers, 1, 2, 8, 128), lambda i: (0, i, 0, 0, 0)),
+            pl.BlockSpec((8, 128), lambda i: (0, 0)),
+            halves,
+            halves,
+        ],
     )
 
 

time: 111 us -> 110 us (level)
  transfers between devices with their start and end apart: 10 -> 10, of which waited for: 3 -> 4; matrix products, arithmetic and copies ran while one was open for 1% -> 1% of each run, Pallas kernels for 21% -> 21%
where the time goes in v4:
time: 110 us
  Pallas kernels  41.2 us (37%)
  starting transfers between devices  26 us (24%)
  waiting for transfers between devices  21.5 us (20%)
  blocking collectives  16.5 us (15%)
  local copies, waits for them, and re-layouts  2.88 us (3%)
  between operations  1.62 us (1%)
    pallas_call x3, Pallas kernels, cells(): pl.pallas_call(kernel, grid=(count // step,), in_specs=[pl.BlockSpec((3,...  30.3 us
    all_to_all x2, waiting for transfers between devices, sliced_body(): recv = lax.all_to_all(send, GROUP, 0, 0, tiled=True)  20.9 us
    all_to_all x1, blocking collectives, sliced_body(): sums = lax.all_to_all(sums, AXES, 0, 0, tiled=True)  16.5 us
    ppermute x8, starting transfers between devices, swap(): return lax.ppermute(value, AXES, pairs + [(b, a) for a, b in pairs])  14.8 us
    all_to_all x2, starting transfers between devices, sliced_body(): recv = lax.all_to_all(send, GROUP, 0, 0, tiled=True)  11.2 us
    pallas_call x7, Pallas kernels, call(): pl.pallas_call(kernel, out_shape=[jax.ShapeDtypeStruct(shape, dtype) for...  10.9 us
  transfers between devices with their start and end apart: 10, of which 4 were waited for; matrix products, arithmetic and copies ran while one was open for 1% of the time, Pallas kernels for 21%

profile of v4, /device:TPU:0, one launch (start us, length us, event | category | flops | bytes accessed | tf_op | source)
XLA Modules:
  0.0 109.8 jit_solution(4281773206590633345)
XLA Ops:
  0.6 2.1 %spread.1 = f32[16,2,4,8,128]{4,3,2,1,0:T(8,128)} custom-call(f32[8,32,128]{2,1,0:T(8,128)} %refs_0_.5, f32[8,32,128]{2,1,0:T(8,128)} %refs_1_.1, f32[8,32,128]{2,1,0:T(8,128)} %refs_2_.1, s32[8,32,128]{2,1,0:T(8,128)} %refs_3_.1, s32[8,32,128]{2,1,0:T(8,128)} %refs_4_.1), custom_call_target="tpu_custom_call" | custom-call | tf_op jit(solution)/shard_map/spread/pallas_call | solution.py:200
  2.7 7.5 %all-to-all-start.16 = ((f32[16,2,4,8,128]{4,3,2,1,0:T(8,128)}), f32[16,2,4,8,128]{4,3,2,1,0:T(8,128)S(1)}, u32[]{:S(2)}, u32[]{:S(2)}) async-start(f32[16,2,4,8,128]{4,3,2,1,0:T(8,128)} %spread.1), calls=%async_computation.16 | async-start | bytes 1048576 | tf_op jit(solution)/shard_map/all_to_all | solution.py:561
  10.3 0.7 copy-done.6
  11.2 0.6 copy-done.7
  11.9 0.7 copy-done.8
  12.7 12.1 %all-to-all-done.16.refs_1_ = f32[16,2,4,8,128]{4,3,2,1,0:T(8,128)S(1)} async-done(((f32[16,2,4,8,128]{4,3,2,1,0:T(8,128)}), f32[16,2,4,8,128]{4,3,2,1,0:T(8,128)S(1)}, u32[]{:S(2)}, u32[]{:S(2)}) %all-to-all-start.16) | async-done | bytes 524320 | tf_op jit(solution)/shard_map/all_to_all | solution.py:561
  24.7 0.6 collect.1
  25.4 0.7 collective-permute-start.67
  26.1 11.4 %cells.5.refs_0_ = f32[4,32,8,128]{3,2,1,0:T(8,128)S(1)} custom-call(f32[3,32,8,128]{3,2,1,0:T(8,128)S(1)} %get-tuple-element.47.refs_0_, s32[32,8,128]{2,1,0:T(8,128)S(1)} %get-tuple-element.48.refs_1_, bf16[256,48]{1,0:T(8,128)(2,1)S(1)} %copy.82.refs_2_, bf16[256,1024]{1,0:T(8,128)(2,1)S(1)} %bitcast.81, bf16[32,512]{1,0:T(8,128)(2,1)S(1)} %fusion.104.refs_4_), custom_call_target="tpu_custom_call" | custom-call | flops 8053063680 | bytes 393216 | tf_op jit(solution)/shard_map/cells/pallas_call | solution.py:107
  37.5 7.5 %cells.6.refs_1_ = f32[4,32,8,128]{3,2,1,0:T(8,128)S(1)} custom-call(f32[3,32,8,128]{3,2,1,0:T(8,128)S(1)} %get-tuple-element.47.refs_0_, s32[32,8,128]{2,1,0:T(8,128)S(1)} %get-tuple-element.48.refs_1_, bf16[256,48]{1,0:T(8,128)(2,1)S(1)} %copy.82.refs_2_, bf16[256,1024]{1,0:T(8,128)(2,1)S(1)} %bitcast.82, bf16[32,512]{1,0:T(8,128)(2,1)S(1)} %fusion.104.refs_4_, ...), custom_call_target="tpu_custom_call" | custom-call | flops 5368709120 | bytes 262144 | tf_op jit(solution)/shard_map/cells/pallas_call | solution.py:107
  45.0 2.6 %collective-permute-start.68 = (f32[4,8,128]{2,1,0:T(8,128)S(1)}, f32[4,8,128]{2,1,0:T(8,128)S(1)}, u32[]{:S(2)}, u32[]{:S(2)}) collective-permute-start(f32[4,8,128]{2,1,0:T(8,128)S(1)} %bitcast.136), channel_id=1, source_target_pairs={{0,1},{2,3},{11,10},{9,8},{16,17},{18,19},{27,26},{25,24},{28,29},... | collective-permute-start | bytes 49160 | tf_op jit(solution)/shard_map/ppermute | solution.py:546
  47.6 0.7 collective-permute-start.69
  48.3 11.4 %cells.7.refs_2_ = f32[4,32,8,128]{3,2,1,0:T(8,128)S(1)} custom-call(f32[3,32,8,128]{3,2,1,0:T(8,128)S(1)} %get-tuple-element.47.refs_0_, s32[32,8,128]{2,1,0:T(8,128)S(1)} %get-tuple-element.48.refs_1_, bf16[256,48]{1,0:T(8,128)(2,1)S(1)} %copy.82.refs_2_, bf16[256,1024]{1,0:T(8,128)(2,1)S(1)} %bitcast.83, bf16[32,512]{1,0:T(8,128)(2,1)S(1)} %fusion.104.refs_4_), custom_call_target="tpu_custom_call" | custom-call | flops 8053063680 | bytes 393216 | tf_op jit(solution)/shard_map/cells/pallas_call | solution.py:107
  59.9 2.7 %collective-permute-start.70 = (f32[2,32,8,128]{3,2,1,0:T(8,128)S(1)}, f32[2,32,8,128]{3,2,1,0:T(8,128)S(1)}, u32[]{:S(2)}, u32[]{:S(2)}) collective-permute-start(f32[2,32,8,128]{3,2,1,0:T(8,128)S(1)} %rhs.1), channel_id=1, source_target_pairs={{0,1},{2,3},{11,10},{9,8},{16,17},{18,19},{27,26},{25,24},{28,29},... | collective-permute-start | bytes 786440 | tf_op jit(solution)/shard_map/ppermute | solution.py:546
  62.6 0.7 collective-permute-start.71
  63.8 2.9 %basis.2 = (f32[5,32,8,128]{3,2,1,0:T(8,128)S(1)}, f32[8,128]{1,0:T(8,128)S(1)}) custom-call(f32[8,128]{1,0:T(8,128)S(1)} %get-tuple-element.46.refs_0_, f32[32,8,128]{2,1,0:T(8,128)S(1)} %get-tuple-element.225.refs_1_, f32[32,8,128]{2,1,0:T(8,128)S(1)} %get-tuple-element.223.refs_2_, f32[32,8,128]{2,1,0:T(8,128)S(1)} %get-tuple-element.221.refs_3_, ...), custom_call_target="tpu_custom_call" | custom-call | tf_op jit(solution)/shard_map/basis/pallas_call | solution.py:200
  66.7 6.6 %collective-permute-start.72 = (f32[32,8,128]{2,1,0:T(8,128)S(1)}, f32[32,8,128]{2,1,0:T(8,128)S(1)}, u32[]{:S(2)}, u32[]{:S(2)}) collective-permute-start(f32[32,8,128]{2,1,0:T(8,128)S(1)} %slice_bitcast_fusion.10.refs_7_), channel_id=1, source_target_pairs={{0,1},{2,3},{11,10},{9,8},{16,17},{18,19},{27,26},{25,24},{28,29},... | collective-permute-start | bytes 393224 | tf_op jit(solution)/shard_map/ppermute | solution.py:546
  73.3 0.8 collective-permute-start.73
  74.3 2.8 %basis.3 = (f32[4,32,8,128]{3,2,1,0:T(8,128)S(1)}, f32[32,128]{1,0:T(8,128)S(1)}) custom-call(f32[8,128]{1,0:T(8,128)S(1)} %get-tuple-element.46.refs_0_, f32[32,8,128]{2,1,0:T(8,128)S(1)} %get-tuple-element.225.refs_1_, f32[32,8,128]{2,1,0:T(8,128)S(1)} %get-tuple-element.223.refs_2_, f32[32,8,128]{2,1,0:T(8,128)S(1)} %get-tuple-element.221.refs_3_, ...), custom_call_target="tpu_custom_call" | custom-call | tf_op jit(solution)/shard_map/basis/pallas_call | solution.py:200
  77.1 16.5 %all_to_all.148 = f32[32,1,128]{2,1,0:T(1,128)S(1)} all-to-all(f32[32,1,128]{2,1,0:T(1,128)S(1)} %bitcast.87), channel_id=1, replica_groups=mesh['blk'=4,'slab'=2,'micro'=4] {'blk','slab','micro'}, dimensions={0} | all-to-all | bytes 32768 | tf_op jit(solution)/shard_map/all_to_all | solution.py:593
  93.6 1.5 %last.1 = (f32[16,2,2,8,128]{4,3,2,1,0:T(8,128)}, f32[8,128]{1,0:T(8,128)S(1)}) custom-call(f32[8,128]{1,0:T(8,128)S(1)} %get-tuple-element.46.refs_0_, f32[32,128]{1,0:T(8,128)S(1)} %bitcast.86, f32[5,32,8,128]{3,2,1,0:T(8,128)S(1)} %get-tuple-element.53.refs_10_.refs_2_, f32[4,32,8,128]{3,2,1,0:T(8,128)S(1)} %get-tuple-element.56.refs_3_), custom_call_target="tpu_custom_call" | custom-call | tf_op jit(solution)/shard_map/last/pallas_call | solution.py:200
  95.1 3.7 %all-to-all-start.18 = ((f32[16,2,2,8,128]{4,3,2,1,0:T(8,128)}), f32[16,2,2,8,128]{4,3,2,1,0:T(8,128)S(1)}, u32[]{:S(2)}, u32[]{:S(2)}) async-start(f32[16,2,2,8,128]{4,3,2,1,0:T(8,128)} %get-tuple-element.58), calls=%async_computation.18 | async-start | bytes 524288 | tf_op jit(solution)/shard_map/all_to_all | solution.py:598
  99.9 8.8 %all-to-all-done.18.refs_1_ = f32[16,2,2,8,128]{4,3,2,1,0:T(8,128)S(1)} async-done(((f32[16,2,2,8,128]{4,3,2,1,0:T(8,128)}), f32[16,2,2,8,128]{4,3,2,1,0:T(8,128)S(1)}, u32[]{:S(2)}, u32[]{:S(2)}) %all-to-all-start.18) | async-done | bytes 262176 | tf_op jit(solution)/shard_map/all_to_all | solution.py:598
  108.9 1.0 deliver.1
  (50 shorter events, 1.8 us)
Async XLA Ops:
  2.7 8.4 %copy-start.2 = (bf16[4,256,256]{2,1,0:T(8,128)(2,1)S(1)}, bf16[4,256,256]{2,1,0:T(8,128)(2,1)}, u32[]{:S(2)}) copy-start(bf16[4,256,256]{2,1,0:T(8,128)(2,1)} %param.17) | copy-start | bytes 1572868
  2.7 22.0 %all-to-all-start.16 = ((f32[16,2,4,8,128]{4,3,2,1,0:T(8,128)}), f32[16,2,4,8,128]{4,3,2,1,0:T(8,128)S(1)}, u32[]{:S(2)}, u32[]{:S(2)}) async-start(f32[16,2,4,8,128]{4,3,2,1,0:T(8,128)} %spread.1), calls=%async_computation.16 | async-start | bytes 1048576 | tf_op jit(solution)/shard_map/all_to_all | solution.py:561
  10.3 0.7 copy-start.6
  11.2 0.7 copy-start.7
  11.9 0.7 copy-start.8
  25.3 12.2 %collective-permute-start.66 = (f32[36,8,128]{2,1,0:T(8,128)S(1)}, f32[36,8,128]{2,1,0:T(8,128)S(1)}, u32[]{:S(2)}, u32[]{:S(2)}) collective-permute-start(f32[36,8,128]{2,1,0:T(8,128)S(1)} %get-tuple-element.49), channel_id=1, source_target_pairs={{0,1},{2,3},{11,10},{9,8},{16,17},{18,19},{27,26},{25,24},{28,29},... | collective-permute-start | bytes 442376 | tf_op jit(solution)/shard_map/ppermute | solution.py:546
  25.4 12.1 %collective-permute-start.67 = (f32[36,8,128]{2,1,0:T(8,128)S(1)}, f32[36,8,128]{2,1,0:T(8,128)S(1)}, u32[]{:S(2)}, u32[]{:S(2)}) collective-permute-start(f32[36,8,128]{2,1,0:T(8,128)S(1)} %get-tuple-element.50), channel_id=1, source_target_pairs={{1,2},{3,11},{10,9},{8,16},{17,18},{19,27},{26,25},{24,28},{29,30}... | collective-permute-start | bytes 442376 | tf_op jit(solution)/shard_map/ppermute | solution.py:546
  45.0 14.6 %collective-permute-start.68 = (f32[4,8,128]{2,1,0:T(8,128)S(1)}, f32[4,8,128]{2,1,0:T(8,128)S(1)}, u32[]{:S(2)}, u32[]{:S(2)}) collective-permute-start(f32[4,8,128]{2,1,0:T(8,128)S(1)} %bitcast.136), channel_id=1, source_target_pairs={{0,1},{2,3},{11,10},{9,8},{16,17},{18,19},{27,26},{25,24},{28,29},... | collective-permute-start | bytes 49160 | tf_op jit(solution)/shard_map/ppermute | solution.py:546
  47.6 12.1 %collective-permute-start.69 = (f32[4,8,128]{2,1,0:T(8,128)S(1)}, f32[4,8,128]{2,1,0:T(8,128)S(1)}, u32[]{:S(2)}, u32[]{:S(2)}) collective-permute-start(f32[4,8,128]{2,1,0:T(8,128)S(1)} %bitcast.135), channel_id=1, source_target_pairs={{1,2},{3,11},{10,9},{8,16},{17,18},{19,27},{26,25},{24,28},{29,30}... | collective-permute-start | bytes 49160 | tf_op jit(solution)/shard_map/ppermute | solution.py:546
  59.9 3.9 %collective-permute-start.70 = (f32[2,32,8,128]{3,2,1,0:T(8,128)S(1)}, f32[2,32,8,128]{3,2,1,0:T(8,128)S(1)}, u32[]{:S(2)}, u32[]{:S(2)}) collective-permute-start(f32[2,32,8,128]{3,2,1,0:T(8,128)S(1)} %rhs.1), channel_id=1, source_target_pairs={{0,1},{2,3},{11,10},{9,8},{16,17},{18,19},{27,26},{25,24},{28,29},... | collective-permute-start | bytes 786440 | tf_op jit(solution)/shard_map/ppermute | solution.py:546
  62.6 1.2 %collective-permute-start.71 = (f32[2,32,8,128]{3,2,1,0:T(8,128)S(1)}, f32[2,32,8,128]{3,2,1,0:T(8,128)S(1)}, u32[]{:S(2)}, u32[]{:S(2)}) collective-permute-start(f32[2,32,8,128]{3,2,1,0:T(8,128)S(1)} %rhs.1), channel_id=1, source_target_pairs={{1,2},{3,11},{10,9},{8,16},{17,18},{19,27},{26,25},{24,28},{29,30}... | collective-permute-start | bytes 786440 | tf_op jit(solution)/shard_map/ppermute | solution.py:546
  66.7 7.6 %collective-permute-start.72 = (f32[32,8,128]{2,1,0:T(8,128)S(1)}, f32[32,8,128]{2,1,0:T(8,128)S(1)}, u32[]{:S(2)}, u32[]{:S(2)}) collective-permute-start(f32[32,8,128]{2,1,0:T(8,128)S(1)} %slice_bitcast_fusion.10.refs_7_), channel_id=1, source_target_pairs={{0,1},{2,3},{11,10},{9,8},{16,17},{18,19},{27,26},{25,24},{28,29},... | collective-permute-start | bytes 393224 | tf_op jit(solution)/shard_map/ppermute | solution.py:546
  73.3 1.0 collective-permute-start.73
  93.6 15.2 %copy-start.5 = (s32[8,32,128]{2,1,0:T(8,128)S(1)}, s32[8,32,128]{2,1,0:T(8,128)}, u32[]{:S(2)}) copy-start(s32[8,32,128]{2,1,0:T(8,128)} %refs_4_.1) | copy-start | bytes 393220
  95.1 13.7 %copy-start = (f32[8,32,128]{2,1,0:T(8,128)S(1)}, f32[8,32,128]{2,1,0:T(8,128)}, u32[]{:S(2)}) copy-start(f32[8,32,128]{2,1,0:T(8,128)} %refs_2_.1) | copy-start | bytes 393220
  95.1 13.7 %copy-start.1 = (f32[8,32,128]{2,1,0:T(8,128)S(1)}, f32[8,32,128]{2,1,0:T(8,128)}, u32[]{:S(2)}) copy-start(f32[8,32,128]{2,1,0:T(8,128)} %refs_0_.5) | copy-start | bytes 393220
  95.1 13.7 %copy-start.3 = (f32[8,32,128]{2,1,0:T(8,128)S(1)}, f32[8,32,128]{2,1,0:T(8,128)}, u32[]{:S(2)}) copy-start(f32[8,32,128]{2,1,0:T(8,128)} %refs_1_.1) | copy-start | bytes 393220
  95.1 13.7 %copy-start.4 = (s32[8,32,128]{2,1,0:T(8,128)S(1)}, s32[8,32,128]{2,1,0:T(8,128)}, u32[]{:S(2)}) copy-start(s32[8,32,128]{2,1,0:T(8,128)} %refs_3_.1) | copy-start | bytes 393220
  95.1 13.7 %all-to-all-start.18 = ((f32[16,2,2,8,128]{4,3,2,1,0:T(8,128)}), f32[16,2,2,8,128]{4,3,2,1,0:T(8,128)S(1)}, u32[]{:S(2)}, u32[]{:S(2)}) async-start(f32[16,2,2,8,128]{4,3,2,1,0:T(8,128)} %get-tuple-element.58), calls=%async_computation.18 | async-start | bytes 524288 | tf_op jit(solution)/shard_map/all_to_all | solution.py:598

commit v5 on v4

--- a/solution.py
+++ b/solution.py
@@ -22,7 +22,6 @@
     spread = jnp.concatenate([spread, spread], axis=2).reshape(modes, 6 * families)
     high, low = split(spread)
     weight_in = jnp.concatenate([high, low], axis=1)
-    weight_mid = jnp.transpose(family_mid, (1, 0, 2)).reshape(modes, families * modes)
     none = jnp.zeros((families, 1, modes), BF)
     stress = jnp.concatenate([family_out, none], axis=1).reshape(4 * families, modes)
     none = jnp.zeros((families, 3, modes), BF)
@@ -36,62 +35,97 @@
         ],
         axis=0,
     )
-    return weight_in, weight_mid, weight_out
-
-
-def cells_kernel(families, planes, strain_ref, code_ref, in_ref, mid_ref, out_ref, *refs):
+    return weight_in, family_mid, weight_out
+
+
+def cells_kernel(families, planes, strain_ref, code_ref, in_ref, mid_ref, out_ref, *refs, info_ref=None):
     *edges, answer_ref = refs
     modes = in_ref.shape[0]
-    spots = [(a, x) for a in range(code_ref.shape[0]) for x in planes]
+    step = code_ref.shape[0]
+    spots = [(a + i, x) for a in range(0, step, 2) for x in planes for i in range(2)]
     width = len(spots) * 128
-    place = lax.broadcasted_iota(jnp.int32, (2 * families, 128), 0)
-    column, family_row, flag_row = [], [], []
-    for a, x in spots:
-        code = code_ref[a, pl.ds(x, 1), :]
-        family = lax.shift_right_logical(code, 1)
-        picked = lax.rem(place, families) == jnp.broadcast_to(family, place.shape)
-        pieces = []
-        for j in range(3):
-            value = strain_ref[j, a, pl.ds(x, 1), :]
-            if edges and j == 2:
-                even, chip_ref, far_ref = edges
-                chip, far = chip_ref[0, pl.ds(a, 1), :], far_ref[0, pl.ds(a, 1), :]
-                beyond = jnp.where(even[...] == (1 if x == 7 else 0), chip, far) * 0.5
-                value = value - beyond if x == 0 else value + beyond
-            value = jnp.broadcast_to(value, place.shape)
-            high = value.astype(BF).astype(F32)
-            piece = jnp.where(place < families, high, value - high)
-            pieces.append(jnp.where(picked, piece, 0.0))
-        column.append(jnp.concatenate(pieces, axis=0))
-        family_row.append(family)
-        flag_row.append(lax.bitwise_and(code, 1))
-    spread = jnp.concatenate(column, axis=1).astype(BF)
-    spread = jnp.concatenate([spread, spread], axis=0)
-    family = jnp.concatenate(family_row, axis=1)
-    flag = jnp.concatenate(flag_row, axis=1)
-    modal = jnp.dot(in_ref[...], spread, preferred_element_type=F32)
-    flagged = jnp.broadcast_to(flag, (modes, width)) > 0
-    active = jnp.where(flagged, jnp.tanh(modal), modal).astype(BF)
-    wide = jnp.broadcast_to(family, (modes, width)).astype(BF)
-    nothing = jnp.zeros_like(active)
-    stacked = jnp.concatenate(
-        [jnp.where(wide == jnp.array(f, BF), active, nothing) for f in range(families)], axis=0
-    )
-    hidden = jnp.dot(mid_ref[...], stacked, preferred_element_type=F32)
-    bounded = jnp.tanh(hidden).astype(BF)
-    both = jnp.concatenate([bounded, bounded * bounded], axis=0)
-    result = jnp.dot(out_ref[...], both, preferred_element_type=F32)
-    result = result[: 4 * families] + result[4 * families :]
-    owner = lax.shift_right_logical(lax.broadcasted_iota(jnp.int32, (4 * families, width), 0), 2)
-    result = jnp.where(owner == family, result, 0.0)
-    total = result[:4]
-    for f in range(1, families):
-        total = total + result[4 * f : 4 * f + 4]
-    for i, (a, x) in enumerate(spots):
-        answer_ref[:, a, x, :] = total[:, i * 128 : (i + 1) * 128]
-
-
-def cells(strain, code, packed, families, step, planes, *edges):
+
+    def evaluate(pairs):
+        place = lax.broadcasted_iota(jnp.int32, (2 * families, 128), 0)
+        column, family_row, flag_row = [], [], []
+        for a, x in spots:
+            code = code_ref[a, pl.ds(x, 1), :]
+            family = lax.shift_right_logical(code, 1)
+            picked = lax.rem(place, families) == jnp.broadcast_to(family, place.shape)
+            pieces = []
+            for j in range(3):
+                value = strain_ref[j, a, pl.ds(x, 1), :]
+                if edges and j == 2:
+                    even, chip_ref, far_ref = edges
+                    chip, far = chip_ref[0, pl.ds(a, 1), :], far_ref[0, pl.ds(a, 1), :]
+                    beyond = jnp.where(even[...] == (1 if x == 7 else 0), chip, far) * 0.5
+                    value = value - beyond if x == 0 else value + beyond
+                value = jnp.broadcast_to(value, place.shape)
+                high = value.astype(BF).astype(F32)
+                piece = jnp.where(place < families, high, value - high)
+                pieces.append(jnp.where(picked, piece, 0.0))
+            column.append(jnp.concatenate(pieces, axis=0))
+            family_row.append(family)
+            flag_row.append(lax.bitwise_and(code, 1))
+        spread = jnp.concatenate(column, axis=1).astype(BF)
+        spread = jnp.concatenate([spread, spread], axis=0)
+        family = jnp.concatenate(family_row, axis=1)
+        flag = jnp.concatenate(flag_row, axis=1)
+        modal = jnp.dot(in_ref[...], spread, preferred_element_type=F32)
+        flagged = jnp.broadcast_to(flag, (modes, width)) > 0
+        active = jnp.where(flagged, jnp.tanh(modal), modal).astype(BF)
+        if pairs is None:
+            wide = jnp.broadcast_to(family, (modes, width)).astype(BF)
+            nothing = jnp.zeros_like(active)
+            stacked = jnp.concatenate(
+                [jnp.where(wide == jnp.array(f, BF), active, nothing) for f in range(families)], axis=0
+            )
+            mixing = jnp.concatenate([mid_ref[f] for f in range(families)], axis=1)
+            hidden = jnp.dot(mixing, stacked, preferred_element_type=F32)
+        else:
+            nothing = jnp.zeros((modes, 256), BF)
+            parts = []
+            for number, (one, other) in enumerate(pairs):
+                part = slice(256 * number, 256 * number + 256)
+                ours = jnp.where(family[:, part] == one, 1.0, 0.0)
+                ours = jnp.broadcast_to(ours, (modes, 256)).astype(BF) > jnp.array(0.5, BF)
+                mine = active[:, part]
+                stacked = jnp.concatenate([jnp.where(ours, mine, nothing), jnp.where(ours, nothing, mine)], axis=0)
+                mixing = jnp.concatenate([mid_ref[one], mid_ref[other]], axis=1)
+                parts.append(jnp.dot(mixing, stacked, preferred_element_type=F32))
+            hidden = jnp.concatenate(parts, axis=1)
+        bounded = jnp.tanh(hidden).astype(BF)
+        both = jnp.concatenate([bounded, bounded * bounded], axis=0)
+        result = jnp.dot(out_ref[...], both, preferred_element_type=F32)
+        result = result[: 4 * families] + result[4 * families :]
+        owner = lax.shift_right_logical(lax.broadcasted_iota(jnp.int32, (4 * families, width), 0), 2)
+        result = jnp.where(owner == family, result, 0.0)
+        total = result[:4]
+        for f in range(1, families):
+            total = total + result[4 * f : 4 * f + 4]
+        for i, (a, x) in enumerate(spots):
+            answer_ref[:, a, x, :] = total[:, i * 128 : (i + 1) * 128]
+
+    if info_ref is None:
+        evaluate(None)
+        return
+    first = pl.program_id(0) * (step // 2)
+    pairs, more = [], 0
+    for a in range(step // 2):
+        for x in planes:
+            pairs.append((info_ref[x, first + a], info_ref[x, 16 + first + a]))
+            more = more + info_ref[x, 32 + first + a]
+
+    @pl.when(more == 0)
+    def _():
+        evaluate(pairs)
+
+    @pl.when(more != 0)
+    def _():
+        evaluate(None)
+
+
+def cells(strain, code, packed, families, step, planes, *edges, info=None):
     weight_in, weight_mid, weight_out = packed
     count = code.shape[0]
     planes = tuple(planes)
@@ -99,31 +133,38 @@
     modes = weight_in.shape[0]
 
     def whole(array):
-        return pl.BlockSpec(array.shape, lambda i: (0,) * array.ndim)
+        return pl.BlockSpec(array.shape, lambda i, *_: (0,) * array.ndim)
 
     def kernel(*refs):
-        cells_kernel(families, planes, *refs)
-
+        if info is None:
+            cells_kernel(families, planes, *refs)
+        else:
+            cells_kernel(families, planes, *refs[1:], info_ref=refs[0])
+
+    scalars = () if info is None else (info,)
     return pl.pallas_call(
         kernel,
-        grid=(count // step,),
-        in_specs=[
-            pl.BlockSpec((3, step, 8, 128), lambda i: (0, i, 0, 0)),
-            pl.BlockSpec((step, 8, 128), lambda i: (i, 0, 0)),
-            whole(weight_in),
-            whole(weight_mid),
-            whole(weight_out),
-        ]
-        + [pl.BlockSpec((1, 128), lambda i: (0, 0)) for _ in edges[:1]]
-        + [pl.BlockSpec((1, 8, 128), lambda i: (count + i, 0, 0)) for _ in edges[1:]],
-        out_specs=pl.BlockSpec((4, step, 8, 128), lambda i: (0, i, 0, 0)),
+        grid_spec=pltpu.PrefetchScalarGridSpec(
+            num_scalar_prefetch=len(scalars),
+            grid=(count // step,),
+            in_specs=[
+                pl.BlockSpec((3, step, 8, 128), lambda i, *_: (0, i, 0, 0)),
+                pl.BlockSpec((step, 8, 128), lambda i, *_: (i, 0, 0)),
+                whole(weight_in),
+                whole(weight_mid),
+                whole(weight_out),
+            ]
+            + [pl.BlockSpec((1, 128), lambda i, *_: (0, 0)) for _ in edges[:1]]
+            + [pl.BlockSpec((1, 8, 128), lambda i, *_: (count + i, 0, 0)) for _ in edges[1:]],
+            out_specs=pl.BlockSpec((4, step, 8, 128), lambda i, *_: (0, i, 0, 0)),
+        ),
         out_shape=jax.ShapeDtypeStruct((4, count, 8, 128), F32),
         compiler_params=pltpu.CompilerParams(vmem_limit_bytes=48 * 2**20),
         cost_estimate=pl.CostEstimate(
             flops=2 * points * modes * modes * (families + 1), bytes_accessed=points * 32, transcendentals=2 * points * modes
         ),
         name="cells",
-    )(strain, code, weight_in, weight_mid, weight_out, *edges)
+    )(*scalars, strain, code, weight_in, weight_mid, weight_out, *edges)
 
 
 def global_sum(value):
@@ -299,7 +340,92 @@
         far_ref[index] = jnp.where(even, bottom, top)
 
 
-def rhs_kernel(around, peers, first_ref, outer_ref, second_ref, rest_ref, chip_ref, far_ref, own_ref, low_ref, high_ref):
+def network(count):
+    pairs = []
+    p = 1
+    while p < count:
+        k = p
+        while k >= 1:
+            for j in range(k % p, count - k, 2 * k):
+                for i in range(j, min(j + k, count - k)):
+                    if i // (2 * p) == (i + k) // (2 * p):
+                        pairs.append((i, i + k))
+            k //= 2
+        p *= 2
+    return pairs
+
+
+def sort_tiles(keys, *carried):
+    keys, carried = list(keys), [list(c) for c in carried]
+    for i, j in network(len(keys)):
+        wrong = keys[i] > keys[j]
+        keys[i], keys[j] = jnp.minimum(keys[i], keys[j]), jnp.maximum(keys[i], keys[j])
+        for c in carried:
+            c[i], c[j] = jnp.where(wrong, c[j], c[i]), jnp.where(wrong, c[i], c[j])
+    return keys, carried
+
+
+def take(tile, index):
+    return jnp.take_along_axis(tile, index, axis=1, mode="promise_in_bounds")
+
+
+def arrange_kernel(around, strain_ref, code_ref, sorted_ref, sorted_code_ref, rank_ref, origin_ref, info_ref):
+    lane = lax.broadcasted_iota(jnp.int32, (8, 128), 1)
+    right = lax.shift_right_logical
+    keys, strains = [], [[], [], []]
+    for at in range(around):
+        code = code_ref[at]
+        shift = right(code, 1) * 8
+        counts = lax.shift_left(jnp.ones((8, 128), jnp.int32), shift)
+        for step in (1, 2, 4, 8, 16, 32, 64):
+            counts = counts + jnp.where(lane >= step, pltpu.roll(counts, step, 1), 0)
+        total = jnp.broadcast_to(counts[:, 127:128], (8, 128))
+        first = total & 255
+        second = first + (right(total, 8) & 255)
+        third = second + (right(total, 16) & 255)
+
+        def start(family):
+            return jnp.where(
+                family < 2, jnp.where(family < 1, 0, first), jnp.where(family < 3, second, third)
+            )
+
+        turn = (at % 8 * 16 + at // 8 * 4) % 128
+        rank_ref[at] = (start(right(code, 1)) + (right(counts, shift) & 255) + (turn - 1)) & 127
+        spot = (lane + (128 - turn)) & 127
+        family = (
+            jnp.where(spot >= first, 1, 0) + jnp.where(spot >= second, 1, 0) + jnp.where(spot >= third, 1, 0)
+        )
+        wanted = spot - start(family)
+        shift = family * 8
+        source = jnp.zeros((8, 128), jnp.int32)
+        for step in (64, 32, 16, 8, 4, 2, 1):
+            seen = right(take(counts, source + (step - 1)), shift) & 255
+            source = jnp.where(seen <= wanted, source + step, source)
+        moved = take(code, source)
+        keys.append(lax.shift_left(right(moved, 1), jnp.full((8, 128), 6, jnp.int32)) + (2 * at) + (moved & 1))
+        for j in range(3):
+            strains[j].append(take(strain_ref[j, at], source))
+    keys, strains = sort_tiles(keys, *strains)
+    info = jnp.zeros((8, 128), jnp.int32)
+    for at in range(around):
+        family = right(keys[at], 6)
+        sorted_code_ref[at] = 2 * family + (keys[at] & 1)
+        origin_ref[at] = right(keys[at], 1) & 31
+        for j in range(3):
+            sorted_ref[j, at] = strains[j][at]
+        if at % 2:
+            before = right(keys[at - 1], 6)
+            low = jnp.min(jnp.minimum(before, family), axis=1, keepdims=True)
+            high = jnp.max(jnp.maximum(before, family), axis=1, keepdims=True)
+            low, high = jnp.broadcast_to(low, (8, 128)), jnp.broadcast_to(high, (8, 128))
+            odd = jnp.where((family != low) & (family != high), 1, 0) + jnp.where((before != low) & (before != high), 1, 0)
+            odd = jnp.broadcast_to(jnp.max(odd, axis=1, keepdims=True), (8, 128))
+            for number, value in enumerate((low, high, odd)):
+                info = jnp.where(lane == 16 * number + at // 2, value, info)
+    info_ref[...] = info
+
+
+def rhs_kernel(around, peers, first_ref, outer_ref, second_ref, rank_ref, origin_ref, rest_ref, chip_ref, far_ref, own_ref, low_ref, high_ref, answers):
     _, _, even = whereabouts(peers)
     for index in range(around // 8):
         low_ref[index] = jnp.where(even, far_ref[index], chip_ref[index])
@@ -307,9 +433,14 @@
     row = lax.broadcasted_iota(jnp.int32, (8, 128), 0)
     rim = (row == 0) | (row == 7)
 
+    moved = [[jnp.where(row < 4, first_ref[j, at], second_ref[j, at]) for at in range(around)] for j in range(4)]
+    _, moved = sort_tiles([origin_ref[at] for at in range(around)], *moved)
+    for at in range(around):
+        for j in range(4):
+            answers[j, at] = jnp.where(rim, outer_ref[j, at], take(moved[j][at], rank_ref[at]))
+
     def answer(number, at):
-        inner = jnp.where(row < 4, first_ref[number, at], second_ref[number, at])
-        return jnp.where(rim, outer_ref[number, at], inner)
+        return answers[number, at]
 
     cycle = [answer(0, at) for at in range(around)]
     for at in range(around):
@@ -568,14 +699,19 @@
         [pltpu.VMEM(field, F32)], "collect", family_tan, recv,
     )
     chip, far = neighbours(to_chip, to_far)
-    first = cells(strain, code, packed, families, 8, (1, 2, 3))
+    grouped, grouped_code, rank, origin, info = call(
+        lambda *refs: arrange_kernel(around, *refs),
+        [((3,) + field, F32), (field, jnp.int32), (field, jnp.int32), (field, jnp.int32), ((8, 128), jnp.int32)],
+        [], "arrange", strain, code,
+    )
+    first = cells(grouped, grouped_code, packed, families, 8, (1, 2, 3), info=info)
     outer = cells(strain, code, packed, families, 8, (0, 7), jnp.broadcast_to(even.astype(jnp.int32), (1, 128)), chip, far)
     top, bottom = outer[2, :, 7].reshape(edge), outer[2, :, 0].reshape(edge)
     edge_chip, edge_far = neighbours(jnp.where(even, top, bottom), jnp.where(even, bottom, top))
-    second = cells(strain, code, packed, families, 8, (4, 5, 6))
+    second = cells(grouped, grouped_code, packed, families, 8, (4, 5, 6), info=info)
     (own,) = call(
-        lambda *refs: rhs_kernel(around, peers, *refs), [((2,) + field, F32)], [pltpu.VMEM(edge, F32)] * 2, "rhs",
-        first, outer, second, rest, edge_chip, edge_far,
+        lambda *refs: rhs_kernel(around, peers, *refs), [((2,) + field, F32)], [pltpu.VMEM(edge, F32)] * 2 + [pltpu.VMEM((4,) + field, F32)], "rhs",
+        first, outer, second, rank, origin, rest, edge_chip, edge_far,
     )
     own_chip, own_far = neighbours(own, own)
 

time: 110 us -> 108 us (0.982)
  Pallas kernels: 41.2 us -> 38.9 us
    pallas_call x3, Pallas kernels: 30.3 us -> 25.3 us  [cells(): pl.pallas_call(kernel, grid_spec=pltpu.PrefetchScalarGridSpec(num_scalar_...]
    pallas_call x7 -> x8, Pallas kernels: 10.9 us -> 13.7 us  [call(): pl.pallas_call(kernel, out_shape=[jax.ShapeDtypeStruct(shape, dtype) for...]
  transfers between devices with their start and end apart: 10 -> 10, of which waited for: 4 -> 4; matrix products, arithmetic and copies ran while one was open for 1% -> 1% of each run, Pallas kernels for 21% -> 18%
where the time goes in v5:
time: 108 us
  Pallas kernels  38.9 us (36%)
  starting transfers between devices  25.8 us (24%)
  waiting for transfers between devices  21.8 us (20%)
  blocking collectives  16.5 us (15%)
  local copies, waits for them, and re-layouts  2.77 us (3%)
  between operations  1.63 us (2%)
    pallas_call x3, Pallas kernels, cells(): pl.pallas_call(kernel, grid_spec=pltpu.PrefetchScalarGridSpec(num_scalar_...  25.3 us
    all_to_all x2, waiting for transfers between devices, sliced_body(): recv = lax.all_to_all(send, GROUP, 0, 0, tiled=True)  21 us
    all_to_all x1, blocking collectives, sliced_body(): sums = lax.all_to_all(sums, AXES, 0, 0, tiled=True)  16.5 us
    ppermute x8, starting transfers between devices, swap(): return lax.ppermute(value, AXES, pairs + [(b, a) for a, b in pairs])  14.8 us
    pallas_call x8, Pallas kernels, call(): pl.pallas_call(kernel, out_shape=[jax.ShapeDtypeStruct(shape, dtype) for...  13.7 us
    all_to_all x2, starting transfers between devices, sliced_body(): recv = lax.all_to_all(send, GROUP, 0, 0, tiled=True)  11.1 us
  transfers between devices with their start and end apart: 10, of which 4 were waited for; matrix products, arithmetic and copies ran while one was open for 1% of the time, Pallas kernels for 18%

profile of v5, /device:TPU:0, one launch (start us, length us, event | category | flops | bytes accessed | tf_op | source)
XLA Modules:
  0.0 107.8 jit_solution(10246062777537194487)
XLA Ops:
  0.6 2.1 %spread.1 = f32[16,2,4,8,128]{4,3,2,1,0:T(8,128)} custom-call(f32[8,32,128]{2,1,0:T(8,128)} %refs_0_.5, f32[8,32,128]{2,1,0:T(8,128)} %refs_1_.1, f32[8,32,128]{2,1,0:T(8,128)} %refs_2_.1, s32[8,32,128]{2,1,0:T(8,128)} %refs_3_.2, s32[8,32,128]{2,1,0:T(8,128)} %refs_4_.3), custom_call_target="tpu_custom_call" | custom-call | tf_op jit(solution)/shard_map/spread/pallas_call | solution.py:241
  2.7 7.4 %all-to-all-start.16 = ((f32[16,2,4,8,128]{4,3,2,1,0:T(8,128)}), f32[16,2,4,8,128]{4,3,2,1,0:T(8,128)S(1)}, u32[]{:S(2)}, u32[]{:S(2)}) async-start(f32[16,2,4,8,128]{4,3,2,1,0:T(8,128)} %spread.1), calls=%async_computation.16 | async-start | bytes 1048576 | tf_op jit(solution)/shard_map/all_to_all | solution.py:692
  10.2 0.7 copy-done.5
  11.7 0.7 copy-done.7
  12.4 12.2 %all-to-all-done.16.refs_1_ = f32[16,2,4,8,128]{4,3,2,1,0:T(8,128)S(1)} async-done(((f32[16,2,4,8,128]{4,3,2,1,0:T(8,128)}), f32[16,2,4,8,128]{4,3,2,1,0:T(8,128)S(1)}, u32[]{:S(2)}, u32[]{:S(2)}) %all-to-all-start.16) | async-done | bytes 524320 | tf_op jit(solution)/shard_map/all_to_all | solution.py:692
  25.2 0.7 collective-permute-start.67
  25.9 2.0 %arrange.1 = (f32[3,32,8,128]{3,2,1,0:T(8,128)S(1)}, s32[32,8,128]{2,1,0:T(8,128)S(1)}, s32[32,8,128]{2,1,0:T(8,128)S(1)}, s32[32,8,128]{2,1,0:T(8,128)S(1)}, s32[8,128]{1,0:T(8,128)S(1)}) custom-call(f32[3,32,8,128]{3,2,1,0:T(8,128)S(1)} %get-tuple-element.52.refs_0_, s32[32,8,128]{2,1,0:T(8,128)S(1)} %get-tuple-element.53.refs_1_), custom_call_target="tpu_custom_call" | custom-call | tf_op jit(solution)/shard_map/arrange/pallas_call | solution.py:241
  27.9 8.8 %cells.5.refs_0_ = f32[4,32,8,128]{3,2,1,0:T(8,128)S(1)} custom-call(s32[8,128]{1,0:T(8,128)S(1)} %get-tuple-element.54.refs_0_, f32[3,32,8,128]{3,2,1,0:T(8,128)S(1)} %get-tuple-element.55.refs_1_, s32[32,8,128]{2,1,0:T(8,128)S(1)} %get-tuple-element.56.refs_2_, bf16[256,48]{1,0:T(8,128)(2,1)S(1)} %copy.73.refs_3_.refs_2_, ...), custom_call_target="tpu_custom_call" | custom-call | flops 8053063680 | bytes 393216 | tf_op jit(solution)/shard_map/cells/pallas_call | solution.py:145
  36.8 7.6 %cells.6.refs_1_ = f32[4,32,8,128]{3,2,1,0:T(8,128)S(1)} custom-call(f32[3,32,8,128]{3,2,1,0:T(8,128)S(1)} %get-tuple-element.52.refs_0_, s32[32,8,128]{2,1,0:T(8,128)S(1)} %get-tuple-element.53.refs_1_, bf16[256,48]{1,0:T(8,128)(2,1)S(1)} %copy.73.refs_3_.refs_2_, bf16[4,256,256]{2,1,0:T(8,128)(2,1)S(1)} %copy-done.8, ...), custom_call_target="tpu_custom_call" | custom-call | flops 5368709120 | bytes 262144 | tf_op jit(solution)/shard_map/cells/pallas_call | solution.py:145
  44.5 2.6 %collective-permute-start.68 = (f32[4,8,128]{2,1,0:T(8,128)S(1)}, f32[4,8,128]{2,1,0:T(8,128)S(1)}, u32[]{:S(2)}, u32[]{:S(2)}) collective-permute-start(f32[4,8,128]{2,1,0:T(8,128)S(1)} %bitcast.124), channel_id=1, source_target_pairs={{0,1},{2,3},{11,10},{9,8},{16,17},{18,19},{27,26},{25,24},{28,29},... | collective-permute-start | bytes 49160 | tf_op jit(solution)/shard_map/ppermute | solution.py:677
  47.0 0.8 collective-permute-start.69
  47.9 8.8 %cells.7.refs_2_ = f32[4,32,8,128]{3,2,1,0:T(8,128)S(1)} custom-call(s32[8,128]{1,0:T(8,128)S(1)} %get-tuple-element.54.refs_0_, f32[3,32,8,128]{3,2,1,0:T(8,128)S(1)} %get-tuple-element.55.refs_1_, s32[32,8,128]{2,1,0:T(8,128)S(1)} %get-tuple-element.56.refs_2_, bf16[256,48]{1,0:T(8,128)(2,1)S(1)} %copy.73.refs_3_.refs_2_, ...), custom_call_target="tpu_custom_call" | custom-call | flops 8053063680 | bytes 393216 | tf_op jit(solution)/shard_map/cells/pallas_call | solution.py:145
  56.7 0.9 rhs.1
  57.6 2.8 %collective-permute-start.70 = (f32[2,32,8,128]{3,2,1,0:T(8,128)S(1)}, f32[2,32,8,128]{3,2,1,0:T(8,128)S(1)}, u32[]{:S(2)}, u32[]{:S(2)}) collective-permute-start(f32[2,32,8,128]{3,2,1,0:T(8,128)S(1)} %rhs.1), channel_id=1, source_target_pairs={{0,1},{2,3},{11,10},{9,8},{16,17},{18,19},{27,26},{25,24},{28,29},... | collective-permute-start | bytes 786440 | tf_op jit(solution)/shard_map/ppermute | solution.py:677
  60.3 0.7 collective-permute-start.71
  61.6 2.9 %basis.2 = (f32[5,32,8,128]{3,2,1,0:T(8,128)S(1)}, f32[8,128]{1,0:T(8,128)S(1)}) custom-call(f32[8,128]{1,0:T(8,128)S(1)} %get-tuple-element.51.refs_0_, f32[32,8,128]{2,1,0:T(8,128)S(1)} %get-tuple-element.235.refs_1_, f32[32,8,128]{2,1,0:T(8,128)S(1)} %get-tuple-element.233.refs_2_, f32[32,8,128]{2,1,0:T(8,128)S(1)} %get-tuple-element.231.refs_3_, ...), custom_call_target="tpu_custom_call" | custom-call | tf_op jit(solution)/shard_map/basis/pallas_call | solution.py:241
  64.4 6.6 %collective-permute-start.72 = (f32[32,8,128]{2,1,0:T(8,128)S(1)}, f32[32,8,128]{2,1,0:T(8,128)S(1)}, u32[]{:S(2)}, u32[]{:S(2)}) collective-permute-start(f32[32,8,128]{2,1,0:T(8,128)S(1)} %slice_bitcast_fusion.10.refs_7_), channel_id=1, source_target_pairs={{0,1},{2,3},{11,10},{9,8},{16,17},{18,19},{27,26},{25,24},{28,29},... | collective-permute-start | bytes 393224 | tf_op jit(solution)/shard_map/ppermute | solution.py:677
  71.0 0.7 collective-permute-start.73
  72.0 2.8 %basis.3 = (f32[4,32,8,128]{3,2,1,0:T(8,128)S(1)}, f32[32,128]{1,0:T(8,128)S(1)}) custom-call(f32[8,128]{1,0:T(8,128)S(1)} %get-tuple-element.51.refs_0_, f32[32,8,128]{2,1,0:T(8,128)S(1)} %get-tuple-element.235.refs_1_, f32[32,8,128]{2,1,0:T(8,128)S(1)} %get-tuple-element.233.refs_2_, f32[32,8,128]{2,1,0:T(8,128)S(1)} %get-tuple-element.231.refs_3_, ...), custom_call_target="tpu_custom_call" | custom-call | tf_op jit(solution)/shard_map/basis/pallas_call | solution.py:241
  74.8 16.5 %all_to_all.148 = f32[32,1,128]{2,1,0:T(1,128)S(1)} all-to-all(f32[32,1,128]{2,1,0:T(1,128)S(1)} %bitcast.77), channel_id=1, replica_groups=mesh['blk'=4,'slab'=2,'micro'=4] {'blk','slab','micro'}, dimensions={0} | all-to-all | bytes 32768 | tf_op jit(solution)/shard_map/all_to_all | solution.py:729
  91.4 1.5 %last.1 = (f32[16,2,2,8,128]{4,3,2,1,0:T(8,128)}, f32[8,128]{1,0:T(8,128)S(1)}) custom-call(f32[8,128]{1,0:T(8,128)S(1)} %get-tuple-element.51.refs_0_, f32[32,128]{1,0:T(8,128)S(1)} %bitcast.76, f32[5,32,8,128]{3,2,1,0:T(8,128)S(1)} %get-tuple-element.63.refs_10_.refs_2_, f32[4,32,8,128]{3,2,1,0:T(8,128)S(1)} %get-tuple-element.66.refs_3_), custom_call_target="tpu_custom_call" | custom-call | tf_op jit(solution)/shard_map/last/pallas_call | solution.py:241
  92.8 3.7 %all-to-all-start.18 = ((f32[16,2,2,8,128]{4,3,2,1,0:T(8,128)}), f32[16,2,2,8,128]{4,3,2,1,0:T(8,128)S(1)}, u32[]{:S(2)}, u32[]{:S(2)}) async-start(f32[16,2,2,8,128]{4,3,2,1,0:T(8,128)} %get-tuple-element.68), calls=%async_computation.18 | async-start | bytes 524288 | tf_op jit(solution)/shard_map/all_to_all | solution.py:734
  97.7 8.8 %all-to-all-done.18.refs_1_ = f32[16,2,2,8,128]{4,3,2,1,0:T(8,128)S(1)} async-done(((f32[16,2,2,8,128]{4,3,2,1,0:T(8,128)}), f32[16,2,2,8,128]{4,3,2,1,0:T(8,128)S(1)}, u32[]{:S(2)}, u32[]{:S(2)}) %all-to-all-start.18) | async-done | bytes 262176 | tf_op jit(solution)/shard_map/all_to_all | solution.py:734
  106.9 1.0 deliver.1
  (50 shorter events, 3.2 us)
Async XLA Ops:
  2.7 21.9 %all-to-all-start.16 = ((f32[16,2,4,8,128]{4,3,2,1,0:T(8,128)}), f32[16,2,4,8,128]{4,3,2,1,0:T(8,128)S(1)}, u32[]{:S(2)}, u32[]{:S(2)}) async-start(f32[16,2,4,8,128]{4,3,2,1,0:T(8,128)} %spread.1), calls=%async_computation.16 | async-start | bytes 1048576 | tf_op jit(solution)/shard_map/all_to_all | solution.py:692
  10.1 0.7 copy-start.5
  10.9 0.7 copy-start.6
  11.6 0.7 copy-start.7
  12.4 15.6 %copy-start.8 = (bf16[4,256,256]{2,1,0:T(8,128)(2,1)S(1)}, bf16[4,256,256]{2,1,0:T(8,128)(2,1)}, u32[]{:S(2)}) copy-start(bf16[4,256,256]{2,1,0:T(8,128)(2,1)} %refs_4_.5) | copy-start | bytes 1572868
  25.1 11.6 %collective-permute-start.66 = (f32[36,8,128]{2,1,0:T(8,128)S(1)}, f32[36,8,128]{2,1,0:T(8,128)S(1)}, u32[]{:S(2)}, u32[]{:S(2)}) collective-permute-start(f32[36,8,128]{2,1,0:T(8,128)S(1)} %get-tuple-element.57), channel_id=1, source_target_pairs={{0,1},{2,3},{11,10},{9,8},{16,17},{18,19},{27,26},{25,24},{28,29},... | collective-permute-start | bytes 442376 | tf_op jit(solution)/shard_map/ppermute | solution.py:677
  25.2 11.6 %collective-permute-start.67 = (f32[36,8,128]{2,1,0:T(8,128)S(1)}, f32[36,8,128]{2,1,0:T(8,128)S(1)}, u32[]{:S(2)}, u32[]{:S(2)}) collective-permute-start(f32[36,8,128]{2,1,0:T(8,128)S(1)} %get-tuple-element.58), channel_id=1, source_target_pairs={{1,2},{3,11},{10,9},{8,16},{17,18},{19,27},{26,25},{24,28},{29,30}... | collective-permute-start | bytes 442376 | tf_op jit(solution)/shard_map/ppermute | solution.py:677
  44.5 12.2 %collective-permute-start.68 = (f32[4,8,128]{2,1,0:T(8,128)S(1)}, f32[4,8,128]{2,1,0:T(8,128)S(1)}, u32[]{:S(2)}, u32[]{:S(2)}) collective-permute-start(f32[4,8,128]{2,1,0:T(8,128)S(1)} %bitcast.124), channel_id=1, source_target_pairs={{0,1},{2,3},{11,10},{9,8},{16,17},{18,19},{27,26},{25,24},{28,29},... | collective-permute-start | bytes 49160 | tf_op jit(solution)/shard_map/ppermute | solution.py:677
  47.0 9.7 %collective-permute-start.69 = (f32[4,8,128]{2,1,0:T(8,128)S(1)}, f32[4,8,128]{2,1,0:T(8,128)S(1)}, u32[]{:S(2)}, u32[]{:S(2)}) collective-permute-start(f32[4,8,128]{2,1,0:T(8,128)S(1)} %bitcast.123), channel_id=1, source_target_pairs={{1,2},{3,11},{10,9},{8,16},{17,18},{19,27},{26,25},{24,28},{29,30}... | collective-permute-start | bytes 49160 | tf_op jit(solution)/shard_map/ppermute | solution.py:677
  57.6 3.9 %collective-permute-start.70 = (f32[2,32,8,128]{3,2,1,0:T(8,128)S(1)}, f32[2,32,8,128]{3,2,1,0:T(8,128)S(1)}, u32[]{:S(2)}, u32[]{:S(2)}) collective-permute-start(f32[2,32,8,128]{3,2,1,0:T(8,128)S(1)} %rhs.1), channel_id=1, source_target_pairs={{0,1},{2,3},{11,10},{9,8},{16,17},{18,19},{27,26},{25,24},{28,29},... | collective-permute-start | bytes 786440 | tf_op jit(solution)/shard_map/ppermute | solution.py:677
  60.3 1.2 %collective-permute-start.71 = (f32[2,32,8,128]{3,2,1,0:T(8,128)S(1)}, f32[2,32,8,128]{3,2,1,0:T(8,128)S(1)}, u32[]{:S(2)}, u32[]{:S(2)}) collective-permute-start(f32[2,32,8,128]{3,2,1,0:T(8,128)S(1)} %rhs.1), channel_id=1, source_target_pairs={{1,2},{3,11},{10,9},{8,16},{17,18},{19,27},{26,25},{24,28},{29,30}... | collective-permute-start | bytes 786440 | tf_op jit(solution)/shard_map/ppermute | solution.py:677
  64.4 7.6 %collective-permute-start.72 = (f32[32,8,128]{2,1,0:T(8,128)S(1)}, f32[32,8,128]{2,1,0:T(8,128)S(1)}, u32[]{:S(2)}, u32[]{:S(2)}) collective-permute-start(f32[32,8,128]{2,1,0:T(8,128)S(1)} %slice_bitcast_fusion.10.refs_7_), channel_id=1, source_target_pairs={{0,1},{2,3},{11,10},{9,8},{16,17},{18,19},{27,26},{25,24},{28,29},... | collective-permute-start | bytes 393224 | tf_op jit(solution)/shard_map/ppermute | solution.py:677
  71.0 1.0 collective-permute-start.73
  91.4 15.2 %copy-start.4 = (s32[8,32,128]{2,1,0:T(8,128)S(1)}, s32[8,32,128]{2,1,0:T(8,128)}, u32[]{:S(2)}) copy-start(s32[8,32,128]{2,1,0:T(8,128)} %refs_4_.3) | copy-start | bytes 393220
  92.8 13.7 %copy-start = (f32[8,32,128]{2,1,0:T(8,128)S(1)}, f32[8,32,128]{2,1,0:T(8,128)}, u32[]{:S(2)}) copy-start(f32[8,32,128]{2,1,0:T(8,128)} %refs_2_.1) | copy-start | bytes 393220
  92.8 13.7 %copy-start.1 = (f32[8,32,128]{2,1,0:T(8,128)S(1)}, f32[8,32,128]{2,1,0:T(8,128)}, u32[]{:S(2)}) copy-start(f32[8,32,128]{2,1,0:T(8,128)} %refs_0_.5) | copy-start | bytes 393220
  92.8 13.7 %copy-start.2 = (f32[8,32,128]{2,1,0:T(8,128)S(1)}, f32[8,32,128]{2,1,0:T(8,128)}, u32[]{:S(2)}) copy-start(f32[8,32,128]{2,1,0:T(8,128)} %refs_1_.1) | copy-start | bytes 393220
  92.8 13.7 %copy-start.3 = (s32[8,32,128]{2,1,0:T(8,128)S(1)}, s32[8,32,128]{2,1,0:T(8,128)}, u32[]{:S(2)}) copy-start(s32[8,32,128]{2,1,0:T(8,128)} %refs_3_.2) | copy-start | bytes 393220
  92.8 13.7 %all-to-all-start.18 = ((f32[16,2,2,8,128]{4,3,2,1,0:T(8,128)}), f32[16,2,2,8,128]{4,3,2,1,0:T(8,128)S(1)}, u32[]{:S(2)}, u32[]{:S(2)}) async-start(f32[16,2,2,8,128]{4,3,2,1,0:T(8,128)} %get-tuple-element.68), calls=%async_computation.18 | async-start | bytes 524288 | tf_op jit(solution)/shard_map/all_to_all | solution.py:734

commit v6 on v5

--- a/solution.py
+++ b/solution.py
@@ -303,6 +303,10 @@
     return (after - before) * 0.5
 
 
+def row_of(at):
+    return at % 8 // 2 * 8 + at // 8 * 2 + at % 2
+
+
 def collect_kernel(around, tan_ref, recv_ref, strain_ref, code_ref, found_ref, rest_ref, chip_ref, far_ref, scale_ref, u):
     _, _, even = whereabouts(recv_ref.shape[0])
     typical = jnp.sum(jnp.sum(tan_ref[...], axis=1, keepdims=True), axis=0, keepdims=True) / tan_ref.shape[0]
@@ -320,9 +324,8 @@
                     elif number == 1:
                         code_ref[at] = tiles[a].astype(jnp.int32)
                     elif number == 2:
-                        found_ref[at] = tiles[a]
-                        chip_ref[at] = tiles[a]
-                        far_ref[at] = tiles[a]
+                        rows = pl.ds(row_of(at), 8, stride=around)
+                        found_ref[rows, :] = tiles[a]
                     else:
                         rest_ref[at] = tiles[a]
     nothing = jnp.zeros((1, 128), F32)
@@ -334,6 +337,10 @@
         strain_ref[2, at] = (after - before) * 0.5
         chip_ref[around + at // 8, pl.ds(at % 8, 1), :] = tile[7:8]
         far_ref[around + at // 8, pl.ds(at % 8, 1), :] = tile[0:1]
+    for index in range(around):
+        value = found_ref[8 * index : 8 * index + 8, :]
+        chip_ref[index] = value
+        far_ref[index] = value
     for index in range(around, around + around // 8):
         bottom, top = far_ref[index], chip_ref[index]
         chip_ref[index] = jnp.where(even, top, bottom)
@@ -449,89 +456,154 @@
         after, before = beside(answer(2, at), low, high)
         divergence = (cycle[(at + 1) % around] - cycle[(at - 1) % around]) * 0.5
         divergence = divergence + radial(answer(1, at)) + (after - before) * 0.5
-        own_ref[0, at] = rest_ref[at] + divergence
-        own_ref[1, at] = 0.5 + answer(3, at)
+        rows = pl.ds(row_of(at), 8, stride=around)
+        own_ref[0, rows, :] = rest_ref[at] + divergence
+        own_ref[1, rows, :] = 0.5 + answer(3, at)
 
 
 HALF = ITERS // 2
 MOST_LOST = 1.0e5
 
 
-def basis_kernel(
-    around, peers, last, scale_ref, tan_ref, tan_chip_ref, tan_far_ref, found_ref, found_chip_ref, found_far_ref,
-    seed_ref, seed_chip_ref, seed_far_ref, *refs
+def tile(plane, quarter):
+    return slice(32 * plane + 8 * quarter, 32 * plane + 8 * quarter + 8)
+
+
+def three(peers, own_ref, chip_ref, far_ref, put):
+    _, _, even = whereabouts(peers)
+    for plane in range(8):
+        for quarter in range(4):
+            rows = tile(plane, quarter)
+            chip, far = chip_ref[rows, :], far_ref[rows, :]
+            put(plane, quarter, jnp.where(even, far, chip))
+            put(plane + 8, quarter, own_ref[rows, :])
+            put(plane + 16, quarter, jnp.where(even, chip, far))
+
+
+def within_plane(here):
+    lane = lax.broadcasted_iota(jnp.int32, (8, 128), 1)
+    even_row = lax.broadcasted_iota(jnp.int32, (8, 128), 0) % 2 == 0
+    up = [pltpu.roll(value, 7, 0) for value in here]
+    down = [pltpu.roll(value, 1, 0) for value in here]
+    result = []
+    for quarter in range(4):
+        after = jnp.where(even_row, up[quarter], down[quarter + 1] if quarter < 3 else up[0])
+        before = jnp.where(even_row, up[quarter - 1] if quarter else down[3], down[quarter])
+        outer = jnp.where(lane == 127, 0.0, pltpu.roll(here[quarter], 127, 1))
+        inner = jnp.where(lane == 0, 0.0, pltpu.roll(here[quarter], 1, 1))
+        out = jnp.where(lane >= 126, 0.0, outer)
+        result.append((after, out, pltpu.roll(out, 2, 1), (after + before) + (outer + inner)))
+    return result
+
+
+def own_kernel(scale_ref, tan_ref, found_ref, main_ref, after_ref, out_ref, back_ref):
+    centre, inverse = scale_ref[0:1, :], scale_ref[1:2, :]
+    for plane in range(8):
+        parts = within_plane([tan_ref[tile(plane, quarter), :] * (0.25 * inverse) for quarter in range(4)])
+        for quarter, (after, out, back, total) in enumerate(parts):
+            rows = tile(plane, quarter)
+            main_ref[rows, :] = (found_ref[rows, :] - centre) * inverse + total
+            after_ref[rows, :] = after
+            out_ref[rows, :] = out
+            back_ref[rows, :] = back
+
+
+def operator_kernel(
+    peers, scale_ref, tan_ref, tan_chip_ref, tan_far_ref, own_main_ref, own_after_ref, own_out_ref, own_back_ref,
+    found_chip_ref, found_far_ref, tan, main, after, out, back
 ):
+    centre, inverse = scale_ref[0:1, :], scale_ref[1:2, :]
+    _, _, even = whereabouts(peers)
+
+    def put_tan(plane, quarter, value):
+        tan[tile(plane, quarter), :] = value * (0.25 * inverse)
+
+    three(peers, tan_ref, tan_chip_ref, tan_far_ref, put_tan)
+    for plane in range(2, 22):
+        inside = 8 <= plane < 16
+        if not inside:
+            parts = within_plane([tan[tile(plane, quarter), :] for quarter in range(4)])
+        for quarter in range(4):
+            rows = tile(plane, quarter)
+            if inside:
+                own = tile(plane - 8, quarter)
+                total = own_main_ref[own, :]
+                after[rows, :] = own_after_ref[own, :]
+                out[rows, :] = own_out_ref[own, :]
+                back[rows, :] = own_back_ref[own, :]
+            else:
+                after[rows, :], out[rows, :], back[rows, :], total = parts[quarter]
+                there = tile(plane % 8, quarter)
+                chip, far = found_chip_ref[there, :], found_far_ref[there, :]
+                found = jnp.where(even, far, chip) if plane < 8 else jnp.where(even, chip, far)
+                total = total + (found - centre) * inverse
+            axial = tan[tile(plane + 1, quarter), :] + tan[tile(plane - 1, quarter), :]
+            main[rows, :] = total + axial
+
+
+def basis_kernel(peers, last, *refs):
     if last:
-        earlier_ref, previous_ref, own_ref, sums_ref, *scratch = refs
+        tan, main, after, out, back, seed_ref, seed_chip_ref, seed_far_ref, earlier_ref, previous_ref, *refs = refs
+        own_ref, sums_ref, vectors = refs
     else:
-        own_ref, sums_ref, *scratch = refs
-    tan, main, off_r, back_r, off_x, back_x, vectors = scratch
-    centre, inverse = scale_ref[0:1, :], scale_ref[1:2, :]
-    is_first, is_last, even = whereabouts(peers)
-    lane = lax.broadcasted_iota(jnp.int32, (24, 128), 1)
-    plane = lax.broadcasted_iota(jnp.int32, (24, 128), 0)
-    cut = ((plane == 7) & is_first) | ((plane == 14) & is_last)
-    quarter = 0.25 * inverse
-
-    def three(own, chip, far):
-        return jnp.concatenate([jnp.where(even, far, chip), own, jnp.where(even, chip, far)], axis=0)
-
-    for at in range(around):
-        tan[at] = three(tan_ref[at], tan_chip_ref[at], tan_far_ref[at]) * quarter
-    for at in range(around):
-        here = tan[at]
-        up_a, down_a = tan[(at + 1) % around], tan[(at - 1) % around]
-        up_r = jnp.where(lane == 127, 0.0, pltpu.roll(here, 127, 1))
-        down_r = jnp.where(lane == 0, 0.0, pltpu.roll(here, 1, 1))
-        up_x = pltpu.roll(here, 23, 0)
-        down_x = pltpu.roll(here, 1, 0)
-        found = three(found_ref[at], found_chip_ref[at], found_far_ref[at])
-        main[at] = (found - centre) * inverse + ((up_a + down_a) + (up_r + down_r) + (up_x + down_x))
-        beyond = jnp.where(lane >= 126, 0.0, up_r)
-        off_r[at] = beyond
-        back_r[at] = pltpu.roll(beyond, 2, 1)
-        beyond = jnp.where(cut, 0.0, up_x)
-        off_x[at] = beyond
-        back_x[at] = pltpu.roll(beyond, 2, 0)
-
-    def apply(index, at):
-        value = vectors[index, at]
-        result = main[at] * value
-        result = result - tan[(at + 1) % around] * vectors[index, (at + 2) % around]
-        result = result - tan[(at - 1) % around] * vectors[index, (at - 2) % around]
-        result = result - off_r[at] * pltpu.roll(value, 126, 1) - back_r[at] * pltpu.roll(value, 2, 1)
-        return result - off_x[at] * pltpu.roll(value, 22, 0) - back_x[at] * pltpu.roll(value, 2, 0)
-
-    for at in range(around):
-        vectors[0, at] = three(seed_ref[at], seed_chip_ref[at], seed_far_ref[at])
+        operator_refs, (seed_ref, seed_chip_ref, seed_far_ref), refs = refs[:10], refs[10:13], refs[13:]
+        own_ref, sums_ref, tan, main, after, out, back, vectors = refs
+        operator_kernel(peers, *operator_refs, tan, main, after, out, back)
+    is_first, is_last, _ = whereabouts(peers)
+
+    def put_seed(plane, quarter, value):
+        vectors[0, tile(plane, quarter), :] = value
+
+    three(peers, seed_ref, seed_chip_ref, seed_far_ref, put_seed)
+
+    def axial(between, plane, degree, quarter):
+        term = tan[tile(between, quarter), :] * vectors[degree, tile(plane, quarter), :]
+        if between == 8 or between == 15:
+            term = jnp.where(is_first if between == 8 else is_last, 0.0, term)
+        return term
+
+    def apply(degree, plane, quarter):
+        rows = tile(plane, quarter)
+        value = vectors[degree, rows, :]
+        result = main[rows, :] * value
+        if quarter < 3:
+            result = result - after[rows, :] * vectors[degree, tile(plane, quarter + 1), :]
+        else:
+            result = result - after[rows, :] * pltpu.roll(vectors[degree, tile(plane, 0), :], 6, 0)
+        before = tile(plane, (quarter - 1) % 4)
+        product = after[before, :] * vectors[degree, before, :]
+        result = result - (product if quarter else pltpu.roll(product, 2, 0))
+        result = result - out[rows, :] * pltpu.roll(value, 126, 1) - back[rows, :] * pltpu.roll(value, 2, 1)
+        return result - axial(plane + 1, plane + 2, degree, quarter) - axial(plane - 1, plane - 2, degree, quarter)
+
     for degree in range(1, HALF + 1):
-        for at in range(around):
-            value = apply(degree - 1, at)
-            if degree > 1:
-                value = value + value - vectors[degree - 2, at]
-            vectors[degree, at] = value
+        for plane in range(2 * degree, 24 - 2 * degree):
+            for quarter in range(4):
+                value = apply(degree - 1, plane, quarter)
+                if degree > 1:
+                    value = value + value - vectors[degree - 2, tile(plane, quarter), :]
+                vectors[degree, tile(plane, quarter), :] = value
+    own_tiles = [(tile(plane, quarter), tile(plane + 8, quarter)) for plane in range(8) for quarter in range(4)]
     pairs = []
     if last:
         for degree in range(1, HALF + 1):
-            for at in range(around):
-                value = vectors[degree, at, 8:16, :]
-                own_ref[degree - 1, at] = value + value - earlier_ref[HALF - degree, at]
+            for rows, wide_rows in own_tiles:
+                value = vectors[degree, wide_rows, :]
+                own_ref[degree - 1, rows, :] = value + value - earlier_ref[HALF - degree, rows, :]
             before = earlier_ref.at[HALF] if degree == 1 else own_ref.at[degree - 2]
             pairs += [(before, own_ref.at[degree - 1]), (own_ref.at[degree - 1], own_ref.at[degree - 1])]
     else:
         for degree in range(HALF + 1):
-            for at in range(around):
-                own_ref[degree, at] = vectors[degree, at, 8:16, :]
+            for rows, wide_rows in own_tiles:
+                own_ref[degree, rows, :] = vectors[degree, wide_rows, :]
             if degree:
                 pairs.append((own_ref.at[degree - 1], own_ref.at[degree]))
             pairs.append((own_ref.at[degree], own_ref.at[degree]))
     column = lax.broadcasted_iota(jnp.int32, (1, 128), 1)
     sums = previous_ref[0:1, :] if last else jnp.zeros((1, 128), F32)
     for number, (left, right) in enumerate(pairs):
-        parts = [left[at] * right[at] for at in range(around)]
-        while len(parts) > 1:
-            parts = [a + b for a, b in zip(parts[::2], parts[1::2], strict=True)]
-        entry = jnp.sum(jnp.sum(parts[0], axis=0, keepdims=True), axis=1, keepdims=True)
+        total = tree([left[rows, :] * right[rows, :] for rows, _ in own_tiles])
+        entry = jnp.sum(jnp.sum(total, axis=0, keepdims=True), axis=1, keepdims=True)
         place_of = number + (2 * HALF + 1 if last else 0)
         sums = jnp.where(column == place_of, jnp.broadcast_to(entry, (1, 128)), sums)
     sums_ref[...] = jnp.broadcast_to(sums, sums_ref.shape)
@@ -550,20 +622,20 @@
     return gram
 
 
+def tree(terms):
+    while len(terms) > 1:
+        terms = [a + b for a, b in zip(terms[::2], terms[1::2])] + ([terms[-1]] if len(terms) % 2 else [])
+    return terms[0]
+
+
 def dot(gram, left, right):
-    total = len(left)
-    result = None
-    for i in range(total):
-        if left[i] is None:
-            continue
-        inner = None
-        for j in range(total):
-            if right[j] is not None:
-                term = gram[i, j] * right[j]
-                inner = term if inner is None else inner + term
-        if inner is not None:
-            result = left[i] * inner if result is None else result + left[i] * inner
-    return result
+    return tree(
+        [
+            a * tree([gram[i, j] * b for j, b in enumerate(right) if b is not None])
+            for i, a in enumerate(left)
+            if a is not None
+        ]
+    )
 
 
 def axpy(scale, left, right):
@@ -605,10 +677,7 @@
         change = axpy(alpha, direction, change)
         residual = axpy(-alpha, image, residual)
         following = dot(gram, residual, residual)
-        bound = None
-        for c, n in zip(residual, norms, strict=True):
-            if c is not None:
-                bound = jnp.abs(c) * n if bound is None else bound + jnp.abs(c) * n
+        bound = tree([jnp.abs(c) * n for c, n in zip(residual, norms, strict=True) if c is not None])
         worst = jnp.maximum(worst, bound * bound / following)
         worst = jnp.where(following > 0.0, worst, jnp.inf)
         if step < ITERS - 1:
@@ -617,24 +686,26 @@
     return change, residual, worst
 
 
-def combine(coefficients, early_ref, late_ref, at):
-    result = None
-    for index, c in enumerate(coefficients):
-        if c is not None:
-            vector = early_ref[index, at] if index <= HALF else late_ref[index - HALF - 1, at]
-            result = c * vector if result is None else result + c * vector
-    return result
-
-
-def last_kernel(around, scale_ref, all_ref, early_ref, late_ref, send_ref, worst_ref):
+def last_kernel(around, scale_ref, all_ref, early_ref, late_ref, send_ref, worst_ref, results):
     total = 2 * HALF + 1
     change, residual, worst = iterate(unpack_gram(all_ref, total), total, scale_ref[0:1, :], scale_ref[2:3, :])
     worst_ref[...] = jnp.broadcast_to(worst, (8, 128))
-    pairs = [[None if c is None else jnp.broadcast_to(c, (8, 128)) for c in part] for part in (change, residual)]
-    for b in range(around // 8):
-        for half in range(2):
-            for number in range(2):
-                tiles = [combine(pairs[number], early_ref, late_ref, 8 * b + 4 * half + a) for a in range(4)]
+    for number, part in enumerate((change, residual)):
+        part = [None if c is None else jnp.broadcast_to(c, (8, 128)) for c in part]
+        for start in range(0, 8 * around, 8):
+            rows = slice(start, start + 8)
+            results[number, rows, :] = tree(
+                [
+                    c * (early_ref[index, rows, :] if index <= HALF else late_ref[index - HALF - 1, rows, :])
+                    for index, c in enumerate(part)
+                    if c is not None
+                ]
+            )
+        for b in range(around // 8):
+            for half in range(2):
+                tiles = [
+                    results[number, pl.ds(row_of(8 * b + 4 * half + a), 8, stride=around), :] for a in range(4)
+                ]
                 tiles = regroup(tiles)
                 for m in range(4):
                     send_ref[4 * b + m, half, number] = tiles[m]
@@ -692,10 +763,11 @@
     recv = lax.all_to_all(send, GROUP, 0, 0, tiled=True)
     field = (around, 8, 128)
     edge = (around // 8, 8, 128)
+    rows = (8 * around, 128)
     message = (around + around // 8, 8, 128)
     strain, code, found, rest, to_chip, to_far, scale = call(
         lambda *refs: collect_kernel(around, *refs),
-        [((3,) + field, F32), (field, jnp.int32), (field, F32), (field, F32), (message, F32), (message, F32), ((8, 128), F32)],
+        [((3,) + field, F32), (field, jnp.int32), (rows, F32), (field, F32), (message, F32), (message, F32), ((8, 128), F32)],
         [pltpu.VMEM(field, F32)], "collect", family_tan, recv,
     )
     chip, far = neighbours(to_chip, to_far)
@@ -708,28 +780,33 @@
     outer = cells(strain, code, packed, families, 8, (0, 7), jnp.broadcast_to(even.astype(jnp.int32), (1, 128)), chip, far)
     top, bottom = outer[2, :, 7].reshape(edge), outer[2, :, 0].reshape(edge)
     edge_chip, edge_far = neighbours(jnp.where(even, top, bottom), jnp.where(even, bottom, top))
+    grouped, outer = lax.optimization_barrier((grouped, outer))
     second = cells(grouped, grouped_code, packed, families, 8, (4, 5, 6), info=info)
     (own,) = call(
-        lambda *refs: rhs_kernel(around, peers, *refs), [((2,) + field, F32)], [pltpu.VMEM(edge, F32)] * 2 + [pltpu.VMEM((4,) + field, F32)], "rhs",
+        lambda *refs: rhs_kernel(around, peers, *refs), [((2,) + rows, F32)], [pltpu.VMEM(edge, F32)] * 2 + [pltpu.VMEM((4,) + field, F32)], "rhs",
         first, outer, second, rank, origin, rest, edge_chip, edge_far,
     )
     own_chip, own_far = neighbours(own, own)
 
-    def basis(last, outputs, *vectors):
-        return call(
-            lambda *refs: basis_kernel(around, peers, last, *refs), outputs,
-            [pltpu.VMEM((around, 24, 128), F32)] * 6 + [pltpu.VMEM((HALF + 1, around, 24, 128), F32)],
-            "basis", scale, own[1], own_chip[1], own_far[1], found, chip, far, *vectors,
-        )
-
-    early, sums = basis(False, [((HALF + 1,) + field, F32), ((8, 128), F32)], own[0], own_chip[0], own_far[0])
-    late, sums = basis(
-        True, [((HALF,) + field, F32), ((everyone, 128), F32)], early[HALF], *neighbours(early[HALF], early[HALF]), early, sums
+    tall = (24 * around, 128)
+    vectors = [pltpu.VMEM((HALF + 1,) + tall, F32)]
+    inside = call(
+        own_kernel, [(rows, F32)] * 4, [], "own", scale, own[1], found,
+    )
+    early, sums, *operator = call(
+        lambda *refs: basis_kernel(peers, False, *refs),
+        [((HALF + 1,) + rows, F32), ((8, 128), F32)] + [(tall, F32)] * 5, vectors, "basis",
+        scale, own[1], own_chip[1], own_far[1], *inside, chip[:around].reshape(rows), far[:around].reshape(rows),
+        own[0], own_chip[0], own_far[0],
+    )
+    late, sums = call(
+        lambda *refs: basis_kernel(peers, True, *refs), [((HALF,) + rows, F32), ((everyone, 128), F32)], vectors, "basis",
+        *operator, early[HALF], *neighbours(early[HALF], early[HALF]), early, sums,
     )
     sums = lax.all_to_all(sums, AXES, 0, 0, tiled=True)
     send, worst = call(
         lambda *refs: last_kernel(around, *refs),
-        [((peers, 2, 2, 8, 128), F32), ((8, 128), F32)], [], "last", scale, sums, early, late,
+        [((peers, 2, 2, 8, 128), F32), ((8, 128), F32)], [pltpu.VMEM((2,) + rows, F32)], "last", scale, sums, early, late,
     )
     recv = lax.all_to_all(send, GROUP, 0, 0, tiled=True)
     inputs = (

time: 108 us -> 105 us (0.972)
  Pallas kernels: 38.9 us -> 36.4 us
    pallas_call x8 -> x9, Pallas kernels: 13.7 us -> 11.1 us  [call(): pl.pallas_call(kernel, out_shape=[jax.ShapeDtypeStruct(shape, dtype) for...]
  transfers between devices with their start and end apart: 10 -> 10, of which waited for: 4 -> 4; matrix products, arithmetic and copies ran while one was open for 1% -> 1% of each run, Pallas kernels for 18% -> 19%
where the time goes in v6:
time: 105 us
  Pallas kernels  36.4 us (35%)
  starting transfers between devices  25.1 us (24%)
  waiting for transfers between devices  22.3 us (21%)
  blocking collectives  16.3 us (16%)
  local copies, waits for them, and re-layouts  2.78 us (3%)
  between operations  1.64 us (2%)
    pallas_call x3, Pallas kernels, cells(): pl.pallas_call(kernel, grid_spec=pltpu.PrefetchScalarGridSpec(num_scalar_...  25.2 us
    all_to_all x2, waiting for transfers between devices, sliced_body(): recv = lax.all_to_all(send, GROUP, 0, 0, tiled=True)  21 us
    all_to_all x1, blocking collectives, sliced_body(): sums = lax.all_to_all(sums, AXES, 0, 0, tiled=True)  16.3 us
    ppermute x8, starting transfers between devices, swap(): return lax.ppermute(value, AXES, pairs + [(b, a) for a, b in pairs])  14.1 us
    pallas_call x9, Pallas kernels, call(): pl.pallas_call(kernel, out_shape=[jax.ShapeDtypeStruct(shape, dtype) for...  11.1 us
    all_to_all x2, starting transfers between devices, sliced_body(): recv = lax.all_to_all(send, GROUP, 0, 0, tiled=True)  11.1 us
  transfers between devices with their start and end apart: 10, of which 4 were waited for; matrix products, arithmetic and copies ran while one was open for 1% of the time, Pallas kernels for 19%

profile of v6, /device:TPU:0, one launch (start us, length us, event | category | flops | bytes accessed | tf_op | source)
XLA Modules:
  0.0 104.6 jit_solution(2796545982242971295)
XLA Ops:
  0.6 2.1 %spread.1 = f32[16,2,4,8,128]{4,3,2,1,0:T(8,128)} custom-call(f32[8,32,128]{2,1,0:T(8,128)} %refs_0_.5, f32[8,32,128]{2,1,0:T(8,128)} %refs_1_.1, f32[8,32,128]{2,1,0:T(8,128)} %refs_2_.1, s32[8,32,128]{2,1,0:T(8,128)} %refs_3_.2, s32[8,32,128]{2,1,0:T(8,128)} %refs_4_.3), custom_call_target="tpu_custom_call" | custom-call | tf_op jit(solution)/shard_map/spread/pallas_call | solution.py:241
  2.7 7.4 %all-to-all-start.16 = ((f32[16,2,4,8,128]{4,3,2,1,0:T(8,128)}), f32[16,2,4,8,128]{4,3,2,1,0:T(8,128)S(1)}, u32[]{:S(2)}, u32[]{:S(2)}) async-start(f32[16,2,4,8,128]{4,3,2,1,0:T(8,128)} %spread.1), calls=%async_computation.16 | async-start | bytes 1048576 | tf_op jit(solution)/shard_map/all_to_all | solution.py:763
  10.2 0.7 copy-done.5
  11.7 0.7 copy-done.7
  12.4 12.2 %all-to-all-done.16.refs_1_ = f32[16,2,4,8,128]{4,3,2,1,0:T(8,128)S(1)} async-done(((f32[16,2,4,8,128]{4,3,2,1,0:T(8,128)}), f32[16,2,4,8,128]{4,3,2,1,0:T(8,128)S(1)}, u32[]{:S(2)}, u32[]{:S(2)}) %all-to-all-start.16) | async-done | bytes 524320 | tf_op jit(solution)/shard_map/all_to_all | solution.py:763
  25.3 0.7 collective-permute-start.67
  25.9 2.0 %arrange.1 = (f32[3,32,8,128]{3,2,1,0:T(8,128)S(1)}, s32[32,8,128]{2,1,0:T(8,128)S(1)}, s32[32,8,128]{2,1,0:T(8,128)S(1)}, s32[32,8,128]{2,1,0:T(8,128)S(1)}, s32[8,128]{1,0:T(8,128)S(1)}) custom-call(f32[3,32,8,128]{3,2,1,0:T(8,128)S(1)} %get-tuple-element.63.refs_0_, s32[32,8,128]{2,1,0:T(8,128)S(1)} %get-tuple-element.64.refs_1_), custom_call_target="tpu_custom_call" | custom-call | tf_op jit(solution)/shard_map/arrange/pallas_call | solution.py:241
  28.0 8.8 %cells.5.refs_0_ = f32[4,32,8,128]{3,2,1,0:T(8,128)S(1)} custom-call(s32[8,128]{1,0:T(8,128)S(1)} %get-tuple-element.65.refs_0_, f32[3,32,8,128]{3,2,1,0:T(8,128)S(1)} %get-tuple-element.71.refs_1_, s32[32,8,128]{2,1,0:T(8,128)S(1)} %get-tuple-element.67.refs_2_, bf16[256,48]{1,0:T(8,128)(2,1)S(1)} %copy.73.refs_3_.refs_2_, ...), custom_call_target="tpu_custom_call" | custom-call | flops 8053063680 | bytes 393216 | tf_op jit(solution)/shard_map/cells/pallas_call | solution.py:145
  36.8 7.6 %cells.6.refs_1_ = f32[4,32,8,128]{3,2,1,0:T(8,128)S(1)} custom-call(f32[3,32,8,128]{3,2,1,0:T(8,128)S(1)} %get-tuple-element.63.refs_0_, s32[32,8,128]{2,1,0:T(8,128)S(1)} %get-tuple-element.64.refs_1_, bf16[256,48]{1,0:T(8,128)(2,1)S(1)} %copy.73.refs_3_.refs_2_, bf16[4,256,256]{2,1,0:T(8,128)(2,1)S(1)} %copy-done.8, ...), custom_call_target="tpu_custom_call" | custom-call | flops 5368709120 | bytes 262144 | tf_op jit(solution)/shard_map/cells/pallas_call | solution.py:145
  44.5 2.6 %collective-permute-start.68 = (f32[4,8,128]{2,1,0:T(8,128)S(1)}, f32[4,8,128]{2,1,0:T(8,128)S(1)}, u32[]{:S(2)}, u32[]{:S(2)}) collective-permute-start(f32[4,8,128]{2,1,0:T(8,128)S(1)} %bitcast.128), channel_id=1, source_target_pairs={{0,1},{2,3},{11,10},{9,8},{16,17},{18,19},{27,26},{25,24},{28,29},... | collective-permute-start | bytes 49160 | tf_op jit(solution)/shard_map/ppermute | solution.py:748
  47.1 0.8 collective-permute-start.69
  47.9 8.8 %cells.7.refs_2_ = f32[4,32,8,128]{3,2,1,0:T(8,128)S(1)} custom-call(s32[8,128]{1,0:T(8,128)S(1)} %get-tuple-element.65.refs_0_, f32[3,32,8,128]{3,2,1,0:T(8,128)S(1)} %get-tuple-element.71.refs_1_, s32[32,8,128]{2,1,0:T(8,128)S(1)} %get-tuple-element.67.refs_2_, bf16[256,48]{1,0:T(8,128)(2,1)S(1)} %copy.73.refs_3_.refs_2_, ...), custom_call_target="tpu_custom_call" | custom-call | flops 8053063680 | bytes 393216 | tf_op jit(solution)/shard_map/cells/pallas_call | solution.py:145
  56.8 0.9 rhs.1
  57.7 0.7 collective-permute-start.71
  58.4 4.3 %collective-permute-start.70 = (f32[2,256,128]{2,1,0:T(8,128)S(1)}, f32[2,256,128]{2,1,0:T(8,128)S(1)}, u32[]{:S(2)}, u32[]{:S(2)}) collective-permute-start(f32[2,256,128]{2,1,0:T(8,128)S(1)} %rhs.1), channel_id=1, source_target_pairs={{0,1},{2,3},{11,10},{9,8},{16,17},{18,19},{27,26},{25,24},{28,29},... | collective-permute-start | bytes 786440 | tf_op jit(solution)/shard_map/ppermute | solution.py:748
  63.0 0.9 collective-permute-done.70
  63.9 1.7 %basis.2 = (f32[5,256,128]{2,1,0:T(8,128)S(1)}, f32[8,128]{1,0:T(8,128)S(1)}, f32[768,128]{1,0:T(8,128)S(1)}, f32[768,128]{1,0:T(8,128)S(1)}, f32[768,128]{1,0:T...) custom-call(f32[8,128]{1,0:T(8,128)S(1)} %get-tuple-element.62.scale_ref.refs_0_, ...), custom_call_target="tpu_custom_call" | custom-call | tf_op jit(solution)/shard_map/basis/pallas_call | solution.py:241
  65.6 4.3 %collective-permute-start.72 = (f32[256,128]{1,0:T(8,128)S(1)}, f32[256,128]{1,0:T(8,128)S(1)}, u32[]{:S(2)}, u32[]{:S(2)}) collective-permute-start(f32[256,128]{1,0:T(8,128)S(1)} %slice_bitcast_fusion.12.refs_5_), channel_id=1, source_target_pairs={{0,1},{2,3},{11,10},{9,8},{16,17},{18,19},{27,26},{25,24},{28,29},... | collective-permute-start | bytes 393224 | tf_op jit(solution)/shard_map/ppermute | solution.py:748
  70.9 0.9 basis.3
  71.8 16.3 %all_to_all.148 = f32[32,1,128]{2,1,0:T(1,128)S(1)} all-to-all(f32[32,1,128]{2,1,0:T(1,128)S(1)} %bitcast.81), channel_id=1, replica_groups=mesh['blk'=4,'slab'=2,'micro'=4] {'blk','slab','micro'}, dimensions={0} | all-to-all | bytes 32768 | tf_op jit(solution)/shard_map/all_to_all | solution.py:806
  88.2 1.7 %last.1 = (f32[16,2,2,8,128]{4,3,2,1,0:T(8,128)}, f32[8,128]{1,0:T(8,128)S(1)}) custom-call(f32[8,128]{1,0:T(8,128)S(1)} %get-tuple-element.62.scale_ref.refs_0_, f32[32,128]{1,0:T(8,128)S(1)} %bitcast.80, f32[5,256,128]{2,1,0:T(8,128)S(1)} %get-tuple-element.85.refs_8_.refs_2_, f32[4,256,128]{2,1,0:T(8,128)S(1)} %get-tuple-element.88.refs_3_), custom_call_target="tpu_custom_call" | custom-call | tf_op jit(solution)/shard_map/last/pallas_call | solution.py:241
  89.9 3.7 %all-to-all-start.18 = ((f32[16,2,2,8,128]{4,3,2,1,0:T(8,128)}), f32[16,2,2,8,128]{4,3,2,1,0:T(8,128)S(1)}, u32[]{:S(2)}, u32[]{:S(2)}) async-start(f32[16,2,2,8,128]{4,3,2,1,0:T(8,128)} %get-tuple-element.90), calls=%async_computation.18 | async-start | bytes 524288 | tf_op jit(solution)/shard_map/all_to_all | solution.py:811
  94.7 8.8 %all-to-all-done.18.refs_1_ = f32[16,2,2,8,128]{4,3,2,1,0:T(8,128)S(1)} async-done(((f32[16,2,2,8,128]{4,3,2,1,0:T(8,128)}), f32[16,2,2,8,128]{4,3,2,1,0:T(8,128)S(1)}, u32[]{:S(2)}, u32[]{:S(2)}) %all-to-all-start.18) | async-done | bytes 262176 | tf_op jit(solution)/shard_map/all_to_all | solution.py:811
  103.6 1.0 deliver.1
  (53 shorter events, 3.4 us)
Async XLA Ops:
  2.7 21.9 %all-to-all-start.16 = ((f32[16,2,4,8,128]{4,3,2,1,0:T(8,128)}), f32[16,2,4,8,128]{4,3,2,1,0:T(8,128)S(1)}, u32[]{:S(2)}, u32[]{:S(2)}) async-start(f32[16,2,4,8,128]{4,3,2,1,0:T(8,128)} %spread.1), calls=%async_computation.16 | async-start | bytes 1048576 | tf_op jit(solution)/shard_map/all_to_all | solution.py:763
  10.1 0.7 copy-start.5
  10.9 0.7 copy-start.6
  11.7 0.7 copy-start.7
  12.4 15.6 %copy-start.8 = (bf16[4,256,256]{2,1,0:T(8,128)(2,1)S(1)}, bf16[4,256,256]{2,1,0:T(8,128)(2,1)}, u32[]{:S(2)}) copy-start(bf16[4,256,256]{2,1,0:T(8,128)(2,1)} %refs_4_.5) | copy-start | bytes 1572868
  25.2 11.6 %collective-permute-start.66 = (f32[36,8,128]{2,1,0:T(8,128)S(1)}, f32[36,8,128]{2,1,0:T(8,128)S(1)}, u32[]{:S(2)}, u32[]{:S(2)}) collective-permute-start(f32[36,8,128]{2,1,0:T(8,128)S(1)} %get-tuple-element.68), channel_id=1, source_target_pairs={{0,1},{2,3},{11,10},{9,8},{16,17},{18,19},{27,26},{25,24},{28,29},... | collective-permute-start | bytes 442376 | tf_op jit(solution)/shard_map/ppermute | solution.py:748
  25.3 11.6 %collective-permute-start.67 = (f32[36,8,128]{2,1,0:T(8,128)S(1)}, f32[36,8,128]{2,1,0:T(8,128)S(1)}, u32[]{:S(2)}, u32[]{:S(2)}) collective-permute-start(f32[36,8,128]{2,1,0:T(8,128)S(1)} %get-tuple-element.69), channel_id=1, source_target_pairs={{1,2},{3,11},{10,9},{8,16},{17,18},{19,27},{26,25},{24,28},{29,30}... | collective-permute-start | bytes 442376 | tf_op jit(solution)/shard_map/ppermute | solution.py:748
  44.5 12.2 %collective-permute-start.68 = (f32[4,8,128]{2,1,0:T(8,128)S(1)}, f32[4,8,128]{2,1,0:T(8,128)S(1)}, u32[]{:S(2)}, u32[]{:S(2)}) collective-permute-start(f32[4,8,128]{2,1,0:T(8,128)S(1)} %bitcast.128), channel_id=1, source_target_pairs={{0,1},{2,3},{11,10},{9,8},{16,17},{18,19},{27,26},{25,24},{28,29},... | collective-permute-start | bytes 49160 | tf_op jit(solution)/shard_map/ppermute | solution.py:748
  47.1 9.7 %collective-permute-start.69 = (f32[4,8,128]{2,1,0:T(8,128)S(1)}, f32[4,8,128]{2,1,0:T(8,128)S(1)}, u32[]{:S(2)}, u32[]{:S(2)}) collective-permute-start(f32[4,8,128]{2,1,0:T(8,128)S(1)} %bitcast.127), channel_id=1, source_target_pairs={{1,2},{3,11},{10,9},{8,16},{17,18},{19,27},{26,25},{24,28},{29,30}... | collective-permute-start | bytes 49160 | tf_op jit(solution)/shard_map/ppermute | solution.py:748
  57.7 5.2 %collective-permute-start.71 = (f32[2,256,128]{2,1,0:T(8,128)S(1)}, f32[2,256,128]{2,1,0:T(8,128)S(1)}, u32[]{:S(2)}, u32[]{:S(2)}) collective-permute-start(f32[2,256,128]{2,1,0:T(8,128)S(1)} %rhs.1), channel_id=1, source_target_pairs={{1,2},{3,11},{10,9},{8,16},{17,18},{19,27},{26,25},{24,28},{29,30}... | collective-permute-start | bytes 786440 | tf_op jit(solution)/shard_map/ppermute | solution.py:748
  58.4 5.5 %collective-permute-start.70 = (f32[2,256,128]{2,1,0:T(8,128)S(1)}, f32[2,256,128]{2,1,0:T(8,128)S(1)}, u32[]{:S(2)}, u32[]{:S(2)}) collective-permute-start(f32[2,256,128]{2,1,0:T(8,128)S(1)} %rhs.1), channel_id=1, source_target_pairs={{0,1},{2,3},{11,10},{9,8},{16,17},{18,19},{27,26},{25,24},{28,29},... | collective-permute-start | bytes 786440 | tf_op jit(solution)/shard_map/ppermute | solution.py:748
  65.6 5.3 %collective-permute-start.72 = (f32[256,128]{1,0:T(8,128)S(1)}, f32[256,128]{1,0:T(8,128)S(1)}, u32[]{:S(2)}, u32[]{:S(2)}) collective-permute-start(f32[256,128]{1,0:T(8,128)S(1)} %slice_bitcast_fusion.12.refs_5_), channel_id=1, source_target_pairs={{0,1},{2,3},{11,10},{9,8},{16,17},{18,19},{27,26},{25,24},{28,29},... | collective-permute-start | bytes 393224 | tf_op jit(solution)/shard_map/ppermute | solution.py:748
  69.9 1.0 collective-permute-start.73
  88.2 15.4 %copy-start.4 = (s32[8,32,128]{2,1,0:T(8,128)S(1)}, s32[8,32,128]{2,1,0:T(8,128)}, u32[]{:S(2)}) copy-start(s32[8,32,128]{2,1,0:T(8,128)} %refs_4_.3) | copy-start | bytes 393220
  89.9 13.7 %copy-start = (f32[8,32,128]{2,1,0:T(8,128)S(1)}, f32[8,32,128]{2,1,0:T(8,128)}, u32[]{:S(2)}) copy-start(f32[8,32,128]{2,1,0:T(8,128)} %refs_2_.1) | copy-start | bytes 393220
  89.9 13.7 %copy-start.1 = (f32[8,32,128]{2,1,0:T(8,128)S(1)}, f32[8,32,128]{2,1,0:T(8,128)}, u32[]{:S(2)}) copy-start(f32[8,32,128]{2,1,0:T(8,128)} %refs_0_.5) | copy-start | bytes 393220
  89.9 13.7 %copy-start.2 = (f32[8,32,128]{2,1,0:T(8,128)S(1)}, f32[8,32,128]{2,1,0:T(8,128)}, u32[]{:S(2)}) copy-start(f32[8,32,128]{2,1,0:T(8,128)} %refs_1_.1) | copy-start | bytes 393220
  89.9 13.7 %copy-start.3 = (s32[8,32,128]{2,1,0:T(8,128)S(1)}, s32[8,32,128]{2,1,0:T(8,128)}, u32[]{:S(2)}) copy-start(s32[8,32,128]{2,1,0:T(8,128)} %refs_3_.2) | copy-start | bytes 393220
  89.9 13.7 %all-to-all-start.18 = ((f32[16,2,2,8,128]{4,3,2,1,0:T(8,128)}), f32[16,2,2,8,128]{4,3,2,1,0:T(8,128)S(1)}, u32[]{:S(2)}, u32[]{:S(2)}) async-start(f32[16,2,2,8,128]{4,3,2,1,0:T(8,128)} %get-tuple-element.90), calls=%async_computation.18 | async-start | bytes 524288 | tf_op jit(solution)/shard_map/all_to_all | solution.py:811

commit v7 on v6

--- a/solution.py
+++ b/solution.py
@@ -24,21 +24,11 @@
     weight_in = jnp.concatenate([high, low], axis=1)
     none = jnp.zeros((families, 1, modes), BF)
     stress = jnp.concatenate([family_out, none], axis=1).reshape(4 * families, modes)
-    none = jnp.zeros((families, 3, modes), BF)
-    tan_high, tan_low = split(family_tan)
-    tan_high = jnp.concatenate([none, tan_high[:, None]], axis=1).reshape(4 * families, modes)
-    tan_low = jnp.concatenate([none, tan_low[:, None]], axis=1).reshape(4 * families, modes)
-    weight_out = jnp.concatenate(
-        [
-            jnp.concatenate([stress, tan_high], axis=1),
-            jnp.concatenate([jnp.zeros_like(stress), tan_low], axis=1),
-        ],
-        axis=0,
-    )
-    return weight_in, family_mid, weight_out
-
-
-def cells_kernel(families, planes, strain_ref, code_ref, in_ref, mid_ref, out_ref, *refs, info_ref=None):
+    weight_tan = jnp.broadcast_to(family_tan[:, :, None], (families, modes, 128))
+    return weight_in, family_mid, stress, weight_tan
+
+
+def cells_kernel(families, planes, strain_ref, code_ref, in_ref, mid_ref, out_ref, tan_ref, *refs, info_ref=None):
     *edges, answer_ref = refs
     modes = in_ref.shape[0]
     step = code_ref.shape[0]
@@ -95,16 +85,26 @@
                 parts.append(jnp.dot(mixing, stacked, preferred_element_type=F32))
             hidden = jnp.concatenate(parts, axis=1)
         bounded = jnp.tanh(hidden).astype(BF)
-        both = jnp.concatenate([bounded, bounded * bounded], axis=0)
-        result = jnp.dot(out_ref[...], both, preferred_element_type=F32)
-        result = result[: 4 * families] + result[4 * families :]
+        result = jnp.dot(out_ref[...], bounded, preferred_element_type=F32)
         owner = lax.shift_right_logical(lax.broadcasted_iota(jnp.int32, (4 * families, width), 0), 2)
         result = jnp.where(owner == family, result, 0.0)
         total = result[:4]
         for f in range(1, families):
             total = total + result[4 * f : 4 * f + 4]
         for i, (a, x) in enumerate(spots):
-            answer_ref[:, a, x, :] = total[:, i * 128 : (i + 1) * 128]
+            part = slice(i * 128, (i + 1) * 128)
+            answer_ref[0:3, a, x, :] = total[0:3, part]
+            square = bounded[:, part].astype(F32)
+            square = square * square
+            owner = jnp.broadcast_to(family_row[i], (modes, 128))
+            if pairs is None:
+                weight = tan_ref[0]
+                for f in range(1, families):
+                    weight = jnp.where(owner == f, tan_ref[f], weight)
+            else:
+                one, other = pairs[i // 2]
+                weight = jnp.where(owner == one, tan_ref[one], tan_ref[other])
+            answer_ref[3, a, pl.ds(x, 1), :] = jnp.sum(weight * square, axis=0, keepdims=True)
 
     if info_ref is None:
         evaluate(None)
@@ -126,7 +126,7 @@
 
 
 def cells(strain, code, packed, families, step, planes, *edges, info=None):
-    weight_in, weight_mid, weight_out = packed
+    weight_in, weight_mid, weight_out, weight_tan = packed
     count = code.shape[0]
     planes = tuple(planes)
     points = count * len(planes) * 128
@@ -153,6 +153,7 @@
                 whole(weight_in),
                 whole(weight_mid),
                 whole(weight_out),
+                whole(weight_tan),
             ]
             + [pl.BlockSpec((1, 128), lambda i, *_: (0, 0)) for _ in edges[:1]]
             + [pl.BlockSpec((1, 8, 128), lambda i, *_: (count + i, 0, 0)) for _ in edges[1:]],
@@ -164,7 +165,7 @@
             flops=2 * points * modes * modes * (families + 1), bytes_accessed=points * 32, transcendentals=2 * points * modes
         ),
         name="cells",
-    )(*scalars, strain, code, weight_in, weight_mid, weight_out, *edges)
+    )(*scalars, strain, code, weight_in, weight_mid, weight_out, weight_tan, *edges)
 
 
 def global_sum(value):
@@ -547,7 +548,7 @@
         own_ref, sums_ref, vectors = refs
     else:
         operator_refs, (seed_ref, seed_chip_ref, seed_far_ref), refs = refs[:10], refs[10:13], refs[13:]
-        own_ref, sums_ref, tan, main, after, out, back, vectors = refs
+        own_ref, tan, main, after, out, back, vectors = refs
         operator_kernel(peers, *operator_refs, tan, main, after, out, back)
     is_first, is_last, _ = whereabouts(peers)
 
@@ -584,28 +585,38 @@
                     value = value + value - vectors[degree - 2, tile(plane, quarter), :]
                 vectors[degree, tile(plane, quarter), :] = value
     own_tiles = [(tile(plane, quarter), tile(plane + 8, quarter)) for plane in range(8) for quarter in range(4)]
-    pairs = []
-    if last:
-        for degree in range(1, HALF + 1):
-            for rows, wide_rows in own_tiles:
-                value = vectors[degree, wide_rows, :]
-                own_ref[degree - 1, rows, :] = value + value - earlier_ref[HALF - degree, rows, :]
-            before = earlier_ref.at[HALF] if degree == 1 else own_ref.at[degree - 2]
-            pairs += [(before, own_ref.at[degree - 1]), (own_ref.at[degree - 1], own_ref.at[degree - 1])]
-    else:
+    if not last:
         for degree in range(HALF + 1):
             for rows, wide_rows in own_tiles:
                 own_ref[degree, rows, :] = vectors[degree, wide_rows, :]
-            if degree:
-                pairs.append((own_ref.at[degree - 1], own_ref.at[degree]))
-            pairs.append((own_ref.at[degree], own_ref.at[degree]))
+        return
+    pairs = []
+    for degree in range(1, HALF + 1):
+        for rows, wide_rows in own_tiles:
+            value = vectors[degree, wide_rows, :]
+            own_ref[degree - 1, rows, :] = value + value - earlier_ref[HALF - degree, rows, :]
+        before = earlier_ref.at[HALF] if degree == 1 else own_ref.at[degree - 2]
+        pairs += [(before, own_ref.at[degree - 1]), (own_ref.at[degree - 1], own_ref.at[degree - 1])]
+    sums = inner_products(pairs, 2 * HALF + 1, previous_ref[0:1, :])
+    sums_ref[...] = jnp.broadcast_to(sums, sums_ref.shape)
+
+
+def inner_products(pairs, first, sums):
     column = lax.broadcasted_iota(jnp.int32, (1, 128), 1)
-    sums = previous_ref[0:1, :] if last else jnp.zeros((1, 128), F32)
     for number, (left, right) in enumerate(pairs):
-        total = tree([left[rows, :] * right[rows, :] for rows, _ in own_tiles])
+        total = tree([left[start : start + 8, :] * right[start : start + 8, :] for start in range(0, left.shape[0], 8)])
         entry = jnp.sum(jnp.sum(total, axis=0, keepdims=True), axis=1, keepdims=True)
-        place_of = number + (2 * HALF + 1 if last else 0)
-        sums = jnp.where(column == place_of, jnp.broadcast_to(entry, (1, 128)), sums)
+        sums = jnp.where(column == first + number, jnp.broadcast_to(entry, (1, 128)), sums)
+    return sums
+
+
+def products_kernel(early_ref, sums_ref):
+    pairs = []
+    for degree in range(HALF + 1):
+        if degree:
+            pairs.append((early_ref.at[degree - 1], early_ref.at[degree]))
+        pairs.append((early_ref.at[degree], early_ref.at[degree]))
+    sums = inner_products(pairs, 0, jnp.zeros((1, 128), F32))
     sums_ref[...] = jnp.broadcast_to(sums, sums_ref.shape)
 
 
@@ -793,12 +804,13 @@
     inside = call(
         own_kernel, [(rows, F32)] * 4, [], "own", scale, own[1], found,
     )
-    early, sums, *operator = call(
+    early, *operator = call(
         lambda *refs: basis_kernel(peers, False, *refs),
-        [((HALF + 1,) + rows, F32), ((8, 128), F32)] + [(tall, F32)] * 5, vectors, "basis",
+        [((HALF + 1,) + rows, F32)] + [(tall, F32)] * 5, vectors, "basis",
         scale, own[1], own_chip[1], own_far[1], *inside, chip[:around].reshape(rows), far[:around].reshape(rows),
         own[0], own_chip[0], own_far[0],
     )
+    (sums,) = call(products_kernel, [((8, 128), F32)], [], "products", early)
     late, sums = call(
         lambda *refs: basis_kernel(peers, True, *refs), [((HALF,) + rows, F32), ((everyone, 128), F32)], vectors, "basis",
         *operator, early[HALF], *neighbours(early[HALF], early[HALF]), early, sums,

time: 105 us -> 105 us (level)
    pallas_call x9 -> x10, Pallas kernels: 11.1 us -> 11 us  [call(): pl.pallas_call(kernel, out_shape=[jax.ShapeDtypeStruct(shape, dtype) for...]
where the time goes in v7:
time: 105 us
  Pallas kernels  36.2 us (34%)
  starting transfers between devices  25.1 us (24%)
  waiting for transfers between devices  22.9 us (22%)
  blocking collectives  16.3 us (16%)
  local copies, waits for them, and re-layouts  2.24 us (2%)
  between operations  1.62 us (2%)
    pallas_call x3, Pallas kernels, cells(): pl.pallas_call(kernel, grid_spec=pltpu.PrefetchScalarGridSpec(num_scalar_...  25.2 us
    all_to_all x2, waiting for transfers between devices, sliced_body(): recv = lax.all_to_all(send, GROUP, 0, 0, tiled=True)  21.8 us
    all_to_all x1, blocking collectives, sliced_body(): sums = lax.all_to_all(sums, AXES, 0, 0, tiled=True)  16.3 us
    ppermute x8, starting transfers between devices, swap(): return lax.ppermute(value, AXES, pairs + [(b, a) for a, b in pairs])  14.1 us
    all_to_all x2, starting transfers between devices, sliced_body(): recv = lax.all_to_all(send, GROUP, 0, 0, tiled=True)  11.1 us
    pallas_call x10, Pallas kernels, call(): pl.pallas_call(kernel, out_shape=[jax.ShapeDtypeStruct(shape, dtype) for...  11 us
  transfers between devices with their start and end apart: 10, of which 4 were waited for; matrix products, arithmetic and copies ran while one was open for 1% of the time, Pallas kernels for 19%

profile of v7, /device:TPU:0, one launch (start us, length us, event | category | flops | bytes accessed | tf_op | source)
XLA Modules:
  0.0 104.5 jit_solution(14183179024004687903)
XLA Ops:
  0.6 2.1 %spread.1 = f32[16,2,4,8,128]{4,3,2,1,0:T(8,128)} custom-call(f32[8,32,128]{2,1,0:T(8,128)} %refs_0_.5, f32[8,32,128]{2,1,0:T(8,128)} %refs_1_.1, f32[8,32,128]{2,1,0:T(8,128)} %refs_2_.1, s32[8,32,128]{2,1,0:T(8,128)} %refs_3_.2, s32[8,32,128]{2,1,0:T(8,128)} %refs_4_.3), custom_call_target="tpu_custom_call" | custom-call | tf_op jit(solution)/shard_map/spread/pallas_call | solution.py:242
  2.7 7.4 %all-to-all-start.16 = ((f32[16,2,4,8,128]{4,3,2,1,0:T(8,128)}), f32[16,2,4,8,128]{4,3,2,1,0:T(8,128)S(1)}, u32[]{:S(2)}, u32[]{:S(2)}) async-start(f32[16,2,4,8,128]{4,3,2,1,0:T(8,128)} %spread.1), calls=%async_computation.16 | async-start | bytes 1048576 | tf_op jit(solution)/shard_map/all_to_all | solution.py:774
  10.2 0.7 copy-done.5
  11.6 13.0 %all-to-all-done.16.refs_1_ = f32[16,2,4,8,128]{4,3,2,1,0:T(8,128)S(1)} async-done(((f32[16,2,4,8,128]{4,3,2,1,0:T(8,128)}), f32[16,2,4,8,128]{4,3,2,1,0:T(8,128)S(1)}, u32[]{:S(2)}, u32[]{:S(2)}) %all-to-all-start.16) | async-done | bytes 524320 | tf_op jit(solution)/shard_map/all_to_all | solution.py:774
  25.3 0.7 collective-permute-start.67
  26.0 2.0 %arrange.1 = (f32[3,32,8,128]{3,2,1,0:T(8,128)S(1)}, s32[32,8,128]{2,1,0:T(8,128)S(1)}, s32[32,8,128]{2,1,0:T(8,128)S(1)}, s32[32,8,128]{2,1,0:T(8,128)S(1)}, s32[8,128]{1,0:T(8,128)S(1)}) custom-call(f32[3,32,8,128]{3,2,1,0:T(8,128)S(1)} %get-tuple-element.62.refs_0_, s32[32,8,128]{2,1,0:T(8,128)S(1)} %get-tuple-element.63.refs_1_), custom_call_target="tpu_custom_call" | custom-call | tf_op jit(solution)/shard_map/arrange/pallas_call | solution.py:242
  28.2 8.7 %cells.5.refs_0_ = f32[4,32,8,128]{3,2,1,0:T(8,128)S(1)} custom-call(s32[8,128]{1,0:T(8,128)S(1)} %get-tuple-element.64.refs_0_, f32[3,32,8,128]{3,2,1,0:T(8,128)S(1)} %get-tuple-element.70.refs_1_, s32[32,8,128]{2,1,0:T(8,128)S(1)} %get-tuple-element.66.refs_2_, bf16[256,48]{1,0:T(8,128)(2,1)S(1)} %copy.53.refs_3_.refs_2_, ...), custom_call_target="tpu_custom_call" | custom-call | flops 8053063680 | bytes 393216 | tf_op jit(solution)/shard_map/cells/pallas_call | solution.py:145
  36.9 7.9 %cells.6.refs_1_ = f32[4,32,8,128]{3,2,1,0:T(8,128)S(1)} custom-call(f32[3,32,8,128]{3,2,1,0:T(8,128)S(1)} %get-tuple-element.62.refs_0_, s32[32,8,128]{2,1,0:T(8,128)S(1)} %get-tuple-element.63.refs_1_, bf16[256,48]{1,0:T(8,128)(2,1)S(1)} %copy.53.refs_3_.refs_2_, bf16[4,256,256]{2,1,0:T(8,128)(2,1)S(1)} %copy-done.8, ...), custom_call_target="tpu_custom_call" | custom-call | flops 5368709120 | bytes 262144 | tf_op jit(solution)/shard_map/cells/pallas_call | solution.py:145
  44.8 2.6 %collective-permute-start.68 = (f32[4,8,128]{2,1,0:T(8,128)S(1)}, f32[4,8,128]{2,1,0:T(8,128)S(1)}, u32[]{:S(2)}, u32[]{:S(2)}) collective-permute-start(f32[4,8,128]{2,1,0:T(8,128)S(1)} %bitcast.120), channel_id=1, source_target_pairs={{0,1},{2,3},{11,10},{9,8},{16,17},{18,19},{27,26},{25,24},{28,29},... | collective-permute-start | bytes 49160 | tf_op jit(solution)/shard_map/ppermute | solution.py:759
  47.4 0.8 collective-permute-start.69
  48.2 8.7 %cells.7.refs_2_ = f32[4,32,8,128]{3,2,1,0:T(8,128)S(1)} custom-call(s32[8,128]{1,0:T(8,128)S(1)} %get-tuple-element.64.refs_0_, f32[3,32,8,128]{3,2,1,0:T(8,128)S(1)} %get-tuple-element.70.refs_1_, s32[32,8,128]{2,1,0:T(8,128)S(1)} %get-tuple-element.66.refs_2_, bf16[256,48]{1,0:T(8,128)(2,1)S(1)} %copy.53.refs_3_.refs_2_, ...), custom_call_target="tpu_custom_call" | custom-call | flops 8053063680 | bytes 393216 | tf_op jit(solution)/shard_map/cells/pallas_call | solution.py:145
  57.0 0.9 rhs.1
  57.9 0.7 collective-permute-start.71
  58.6 4.3 %collective-permute-start.70 = (f32[2,256,128]{2,1,0:T(8,128)S(1)}, f32[2,256,128]{2,1,0:T(8,128)S(1)}, u32[]{:S(2)}, u32[]{:S(2)}) collective-permute-start(f32[2,256,128]{2,1,0:T(8,128)S(1)} %rhs.1), channel_id=1, source_target_pairs={{0,1},{2,3},{11,10},{9,8},{16,17},{18,19},{27,26},{25,24},{28,29},... | collective-permute-start | bytes 786440 | tf_op jit(solution)/shard_map/ppermute | solution.py:759
  63.2 0.9 collective-permute-done.70
  64.1 1.5 %basis.2 = (f32[5,256,128]{2,1,0:T(8,128)S(1)}, f32[768,128]{1,0:T(8,128)S(1)}, f32[768,128]{1,0:T(8,128)S(1)}, f32[768,128]{1,0:T(8,128)S(1)}, f32[768,128]{1,0:T(8,128)S(1)}, /*index=5*/f32[768,128]{1,0:T(8,128)S(1)}) custom-call(f32[8,128]{1,0:T(8,128)S(1)} %get-tuple-element.61.scale_ref.refs_0_, f32[256,128]{1,0:T(8,128)S(1)} %get-tuple-element.253.tan_ref.refs_1_, ...), custom_call_target="tpu_custom_call" | custom-call | tf_op jit(solution)/shard_map/basis/pallas_call | solution.py:242
  65.6 4.3 %collective-permute-start.72 = (f32[256,128]{1,0:T(8,128)S(1)}, f32[256,128]{1,0:T(8,128)S(1)}, u32[]{:S(2)}, u32[]{:S(2)}) collective-permute-start(f32[256,128]{1,0:T(8,128)S(1)} %slice_bitcast_fusion.12.refs_5_), channel_id=1, source_target_pairs={{0,1},{2,3},{11,10},{9,8},{16,17},{18,19},{27,26},{25,24},{28,29},... | collective-permute-start | bytes 393224 | tf_op jit(solution)/shard_map/ppermute | solution.py:759
  69.9 0.7 collective-permute-start.73
  70.9 0.9 basis.3
  71.8 16.3 %all_to_all.148 = f32[32,1,128]{2,1,0:T(1,128)S(1)} all-to-all(f32[32,1,128]{2,1,0:T(1,128)S(1)} %bitcast.73), channel_id=1, replica_groups=mesh['blk'=4,'slab'=2,'micro'=4] {'blk','slab','micro'}, dimensions={0} | all-to-all | bytes 32768 | tf_op jit(solution)/shard_map/all_to_all | solution.py:818
  88.1 1.7 %last.1 = (f32[16,2,2,8,128]{4,3,2,1,0:T(8,128)}, f32[8,128]{1,0:T(8,128)S(1)}) custom-call(f32[8,128]{1,0:T(8,128)S(1)} %get-tuple-element.61.scale_ref.refs_0_, f32[32,128]{1,0:T(8,128)S(1)} %bitcast.72, f32[5,256,128]{2,1,0:T(8,128)S(1)} %get-tuple-element.84.early_ref.refs_8_.refs_2_, f32[4,256,128]{2,1,0:T(8,128)S(1)} %get-tuple-element.86.refs_3_), custom_call_target="tpu_custom_call" | custom-call | tf_op jit(solution)/shard_map/last/pallas_call | solution.py:242
  89.8 3.7 %all-to-all-start.18 = ((f32[16,2,2,8,128]{4,3,2,1,0:T(8,128)}), f32[16,2,2,8,128]{4,3,2,1,0:T(8,128)S(1)}, u32[]{:S(2)}, u32[]{:S(2)}) async-start(f32[16,2,2,8,128]{4,3,2,1,0:T(8,128)} %get-tuple-element.88), calls=%async_computation.18 | async-start | bytes 524288 | tf_op jit(solution)/shard_map/all_to_all | solution.py:823
  94.6 8.8 %all-to-all-done.18.refs_1_ = f32[16,2,2,8,128]{4,3,2,1,0:T(8,128)S(1)} async-done(((f32[16,2,2,8,128]{4,3,2,1,0:T(8,128)}), f32[16,2,2,8,128]{4,3,2,1,0:T(8,128)S(1)}, u32[]{:S(2)}, u32[]{:S(2)}) %all-to-all-start.18) | async-done | bytes 262176 | tf_op jit(solution)/shard_map/all_to_all | solution.py:823
  103.6 1.0 deliver.1
  (47 shorter events, 2.8 us)
Async XLA Ops:
  2.7 21.9 %all-to-all-start.16 = ((f32[16,2,4,8,128]{4,3,2,1,0:T(8,128)}), f32[16,2,4,8,128]{4,3,2,1,0:T(8,128)S(1)}, u32[]{:S(2)}, u32[]{:S(2)}) async-start(f32[16,2,4,8,128]{4,3,2,1,0:T(8,128)} %spread.1), calls=%async_computation.16 | async-start | bytes 1048576 | tf_op jit(solution)/shard_map/all_to_all | solution.py:774
  10.2 0.7 copy-start.5
  10.9 0.7 copy-start.7
  11.6 13.0 %copy-start.6 = (f32[4,256]{1,0:T(4,128)S(1)}, f32[4,256]{1,0:T(4,128)}, u32[]{:S(2)}) copy-start(f32[4,256]{1,0:T(4,128)} %refs_0_.4) | copy-start | bytes 12292
  25.2 11.7 %collective-permute-start.66 = (f32[36,8,128]{2,1,0:T(8,128)S(1)}, f32[36,8,128]{2,1,0:T(8,128)S(1)}, u32[]{:S(2)}, u32[]{:S(2)}) collective-permute-start(f32[36,8,128]{2,1,0:T(8,128)S(1)} %get-tuple-element.67), channel_id=1, source_target_pairs={{0,1},{2,3},{11,10},{9,8},{16,17},{18,19},{27,26},{25,24},{28,29},... | collective-permute-start | bytes 442376 | tf_op jit(solution)/shard_map/ppermute | solution.py:759
  25.3 11.6 %collective-permute-start.67 = (f32[36,8,128]{2,1,0:T(8,128)S(1)}, f32[36,8,128]{2,1,0:T(8,128)S(1)}, u32[]{:S(2)}, u32[]{:S(2)}) collective-permute-start(f32[36,8,128]{2,1,0:T(8,128)S(1)} %get-tuple-element.68), channel_id=1, source_target_pairs={{1,2},{3,11},{10,9},{8,16},{17,18},{19,27},{26,25},{24,28},{29,30}... | collective-permute-start | bytes 442376 | tf_op jit(solution)/shard_map/ppermute | solution.py:759
  25.9 2.2 %copy-start.8 = (bf16[4,256,256]{2,1,0:T(8,128)(2,1)S(1)}, bf16[4,256,256]{2,1,0:T(8,128)(2,1)}, u32[]{:S(2)}) copy-start(bf16[4,256,256]{2,1,0:T(8,128)(2,1)} %refs_4_.5) | copy-start | bytes 1572868
  44.8 12.1 %collective-permute-start.68 = (f32[4,8,128]{2,1,0:T(8,128)S(1)}, f32[4,8,128]{2,1,0:T(8,128)S(1)}, u32[]{:S(2)}, u32[]{:S(2)}) collective-permute-start(f32[4,8,128]{2,1,0:T(8,128)S(1)} %bitcast.120), channel_id=1, source_target_pairs={{0,1},{2,3},{11,10},{9,8},{16,17},{18,19},{27,26},{25,24},{28,29},... | collective-permute-start | bytes 49160 | tf_op jit(solution)/shard_map/ppermute | solution.py:759
  47.4 9.5 %collective-permute-start.69 = (f32[4,8,128]{2,1,0:T(8,128)S(1)}, f32[4,8,128]{2,1,0:T(8,128)S(1)}, u32[]{:S(2)}, u32[]{:S(2)}) collective-permute-start(f32[4,8,128]{2,1,0:T(8,128)S(1)} %bitcast.119), channel_id=1, source_target_pairs={{1,2},{3,11},{10,9},{8,16},{17,18},{19,27},{26,25},{24,28},{29,30}... | collective-permute-start | bytes 49160 | tf_op jit(solution)/shard_map/ppermute | solution.py:759
  57.9 5.2 %collective-permute-start.71 = (f32[2,256,128]{2,1,0:T(8,128)S(1)}, f32[2,256,128]{2,1,0:T(8,128)S(1)}, u32[]{:S(2)}, u32[]{:S(2)}) collective-permute-start(f32[2,256,128]{2,1,0:T(8,128)S(1)} %rhs.1), channel_id=1, source_target_pairs={{1,2},{3,11},{10,9},{8,16},{17,18},{19,27},{26,25},{24,28},{29,30}... | collective-permute-start | bytes 786440 | tf_op jit(solution)/shard_map/ppermute | solution.py:759
  58.6 5.5 %collective-permute-start.70 = (f32[2,256,128]{2,1,0:T(8,128)S(1)}, f32[2,256,128]{2,1,0:T(8,128)S(1)}, u32[]{:S(2)}, u32[]{:S(2)}) collective-permute-start(f32[2,256,128]{2,1,0:T(8,128)S(1)} %rhs.1), channel_id=1, source_target_pairs={{0,1},{2,3},{11,10},{9,8},{16,17},{18,19},{27,26},{25,24},{28,29},... | collective-permute-start | bytes 786440 | tf_op jit(solution)/shard_map/ppermute | solution.py:759
  65.6 5.3 %collective-permute-start.72 = (f32[256,128]{1,0:T(8,128)S(1)}, f32[256,128]{1,0:T(8,128)S(1)}, u32[]{:S(2)}, u32[]{:S(2)}) collective-permute-start(f32[256,128]{1,0:T(8,128)S(1)} %slice_bitcast_fusion.12.refs_5_), channel_id=1, source_target_pairs={{0,1},{2,3},{11,10},{9,8},{16,17},{18,19},{27,26},{25,24},{28,29},... | collective-permute-start | bytes 393224 | tf_op jit(solution)/shard_map/ppermute | solution.py:759
  69.9 1.0 collective-permute-start.73
  88.1 15.4 %copy-start.4 = (s32[8,32,128]{2,1,0:T(8,128)S(1)}, s32[8,32,128]{2,1,0:T(8,128)}, u32[]{:S(2)}) copy-start(s32[8,32,128]{2,1,0:T(8,128)} %refs_4_.3) | copy-start | bytes 393220
  89.8 13.7 %copy-start = (f32[8,32,128]{2,1,0:T(8,128)S(1)}, f32[8,32,128]{2,1,0:T(8,128)}, u32[]{:S(2)}) copy-start(f32[8,32,128]{2,1,0:T(8,128)} %refs_2_.1) | copy-start | bytes 393220
  89.8 13.7 %copy-start.1 = (f32[8,32,128]{2,1,0:T(8,128)S(1)}, f32[8,32,128]{2,1,0:T(8,128)}, u32[]{:S(2)}) copy-start(f32[8,32,128]{2,1,0:T(8,128)} %refs_0_.5) | copy-start | bytes 393220
  89.8 13.7 %copy-start.2 = (f32[8,32,128]{2,1,0:T(8,128)S(1)}, f32[8,32,128]{2,1,0:T(8,128)}, u32[]{:S(2)}) copy-start(f32[8,32,128]{2,1,0:T(8,128)} %refs_1_.1) | copy-start | bytes 393220
  89.8 13.7 %copy-start.3 = (s32[8,32,128]{2,1,0:T(8,128)S(1)}, s32[8,32,128]{2,1,0:T(8,128)}, u32[]{:S(2)}) copy-start(s32[8,32,128]{2,1,0:T(8,128)} %refs_3_.2) | copy-start | bytes 393220
  89.8 13.7 %all-to-all-start.18 = ((f32[16,2,2,8,128]{4,3,2,1,0:T(8,128)}), f32[16,2,2,8,128]{4,3,2,1,0:T(8,128)S(1)}, u32[]{:S(2)}, u32[]{:S(2)}) async-start(f32[16,2,2,8,128]{4,3,2,1,0:T(8,128)} %get-tuple-element.88), calls=%async_computation.18 | async-start | bytes 524288 | tf_op jit(solution)/shard_map/all_to_all | solution.py:823

commit v8 on v7

--- a/solution.py
+++ b/solution.py
@@ -544,7 +544,7 @@
 
 def basis_kernel(peers, last, *refs):
     if last:
-        tan, main, after, out, back, seed_ref, seed_chip_ref, seed_far_ref, earlier_ref, previous_ref, *refs = refs
+        seed_far_ref, tan, main, after, out, back, earlier_ref, previous_ref, seed_ref, seed_chip_ref, *refs = refs
         own_ref, sums_ref, vectors = refs
     else:
         operator_refs, (seed_ref, seed_chip_ref, seed_far_ref), refs = refs[:10], refs[10:13], refs[13:]
@@ -810,10 +810,11 @@
         scale, own[1], own_chip[1], own_far[1], *inside, chip[:around].reshape(rows), far[:around].reshape(rows),
         own[0], own_chip[0], own_far[0],
     )
+    seed_chip, seed_far = neighbours(early[HALF], early[HALF])
     (sums,) = call(products_kernel, [((8, 128), F32)], [], "products", early)
     late, sums = call(
         lambda *refs: basis_kernel(peers, True, *refs), [((HALF,) + rows, F32), ((everyone, 128), F32)], vectors, "basis",
-        *operator, early[HALF], *neighbours(early[HALF], early[HALF]), early, sums,
+        seed_far, *operator, early, sums, early[HALF], seed_chip,
     )
     sums = lax.all_to_all(sums, AXES, 0, 0, tiled=True)
     send, worst = call(

time: 105 us -> 105 us (level)
  blocking collectives: 16.3 us -> 14 us
  starting transfers between devices: 25.1 us -> 26.7 us
    all_to_all x1, blocking collectives: 16.3 us -> 14 us  [sliced_body(): sums = lax.all_to_all(sums, AXES, 0, 0, tiled=True)]
    ppermute x8, starting transfers between devices: 14.1 us -> 15.7 us  [swap(): return lax.ppermute(value, AXES, pairs + [(b, a) for a, b in pairs])]
where the time goes in v8:
time: 105 us; the launch traced here: 104 us
  Pallas kernels  36.2 us (34%)
  starting transfers between devices  26.7 us (25%)
  waiting for transfers between devices  23.5 us (22%)
  blocking collectives  14 us (13%)
  local copies, waits for them, and re-layouts  2.24 us (2%)
  between operations  1.62 us (2%)
    pallas_call x3, Pallas kernels, cells(): pl.pallas_call(kernel, grid_spec=pltpu.PrefetchScalarGridSpec(num_scalar_...  25.2 us
    all_to_all x2, waiting for transfers between devices, sliced_body(): recv = lax.all_to_all(send, GROUP, 0, 0, tiled=True)  21.8 us
    ppermute x8, starting transfers between devices, swap(): return lax.ppermute(value, AXES, pairs + [(b, a) for a, b in pairs])  15.7 us
    all_to_all x1, blocking collectives, sliced_body(): sums = lax.all_to_all(sums, AXES, 0, 0, tiled=True)  14 us
    all_to_all x2, starting transfers between devices, sliced_body(): recv = lax.all_to_all(send, GROUP, 0, 0, tiled=True)  11.1 us
    pallas_call x10, Pallas kernels, call(): pl.pallas_call(kernel, out_shape=[jax.ShapeDtypeStruct(shape, dtype) for...  11 us
  transfers between devices with their start and end apart: 10, of which 4 were waited for; matrix products, arithmetic and copies ran while one was open for 1% of the time, Pallas kernels for 19%

profile of v8, /device:TPU:0, one launch (start us, length us, event | category | flops | bytes accessed | tf_op | source)
XLA Modules:
  0.0 104.5 jit_solution(10120834059631223647)
XLA Ops:
  0.6 2.1 %spread.1 = f32[16,2,4,8,128]{4,3,2,1,0:T(8,128)} custom-call(f32[8,32,128]{2,1,0:T(8,128)} %refs_0_.5, f32[8,32,128]{2,1,0:T(8,128)} %refs_1_.1, f32[8,32,128]{2,1,0:T(8,128)} %refs_2_.1, s32[8,32,128]{2,1,0:T(8,128)} %refs_3_.2, s32[8,32,128]{2,1,0:T(8,128)} %refs_4_.3), custom_call_target="tpu_custom_call" | custom-call | tf_op jit(solution)/shard_map/spread/pallas_call | solution.py:242
  2.7 7.4 %all-to-all-start.16 = ((f32[16,2,4,8,128]{4,3,2,1,0:T(8,128)}), f32[16,2,4,8,128]{4,3,2,1,0:T(8,128)S(1)}, u32[]{:S(2)}, u32[]{:S(2)}) async-start(f32[16,2,4,8,128]{4,3,2,1,0:T(8,128)} %spread.1), calls=%async_computation.16 | async-start | bytes 1048576 | tf_op jit(solution)/shard_map/all_to_all | solution.py:774
  10.2 0.7 copy-done.5
  11.6 13.0 %all-to-all-done.16.refs_1_ = f32[16,2,4,8,128]{4,3,2,1,0:T(8,128)S(1)} async-done(((f32[16,2,4,8,128]{4,3,2,1,0:T(8,128)}), f32[16,2,4,8,128]{4,3,2,1,0:T(8,128)S(1)}, u32[]{:S(2)}, u32[]{:S(2)}) %all-to-all-start.16) | async-done | bytes 524320 | tf_op jit(solution)/shard_map/all_to_all | solution.py:774
  26.0 2.0 %arrange.1 = (f32[3,32,8,128]{3,2,1,0:T(8,128)S(1)}, s32[32,8,128]{2,1,0:T(8,128)S(1)}, s32[32,8,128]{2,1,0:T(8,128)S(1)}, s32[32,8,128]{2,1,0:T(8,128)S(1)}, s32[8,128]{1,0:T(8,128)S(1)}) custom-call(f32[3,32,8,128]{3,2,1,0:T(8,128)S(1)} %get-tuple-element.62.refs_0_, s32[32,8,128]{2,1,0:T(8,128)S(1)} %get-tuple-element.63.refs_1_), custom_call_target="tpu_custom_call" | custom-call | tf_op jit(solution)/shard_map/arrange/pallas_call | solution.py:242
  28.2 8.7 %cells.5.refs_0_ = f32[4,32,8,128]{3,2,1,0:T(8,128)S(1)} custom-call(s32[8,128]{1,0:T(8,128)S(1)} %get-tuple-element.64.refs_0_, f32[3,32,8,128]{3,2,1,0:T(8,128)S(1)} %get-tuple-element.70.refs_1_, s32[32,8,128]{2,1,0:T(8,128)S(1)} %get-tuple-element.66.refs_2_, bf16[256,48]{1,0:T(8,128)(2,1)S(1)} %copy.53.refs_3_.refs_2_, ...), custom_call_target="tpu_custom_call" | custom-call | flops 8053063680 | bytes 393216 | tf_op jit(solution)/shard_map/cells/pallas_call | solution.py:145
  36.9 7.9 %cells.6.refs_1_ = f32[4,32,8,128]{3,2,1,0:T(8,128)S(1)} custom-call(f32[3,32,8,128]{3,2,1,0:T(8,128)S(1)} %get-tuple-element.62.refs_0_, s32[32,8,128]{2,1,0:T(8,128)S(1)} %get-tuple-element.63.refs_1_, bf16[256,48]{1,0:T(8,128)(2,1)S(1)} %copy.53.refs_3_.refs_2_, bf16[4,256,256]{2,1,0:T(8,128)(2,1)S(1)} %copy-done.8, ...), custom_call_target="tpu_custom_call" | custom-call | flops 5368709120 | bytes 262144 | tf_op jit(solution)/shard_map/cells/pallas_call | solution.py:145
  44.8 2.6 %collective-permute-start.68 = (f32[4,8,128]{2,1,0:T(8,128)S(1)}, f32[4,8,128]{2,1,0:T(8,128)S(1)}, u32[]{:S(2)}, u32[]{:S(2)}) collective-permute-start(f32[4,8,128]{2,1,0:T(8,128)S(1)} %bitcast.120), channel_id=1, source_target_pairs={{0,1},{2,3},{11,10},{9,8},{16,17},{18,19},{27,26},{25,24},{28,29},... | collective-permute-start | bytes 49160 | tf_op jit(solution)/shard_map/ppermute | solution.py:759
  47.4 0.8 collective-permute-start.69
  48.2 8.7 %cells.7.refs_2_ = f32[4,32,8,128]{3,2,1,0:T(8,128)S(1)} custom-call(s32[8,128]{1,0:T(8,128)S(1)} %get-tuple-element.64.refs_0_, f32[3,32,8,128]{3,2,1,0:T(8,128)S(1)} %get-tuple-element.70.refs_1_, s32[32,8,128]{2,1,0:T(8,128)S(1)} %get-tuple-element.66.refs_2_, bf16[256,48]{1,0:T(8,128)(2,1)S(1)} %copy.53.refs_3_.refs_2_, ...), custom_call_target="tpu_custom_call" | custom-call | flops 8053063680 | bytes 393216 | tf_op jit(solution)/shard_map/cells/pallas_call | solution.py:145
  57.0 0.9 rhs.1
  57.9 0.7 collective-permute-start.71
  58.6 4.3 %collective-permute-start.70 = (f32[2,256,128]{2,1,0:T(8,128)S(1)}, f32[2,256,128]{2,1,0:T(8,128)S(1)}, u32[]{:S(2)}, u32[]{:S(2)}) collective-permute-start(f32[2,256,128]{2,1,0:T(8,128)S(1)} %rhs.1), channel_id=1, source_target_pairs={{0,1},{2,3},{11,10},{9,8},{16,17},{18,19},{27,26},{25,24},{28,29},... | collective-permute-start | bytes 786440 | tf_op jit(solution)/shard_map/ppermute | solution.py:759
  63.2 0.9 collective-permute-done.70
  64.1 1.5 %basis.2 = (f32[5,256,128]{2,1,0:T(8,128)S(1)}, f32[768,128]{1,0:T(8,128)S(1)}, f32[768,128]{1,0:T(8,128)S(1)}, f32[768,128]{1,0:T(8,128)S(1)}, f32[768,128]{1,0:T(8,128)S(1)}, /*index=5*/f32[768,128]{1,0:T(8,128)S(1)}) custom-call(f32[8,128]{1,0:T(8,128)S(1)} %get-tuple-element.61.scale_ref.refs_0_, f32[256,128]{1,0:T(8,128)S(1)} %get-tuple-element.253.tan_ref.refs_1_, ...), custom_call_target="tpu_custom_call" | custom-call | tf_op jit(solution)/shard_map/basis/pallas_call | solution.py:242
  65.6 0.7 collective-permute-start.72
  66.2 5.9 %collective-permute-start.73 = (f32[256,128]{1,0:T(8,128)S(1)}, f32[256,128]{1,0:T(8,128)S(1)}, u32[]{:S(2)}, u32[]{:S(2)}) collective-permute-start(f32[256,128]{1,0:T(8,128)S(1)} %slice_bitcast_fusion.12.refs_8_), channel_id=1, source_target_pairs={{0,1},{2,3},{11,10},{9,8},{16,17},{18,19},{27,26},{25,24},{28,29},... | collective-permute-start | bytes 393224 | tf_op jit(solution)/shard_map/ppermute | solution.py:759
  72.3 0.8 collective-permute-done.73.refs_9_
  73.1 0.9 basis.3
  74.0 14.0 %all_to_all.148 = f32[32,1,128]{2,1,0:T(1,128)S(1)} all-to-all(f32[32,1,128]{2,1,0:T(1,128)S(1)} %bitcast.73), channel_id=1, replica_groups=mesh['blk'=4,'slab'=2,'micro'=4] {'blk','slab','micro'}, dimensions={0} | all-to-all | bytes 32768 | tf_op jit(solution)/shard_map/all_to_all | solution.py:819
  88.0 1.7 %last.1 = (f32[16,2,2,8,128]{4,3,2,1,0:T(8,128)}, f32[8,128]{1,0:T(8,128)S(1)}) custom-call(f32[8,128]{1,0:T(8,128)S(1)} %get-tuple-element.61.scale_ref.refs_0_, f32[32,128]{1,0:T(8,128)S(1)} %bitcast.72, f32[5,256,128]{2,1,0:T(8,128)S(1)} %get-tuple-element.79.early_ref.refs_6_.refs_2_, f32[4,256,128]{2,1,0:T(8,128)S(1)} %get-tuple-element.86.refs_3_), custom_call_target="tpu_custom_call" | custom-call | tf_op jit(solution)/shard_map/last/pallas_call | solution.py:242
  89.7 3.7 %all-to-all-start.18 = ((f32[16,2,2,8,128]{4,3,2,1,0:T(8,128)}), f32[16,2,2,8,128]{4,3,2,1,0:T(8,128)S(1)}, u32[]{:S(2)}, u32[]{:S(2)}) async-start(f32[16,2,2,8,128]{4,3,2,1,0:T(8,128)} %get-tuple-element.88), calls=%async_computation.18 | async-start | bytes 524288 | tf_op jit(solution)/shard_map/all_to_all | solution.py:824
  94.6 8.8 %all-to-all-done.18.refs_1_ = f32[16,2,2,8,128]{4,3,2,1,0:T(8,128)S(1)} async-done(((f32[16,2,2,8,128]{4,3,2,1,0:T(8,128)}), f32[16,2,2,8,128]{4,3,2,1,0:T(8,128)S(1)}, u32[]{:S(2)}, u32[]{:S(2)}) %all-to-all-start.18) | async-done | bytes 262176 | tf_op jit(solution)/shard_map/all_to_all | solution.py:824
  103.5 1.0 deliver.1
  (47 shorter events, 3.4 us)
Async XLA Ops:
  2.7 21.9 %all-to-all-start.16 = ((f32[16,2,4,8,128]{4,3,2,1,0:T(8,128)}), f32[16,2,4,8,128]{4,3,2,1,0:T(8,128)S(1)}, u32[]{:S(2)}, u32[]{:S(2)}) async-start(f32[16,2,4,8,128]{4,3,2,1,0:T(8,128)} %spread.1), calls=%async_computation.16 | async-start | bytes 1048576 | tf_op jit(solution)/shard_map/all_to_all | solution.py:774
  10.2 0.7 copy-start.5
  10.9 0.7 copy-start.7
  11.6 13.0 %copy-start.6 = (f32[4,256]{1,0:T(4,128)S(1)}, f32[4,256]{1,0:T(4,128)}, u32[]{:S(2)}) copy-start(f32[4,256]{1,0:T(4,128)} %refs_0_.4) | copy-start | bytes 12292
  25.2 11.7 %collective-permute-start.66 = (f32[36,8,128]{2,1,0:T(8,128)S(1)}, f32[36,8,128]{2,1,0:T(8,128)S(1)}, u32[]{:S(2)}, u32[]{:S(2)}) collective-permute-start(f32[36,8,128]{2,1,0:T(8,128)S(1)} %get-tuple-element.67), channel_id=1, source_target_pairs={{0,1},{2,3},{11,10},{9,8},{16,17},{18,19},{27,26},{25,24},{28,29},... | collective-permute-start | bytes 442376 | tf_op jit(solution)/shard_map/ppermute | solution.py:759
  25.3 11.6 %collective-permute-start.67 = (f32[36,8,128]{2,1,0:T(8,128)S(1)}, f32[36,8,128]{2,1,0:T(8,128)S(1)}, u32[]{:S(2)}, u32[]{:S(2)}) collective-permute-start(f32[36,8,128]{2,1,0:T(8,128)S(1)} %get-tuple-element.68), channel_id=1, source_target_pairs={{1,2},{3,11},{10,9},{8,16},{17,18},{19,27},{26,25},{24,28},{29,30}... | collective-permute-start | bytes 442376 | tf_op jit(solution)/shard_map/ppermute | solution.py:759
  25.9 2.2 %copy-start.8 = (bf16[4,256,256]{2,1,0:T(8,128)(2,1)S(1)}, bf16[4,256,256]{2,1,0:T(8,128)(2,1)}, u32[]{:S(2)}) copy-start(bf16[4,256,256]{2,1,0:T(8,128)(2,1)} %refs_4_.5) | copy-start | bytes 1572868
  44.8 12.1 %collective-permute-start.68 = (f32[4,8,128]{2,1,0:T(8,128)S(1)}, f32[4,8,128]{2,1,0:T(8,128)S(1)}, u32[]{:S(2)}, u32[]{:S(2)}) collective-permute-start(f32[4,8,128]{2,1,0:T(8,128)S(1)} %bitcast.120), channel_id=1, source_target_pairs={{0,1},{2,3},{11,10},{9,8},{16,17},{18,19},{27,26},{25,24},{28,29},... | collective-permute-start | bytes 49160 | tf_op jit(solution)/shard_map/ppermute | solution.py:759
  47.4 9.5 %collective-permute-start.69 = (f32[4,8,128]{2,1,0:T(8,128)S(1)}, f32[4,8,128]{2,1,0:T(8,128)S(1)}, u32[]{:S(2)}, u32[]{:S(2)}) collective-permute-start(f32[4,8,128]{2,1,0:T(8,128)S(1)} %bitcast.119), channel_id=1, source_target_pairs={{1,2},{3,11},{10,9},{8,16},{17,18},{19,27},{26,25},{24,28},{29,30}... | collective-permute-start | bytes 49160 | tf_op jit(solution)/shard_map/ppermute | solution.py:759
  57.9 5.2 %collective-permute-start.71 = (f32[2,256,128]{2,1,0:T(8,128)S(1)}, f32[2,256,128]{2,1,0:T(8,128)S(1)}, u32[]{:S(2)}, u32[]{:S(2)}) collective-permute-start(f32[2,256,128]{2,1,0:T(8,128)S(1)} %rhs.1), channel_id=1, source_target_pairs={{1,2},{3,11},{10,9},{8,16},{17,18},{19,27},{26,25},{24,28},{29,30}... | collective-permute-start | bytes 786440 | tf_op jit(solution)/shard_map/ppermute | solution.py:759
  58.6 5.5 %collective-permute-start.70 = (f32[2,256,128]{2,1,0:T(8,128)S(1)}, f32[2,256,128]{2,1,0:T(8,128)S(1)}, u32[]{:S(2)}, u32[]{:S(2)}) collective-permute-start(f32[2,256,128]{2,1,0:T(8,128)S(1)} %rhs.1), channel_id=1, source_target_pairs={{0,1},{2,3},{11,10},{9,8},{16,17},{18,19},{27,26},{25,24},{28,29},... | collective-permute-start | bytes 786440 | tf_op jit(solution)/shard_map/ppermute | solution.py:759
  65.6 6.7 %collective-permute-start.72 = (f32[256,128]{1,0:T(8,128)S(1)}, f32[256,128]{1,0:T(8,128)S(1)}, u32[]{:S(2)}, u32[]{:S(2)}) collective-permute-start(f32[256,128]{1,0:T(8,128)S(1)} %slice_bitcast_fusion.12.refs_8_), channel_id=1, source_target_pairs={{1,2},{3,11},{10,9},{8,16},{17,18},{19,27},{26,25},{24,28},{29,30}... | collective-permute-start | bytes 393224 | tf_op jit(solution)/shard_map/ppermute | solution.py:759
  66.2 6.9 %collective-permute-start.73 = (f32[256,128]{1,0:T(8,128)S(1)}, f32[256,128]{1,0:T(8,128)S(1)}, u32[]{:S(2)}, u32[]{:S(2)}) collective-permute-start(f32[256,128]{1,0:T(8,128)S(1)} %slice_bitcast_fusion.12.refs_8_), channel_id=1, source_target_pairs={{0,1},{2,3},{11,10},{9,8},{16,17},{18,19},{27,26},{25,24},{28,29},... | collective-permute-start | bytes 393224 | tf_op jit(solution)/shard_map/ppermute | solution.py:759
  88.0 15.4 %copy-start.4 = (s32[8,32,128]{2,1,0:T(8,128)S(1)}, s32[8,32,128]{2,1,0:T(8,128)}, u32[]{:S(2)}) copy-start(s32[8,32,128]{2,1,0:T(8,128)} %refs_4_.3) | copy-start | bytes 393220
  89.7 13.7 %copy-start = (f32[8,32,128]{2,1,0:T(8,128)S(1)}, f32[8,32,128]{2,1,0:T(8,128)}, u32[]{:S(2)}) copy-start(f32[8,32,128]{2,1,0:T(8,128)} %refs_2_.1) | copy-start | bytes 393220
  89.7 13.7 %copy-start.1 = (f32[8,32,128]{2,1,0:T(8,128)S(1)}, f32[8,32,128]{2,1,0:T(8,128)}, u32[]{:S(2)}) copy-start(f32[8,32,128]{2,1,0:T(8,128)} %refs_0_.5) | copy-start | bytes 393220
  89.7 13.7 %copy-start.2 = (f32[8,32,128]{2,1,0:T(8,128)S(1)}, f32[8,32,128]{2,1,0:T(8,128)}, u32[]{:S(2)}) copy-start(f32[8,32,128]{2,1,0:T(8,128)} %refs_1_.1) | copy-start | bytes 393220
  89.7 13.7 %copy-start.3 = (s32[8,32,128]{2,1,0:T(8,128)S(1)}, s32[8,32,128]{2,1,0:T(8,128)}, u32[]{:S(2)}) copy-start(s32[8,32,128]{2,1,0:T(8,128)} %refs_3_.2) | copy-start | bytes 393220
  89.7 13.7 %all-to-all-start.18 = ((f32[16,2,2,8,128]{4,3,2,1,0:T(8,128)}), f32[16,2,2,8,128]{4,3,2,1,0:T(8,128)S(1)}, u32[]{:S(2)}, u32[]{:S(2)}) async-start(f32[16,2,2,8,128]{4,3,2,1,0:T(8,128)} %get-tuple-element.88), calls=%async_computation.18 | async-start | bytes 524288 | tf_op jit(solution)/shard_map/all_to_all | solution.py:824

commit v9 on v8

--- a/solution.py
+++ b/solution.py
@@ -25,11 +25,23 @@
     none = jnp.zeros((families, 1, modes), BF)
     stress = jnp.concatenate([family_out, none], axis=1).reshape(4 * families, modes)
     weight_tan = jnp.broadcast_to(family_tan[:, :, None], (families, modes, 128))
-    return weight_in, family_mid, stress, weight_tan
-
-
-def cells_kernel(families, planes, strain_ref, code_ref, in_ref, mid_ref, out_ref, tan_ref, *refs, info_ref=None):
-    *edges, answer_ref = refs
+    none = jnp.zeros((families, 3, modes), BF)
+    tan_high, tan_low = split(family_tan)
+    tan_high = jnp.concatenate([none, tan_high[:, None]], axis=1).reshape(4 * families, modes)
+    tan_low = jnp.concatenate([none, tan_low[:, None]], axis=1).reshape(4 * families, modes)
+    wide = jnp.concatenate(
+        [
+            jnp.concatenate([stress, tan_high], axis=1),
+            jnp.concatenate([jnp.zeros_like(stress), tan_low], axis=1),
+        ],
+        axis=0,
+    )
+    return weight_in, family_mid, wide, stress, weight_tan
+
+
+def cells_kernel(families, planes, strain_ref, code_ref, in_ref, mid_ref, out_ref, *refs, info_ref=None):
+    *edges, answer_ref = refs if info_ref is None else refs[1:]
+    tan_ref = None if info_ref is None else refs[0]
     modes = in_ref.shape[0]
     step = code_ref.shape[0]
     spots = [(a + i, x) for a in range(0, step, 2) for x in planes for i in range(2)]
@@ -85,7 +97,12 @@
                 parts.append(jnp.dot(mixing, stacked, preferred_element_type=F32))
             hidden = jnp.concatenate(parts, axis=1)
         bounded = jnp.tanh(hidden).astype(BF)
-        result = jnp.dot(out_ref[...], bounded, preferred_element_type=F32)
+        if tan_ref is None:
+            both = jnp.concatenate([bounded, bounded * bounded], axis=0)
+            result = jnp.dot(out_ref[...], both, preferred_element_type=F32)
+            result = result[: 4 * families] + result[4 * families :]
+        else:
+            result = jnp.dot(out_ref[...], bounded, preferred_element_type=F32)
         owner = lax.shift_right_logical(lax.broadcasted_iota(jnp.int32, (4 * families, width), 0), 2)
         result = jnp.where(owner == family, result, 0.0)
         total = result[:4]
@@ -93,6 +110,9 @@
             total = total + result[4 * f : 4 * f + 4]
         for i, (a, x) in enumerate(spots):
             part = slice(i * 128, (i + 1) * 128)
+            if tan_ref is None:
+                answer_ref[:, a, x, :] = total[:, part]
+                continue
             answer_ref[0:3, a, x, :] = total[0:3, part]
             square = bounded[:, part].astype(F32)
             square = square * square
@@ -126,7 +146,8 @@
 
 
 def cells(strain, code, packed, families, step, planes, *edges, info=None):
-    weight_in, weight_mid, weight_out, weight_tan = packed
+    weight_in, weight_mid, weight_wide, weight_out, weight_tan = packed
+    weights = (weight_in, weight_mid, weight_wide) if info is None else (weight_in, weight_mid, weight_out, weight_tan)
     count = code.shape[0]
     planes = tuple(planes)
     points = count * len(planes) * 128
@@ -150,11 +171,8 @@
             in_specs=[
                 pl.BlockSpec((3, step, 8, 128), lambda i, *_: (0, i, 0, 0)),
                 pl.BlockSpec((step, 8, 128), lambda i, *_: (i, 0, 0)),
-                whole(weight_in),
-                whole(weight_mid),
-                whole(weight_out),
-                whole(weight_tan),
             ]
+            + [whole(weight) for weight in weights]
             + [pl.BlockSpec((1, 128), lambda i, *_: (0, 0)) for _ in edges[:1]]
             + [pl.BlockSpec((1, 8, 128), lambda i, *_: (count + i, 0, 0)) for _ in edges[1:]],
             out_specs=pl.BlockSpec((4, step, 8, 128), lambda i, *_: (0, i, 0, 0)),
@@ -165,7 +183,7 @@
             flops=2 * points * modes * modes * (families + 1), bytes_accessed=points * 32, transcendentals=2 * points * modes
         ),
         name="cells",
-    )(*scalars, strain, code, weight_in, weight_mid, weight_out, weight_tan, *edges)
+    )(*scalars, strain, code, *weights, *edges)
 
 
 def global_sum(value):

time: 105 us -> 104 us (level)
  no operation moved by 1% of the time
where the time goes in v9:
time: 104 us
  Pallas kernels  35.5 us (34%)
  starting transfers between devices  26.7 us (26%)
  waiting for transfers between devices  22.8 us (22%)
  blocking collectives  14 us (13%)
  local copies, waits for them, and re-layouts  2.96 us (3%)
  between operations  1.65 us (2%)
    pallas_call x3, Pallas kernels, cells(): pl.pallas_call(kernel, grid_spec=pltpu.PrefetchScalarGridSpec(num_scalar_...  24.5 us
    all_to_all x2, waiting for transfers between devices, sliced_body(): recv = lax.all_to_all(send, GROUP, 0, 0, tiled=True)  21 us
    ppermute x8, starting transfers between devices, swap(): return lax.ppermute(value, AXES, pairs + [(b, a) for a, b in pairs])  15.7 us
    all_to_all x1, blocking collectives, sliced_body(): sums = lax.all_to_all(sums, AXES, 0, 0, tiled=True)  14 us
    all_to_all x2, starting transfers between devices, sliced_body(): recv = lax.all_to_all(send, GROUP, 0, 0, tiled=True)  11.1 us
    pallas_call x10, Pallas kernels, call(): pl.pallas_call(kernel, out_shape=[jax.ShapeDtypeStruct(shape, dtype) for...  11 us
  transfers between devices with their start and end apart: 10, of which 4 were waited for; matrix products, arithmetic and copies ran while one was open for 1% of the time, Pallas kernels for 19%

profile of v9, /device:TPU:0, one launch (start us, length us, event | category | flops | bytes accessed | tf_op | source)
XLA Modules:
  0.0 103.7 jit_solution(14802156312163043388)
XLA Ops:
  0.6 2.1 %spread.1 = f32[16,2,4,8,128]{4,3,2,1,0:T(8,128)} custom-call(f32[8,32,128]{2,1,0:T(8,128)} %refs_0_.5, f32[8,32,128]{2,1,0:T(8,128)} %refs_1_.1, f32[8,32,128]{2,1,0:T(8,128)} %refs_2_.1, s32[8,32,128]{2,1,0:T(8,128)} %refs_3_.2, s32[8,32,128]{2,1,0:T(8,128)} %refs_4_.3), custom_call_target="tpu_custom_call" | custom-call | tf_op jit(solution)/shard_map/spread/pallas_call | solution.py:260
  2.7 7.4 %all-to-all-start.16 = ((f32[16,2,4,8,128]{4,3,2,1,0:T(8,128)}), f32[16,2,4,8,128]{4,3,2,1,0:T(8,128)S(1)}, u32[]{:S(2)}, u32[]{:S(2)}) async-start(f32[16,2,4,8,128]{4,3,2,1,0:T(8,128)} %spread.1), calls=%async_computation.16 | async-start | bytes 1048576 | tf_op jit(solution)/shard_map/all_to_all | solution.py:792
  10.2 0.7 copy-done.6
  12.4 12.2 %all-to-all-done.16.refs_1_ = f32[16,2,4,8,128]{4,3,2,1,0:T(8,128)S(1)} async-done(((f32[16,2,4,8,128]{4,3,2,1,0:T(8,128)}), f32[16,2,4,8,128]{4,3,2,1,0:T(8,128)S(1)}, u32[]{:S(2)}, u32[]{:S(2)}) %all-to-all-start.16) | async-done | bytes 524320 | tf_op jit(solution)/shard_map/all_to_all | solution.py:792
  25.9 2.0 %arrange.1 = (f32[3,32,8,128]{3,2,1,0:T(8,128)S(1)}, s32[32,8,128]{2,1,0:T(8,128)S(1)}, s32[32,8,128]{2,1,0:T(8,128)S(1)}, s32[32,8,128]{2,1,0:T(8,128)S(1)}, s32[8,128]{1,0:T(8,128)S(1)}) custom-call(f32[3,32,8,128]{3,2,1,0:T(8,128)S(1)} %get-tuple-element.62.refs_0_, s32[32,8,128]{2,1,0:T(8,128)S(1)} %get-tuple-element.63.refs_1_), custom_call_target="tpu_custom_call" | custom-call | tf_op jit(solution)/shard_map/arrange/pallas_call | solution.py:260
  28.2 8.4 %cells.5.refs_0_ = f32[4,32,8,128]{3,2,1,0:T(8,128)S(1)} custom-call(s32[8,128]{1,0:T(8,128)S(1)} %get-tuple-element.64.refs_0_, f32[3,32,8,128]{3,2,1,0:T(8,128)S(1)} %get-tuple-element.70.refs_1_, s32[32,8,128]{2,1,0:T(8,128)S(1)} %get-tuple-element.66.refs_2_, bf16[256,48]{1,0:T(8,128)(2,1)S(1)} %copy.71.refs_3_.refs_2_, ...), custom_call_target="tpu_custom_call" | custom-call | flops 8053063680 | bytes 393216 | tf_op jit(solution)/shard_map/cells/pallas_call | solution.py:166
  36.6 7.6 %cells.6.refs_1_ = f32[4,32,8,128]{3,2,1,0:T(8,128)S(1)} custom-call(f32[3,32,8,128]{3,2,1,0:T(8,128)S(1)} %get-tuple-element.62.refs_0_, s32[32,8,128]{2,1,0:T(8,128)S(1)} %get-tuple-element.63.refs_1_, bf16[256,48]{1,0:T(8,128)(2,1)S(1)} %copy.71.refs_3_.refs_2_, bf16[4,256,256]{2,1,0:T(8,128)(2,1)S(1)} %copy-done.8, bf16[32,512]{1,0:T(8,128)(2,1)S(1)} %fusion.104.refs_4_, ...), custom_call_target="tpu_custom_call" | custom-call | flops 5368709120 | bytes 262144 | tf_op jit(solution)/shard_map/cells/pallas_call | solution.py:166
  44.3 2.6 %collective-permute-start.68 = (f32[4,8,128]{2,1,0:T(8,128)S(1)}, f32[4,8,128]{2,1,0:T(8,128)S(1)}, u32[]{:S(2)}, u32[]{:S(2)}) collective-permute-start(f32[4,8,128]{2,1,0:T(8,128)S(1)} %bitcast.128), channel_id=1, source_target_pairs={{0,1},{2,3},{11,10},{9,8},{16,17},{18,19},{27,26},{25,24},{28,29},... | collective-permute-start | bytes 49160 | tf_op jit(solution)/shard_map/ppermute | solution.py:777
  46.9 0.8 collective-permute-start.69
  47.7 8.4 %cells.7.refs_2_ = f32[4,32,8,128]{3,2,1,0:T(8,128)S(1)} custom-call(s32[8,128]{1,0:T(8,128)S(1)} %get-tuple-element.64.refs_0_, f32[3,32,8,128]{3,2,1,0:T(8,128)S(1)} %get-tuple-element.70.refs_1_, s32[32,8,128]{2,1,0:T(8,128)S(1)} %get-tuple-element.66.refs_2_, bf16[256,48]{1,0:T(8,128)(2,1)S(1)} %copy.71.refs_3_.refs_2_, ...), custom_call_target="tpu_custom_call" | custom-call | flops 8053063680 | bytes 393216 | tf_op jit(solution)/shard_map/cells/pallas_call | solution.py:166
  56.2 0.9 rhs.1
  57.1 0.7 collective-permute-start.71
  57.8 4.3 %collective-permute-start.70 = (f32[2,256,128]{2,1,0:T(8,128)S(1)}, f32[2,256,128]{2,1,0:T(8,128)S(1)}, u32[]{:S(2)}, u32[]{:S(2)}) collective-permute-start(f32[2,256,128]{2,1,0:T(8,128)S(1)} %rhs.1), channel_id=1, source_target_pairs={{0,1},{2,3},{11,10},{9,8},{16,17},{18,19},{27,26},{25,24},{28,29},... | collective-permute-start | bytes 786440 | tf_op jit(solution)/shard_map/ppermute | solution.py:777
  62.4 0.9 collective-permute-done.70
  63.3 1.5 %basis.2 = (f32[5,256,128]{2,1,0:T(8,128)S(1)}, f32[768,128]{1,0:T(8,128)S(1)}, f32[768,128]{1,0:T(8,128)S(1)}, f32[768,128]{1,0:T(8,128)S(1)}, f32[768,128]{1,0:T(8,128)S(1)}, /*index=5*/f32[768,128]{1,0:T(8,128)S(1)}) custom-call(f32[8,128]{1,0:T(8,128)S(1)} %get-tuple-element.61.scale_ref.refs_0_, f32[256,128]{1,0:T(8,128)S(1)} %get-tuple-element.255.tan_ref.refs_1_, ...), custom_call_target="tpu_custom_call" | custom-call | tf_op jit(solution)/shard_map/basis/pallas_call | solution.py:260
  64.8 0.7 collective-permute-start.72
  65.5 5.9 %collective-permute-start.73 = (f32[256,128]{1,0:T(8,128)S(1)}, f32[256,128]{1,0:T(8,128)S(1)}, u32[]{:S(2)}, u32[]{:S(2)}) collective-permute-start(f32[256,128]{1,0:T(8,128)S(1)} %slice_bitcast_fusion.12.refs_8_), channel_id=1, source_target_pairs={{0,1},{2,3},{11,10},{9,8},{16,17},{18,19},{27,26},{25,24},{28,29},... | collective-permute-start | bytes 393224 | tf_op jit(solution)/shard_map/ppermute | solution.py:777
  71.5 0.8 collective-permute-done.73.refs_9_
  72.3 0.9 basis.3
  73.2 14.0 %all_to_all.148 = f32[32,1,128]{2,1,0:T(1,128)S(1)} all-to-all(f32[32,1,128]{2,1,0:T(1,128)S(1)} %bitcast.81), channel_id=1, replica_groups=mesh['blk'=4,'slab'=2,'micro'=4] {'blk','slab','micro'}, dimensions={0} | all-to-all | bytes 32768 | tf_op jit(solution)/shard_map/all_to_all | solution.py:837
  87.3 1.7 %last.1 = (f32[16,2,2,8,128]{4,3,2,1,0:T(8,128)}, f32[8,128]{1,0:T(8,128)S(1)}) custom-call(f32[8,128]{1,0:T(8,128)S(1)} %get-tuple-element.61.scale_ref.refs_0_, f32[32,128]{1,0:T(8,128)S(1)} %bitcast.80, f32[5,256,128]{2,1,0:T(8,128)S(1)} %get-tuple-element.79.early_ref.refs_6_.refs_2_, f32[4,256,128]{2,1,0:T(8,128)S(1)} %get-tuple-element.86.refs_3_), custom_call_target="tpu_custom_call" | custom-call | tf_op jit(solution)/shard_map/last/pallas_call | solution.py:260
  89.0 3.7 %all-to-all-start.18 = ((f32[16,2,2,8,128]{4,3,2,1,0:T(8,128)}), f32[16,2,2,8,128]{4,3,2,1,0:T(8,128)S(1)}, u32[]{:S(2)}, u32[]{:S(2)}) async-start(f32[16,2,2,8,128]{4,3,2,1,0:T(8,128)} %get-tuple-element.88), calls=%async_computation.18 | async-start | bytes 524288 | tf_op jit(solution)/shard_map/all_to_all | solution.py:842
  93.8 8.8 %all-to-all-done.18.refs_1_ = f32[16,2,2,8,128]{4,3,2,1,0:T(8,128)S(1)} async-done(((f32[16,2,2,8,128]{4,3,2,1,0:T(8,128)}), f32[16,2,2,8,128]{4,3,2,1,0:T(8,128)S(1)}, u32[]{:S(2)}, u32[]{:S(2)}) %all-to-all-start.18) | async-done | bytes 262176 | tf_op jit(solution)/shard_map/all_to_all | solution.py:842
  102.7 1.0 deliver.1
  (55 shorter events, 4.1 us)
Async XLA Ops:
  2.7 21.9 %all-to-all-start.16 = ((f32[16,2,4,8,128]{4,3,2,1,0:T(8,128)}), f32[16,2,4,8,128]{4,3,2,1,0:T(8,128)S(1)}, u32[]{:S(2)}, u32[]{:S(2)}) async-start(f32[16,2,4,8,128]{4,3,2,1,0:T(8,128)} %spread.1), calls=%async_computation.16 | async-start | bytes 1048576 | tf_op jit(solution)/shard_map/all_to_all | solution.py:792
  10.1 0.7 copy-start.6
  10.9 0.7 copy-start.7
  11.6 0.7 copy-start.5
  25.2 11.5 %collective-permute-start.66 = (f32[36,8,128]{2,1,0:T(8,128)S(1)}, f32[36,8,128]{2,1,0:T(8,128)S(1)}, u32[]{:S(2)}, u32[]{:S(2)}) collective-permute-start(f32[36,8,128]{2,1,0:T(8,128)S(1)} %get-tuple-element.67), channel_id=1, source_target_pairs={{0,1},{2,3},{11,10},{9,8},{16,17},{18,19},{27,26},{25,24},{28,29},... | collective-permute-start | bytes 442376 | tf_op jit(solution)/shard_map/ppermute | solution.py:777
  25.2 11.4 %collective-permute-start.67 = (f32[36,8,128]{2,1,0:T(8,128)S(1)}, f32[36,8,128]{2,1,0:T(8,128)S(1)}, u32[]{:S(2)}, u32[]{:S(2)}) collective-permute-start(f32[36,8,128]{2,1,0:T(8,128)S(1)} %get-tuple-element.68), channel_id=1, source_target_pairs={{1,2},{3,11},{10,9},{8,16},{17,18},{19,27},{26,25},{24,28},{29,30}... | collective-permute-start | bytes 442376 | tf_op jit(solution)/shard_map/ppermute | solution.py:777
  25.9 2.3 %copy-start.8 = (bf16[4,256,256]{2,1,0:T(8,128)(2,1)S(1)}, bf16[4,256,256]{2,1,0:T(8,128)(2,1)}, u32[]{:S(2)}) copy-start(bf16[4,256,256]{2,1,0:T(8,128)(2,1)} %refs_4_.5) | copy-start | bytes 1572868
  44.3 11.9 %collective-permute-start.68 = (f32[4,8,128]{2,1,0:T(8,128)S(1)}, f32[4,8,128]{2,1,0:T(8,128)S(1)}, u32[]{:S(2)}, u32[]{:S(2)}) collective-permute-start(f32[4,8,128]{2,1,0:T(8,128)S(1)} %bitcast.128), channel_id=1, source_target_pairs={{0,1},{2,3},{11,10},{9,8},{16,17},{18,19},{27,26},{25,24},{28,29},... | collective-permute-start | bytes 49160 | tf_op jit(solution)/shard_map/ppermute | solution.py:777
  46.9 9.3 %collective-permute-start.69 = (f32[4,8,128]{2,1,0:T(8,128)S(1)}, f32[4,8,128]{2,1,0:T(8,128)S(1)}, u32[]{:S(2)}, u32[]{:S(2)}) collective-permute-start(f32[4,8,128]{2,1,0:T(8,128)S(1)} %bitcast.127), channel_id=1, source_target_pairs={{1,2},{3,11},{10,9},{8,16},{17,18},{19,27},{26,25},{24,28},{29,30}... | collective-permute-start | bytes 49160 | tf_op jit(solution)/shard_map/ppermute | solution.py:777
  57.1 5.2 %collective-permute-start.71 = (f32[2,256,128]{2,1,0:T(8,128)S(1)}, f32[2,256,128]{2,1,0:T(8,128)S(1)}, u32[]{:S(2)}, u32[]{:S(2)}) collective-permute-start(f32[2,256,128]{2,1,0:T(8,128)S(1)} %rhs.1), channel_id=1, source_target_pairs={{1,2},{3,11},{10,9},{8,16},{17,18},{19,27},{26,25},{24,28},{29,30}... | collective-permute-start | bytes 786440 | tf_op jit(solution)/shard_map/ppermute | solution.py:777
  57.8 5.5 %collective-permute-start.70 = (f32[2,256,128]{2,1,0:T(8,128)S(1)}, f32[2,256,128]{2,1,0:T(8,128)S(1)}, u32[]{:S(2)}, u32[]{:S(2)}) collective-permute-start(f32[2,256,128]{2,1,0:T(8,128)S(1)} %rhs.1), channel_id=1, source_target_pairs={{0,1},{2,3},{11,10},{9,8},{16,17},{18,19},{27,26},{25,24},{28,29},... | collective-permute-start | bytes 786440 | tf_op jit(solution)/shard_map/ppermute | solution.py:777
  64.8 6.7 %collective-permute-start.72 = (f32[256,128]{1,0:T(8,128)S(1)}, f32[256,128]{1,0:T(8,128)S(1)}, u32[]{:S(2)}, u32[]{:S(2)}) collective-permute-start(f32[256,128]{1,0:T(8,128)S(1)} %slice_bitcast_fusion.12.refs_8_), channel_id=1, source_target_pairs={{1,2},{3,11},{10,9},{8,16},{17,18},{19,27},{26,25},{24,28},{29,30}... | collective-permute-start | bytes 393224 | tf_op jit(solution)/shard_map/ppermute | solution.py:777
  65.5 6.9 %collective-permute-start.73 = (f32[256,128]{1,0:T(8,128)S(1)}, f32[256,128]{1,0:T(8,128)S(1)}, u32[]{:S(2)}, u32[]{:S(2)}) collective-permute-start(f32[256,128]{1,0:T(8,128)S(1)} %slice_bitcast_fusion.12.refs_8_), channel_id=1, source_target_pairs={{0,1},{2,3},{11,10},{9,8},{16,17},{18,19},{27,26},{25,24},{28,29},... | collective-permute-start | bytes 393224 | tf_op jit(solution)/shard_map/ppermute | solution.py:777
  87.3 15.4 %copy-start.4 = (s32[8,32,128]{2,1,0:T(8,128)S(1)}, s32[8,32,128]{2,1,0:T(8,128)}, u32[]{:S(2)}) copy-start(s32[8,32,128]{2,1,0:T(8,128)} %refs_4_.3) | copy-start | bytes 393220
  88.9 13.7 %copy-start = (f32[8,32,128]{2,1,0:T(8,128)S(1)}, f32[8,32,128]{2,1,0:T(8,128)}, u32[]{:S(2)}) copy-start(f32[8,32,128]{2,1,0:T(8,128)} %refs_2_.1) | copy-start | bytes 393220
  89.0 13.7 %copy-start.1 = (f32[8,32,128]{2,1,0:T(8,128)S(1)}, f32[8,32,128]{2,1,0:T(8,128)}, u32[]{:S(2)}) copy-start(f32[8,32,128]{2,1,0:T(8,128)} %refs_0_.5) | copy-start | bytes 393220
  89.0 13.7 %copy-start.2 = (f32[8,32,128]{2,1,0:T(8,128)S(1)}, f32[8,32,128]{2,1,0:T(8,128)}, u32[]{:S(2)}) copy-start(f32[8,32,128]{2,1,0:T(8,128)} %refs_1_.1) | copy-start | bytes 393220
  89.0 13.7 %copy-start.3 = (s32[8,32,128]{2,1,0:T(8,128)S(1)}, s32[8,32,128]{2,1,0:T(8,128)}, u32[]{:S(2)}) copy-start(s32[8,32,128]{2,1,0:T(8,128)} %refs_3_.2) | copy-start | bytes 393220
  89.0 13.7 %all-to-all-start.18 = ((f32[16,2,2,8,128]{4,3,2,1,0:T(8,128)}), f32[16,2,2,8,128]{4,3,2,1,0:T(8,128)S(1)}, u32[]{:S(2)}, u32[]{:S(2)}) async-start(f32[16,2,2,8,128]{4,3,2,1,0:T(8,128)} %get-tuple-element.88), calls=%async_computation.18 | async-start | bytes 524288 | tf_op jit(solution)/shard_map/all_to_all | solution.py:842

commit v10 on v9

--- a/solution.py
+++ b/solution.py
@@ -59,7 +59,7 @@
                 value = strain_ref[j, a, pl.ds(x, 1), :]
                 if edges and j == 2:
                     even, chip_ref, far_ref = edges
-                    chip, far = chip_ref[0, pl.ds(a, 1), :], far_ref[0, pl.ds(a, 1), :]
+                    chip, far = chip_ref[a // 8, pl.ds(a % 8, 1), :], far_ref[a // 8, pl.ds(a % 8, 1), :]
                     beyond = jnp.where(even[...] == (1 if x == 7 else 0), chip, far) * 0.5
                     value = value - beyond if x == 0 else value + beyond
                 value = jnp.broadcast_to(value, place.shape)
@@ -174,7 +174,7 @@
             ]
             + [whole(weight) for weight in weights]
             + [pl.BlockSpec((1, 128), lambda i, *_: (0, 0)) for _ in edges[:1]]
-            + [pl.BlockSpec((1, 8, 128), lambda i, *_: (count + i, 0, 0)) for _ in edges[1:]],
+            + [pl.BlockSpec((step // 8, 8, 128), lambda i, *_: (count * 8 // step + i, 0, 0)) for _ in edges[1:]],
             out_specs=pl.BlockSpec((4, step, 8, 128), lambda i, *_: (0, i, 0, 0)),
         ),
         out_shape=jax.ShapeDtypeStruct((4, count, 8, 128), F32),
@@ -806,7 +806,7 @@
         [], "arrange", strain, code,
     )
     first = cells(grouped, grouped_code, packed, families, 8, (1, 2, 3), info=info)
-    outer = cells(strain, code, packed, families, 8, (0, 7), jnp.broadcast_to(even.astype(jnp.int32), (1, 128)), chip, far)
+    outer = cells(strain, code, packed, families, 16, (0, 7), jnp.broadcast_to(even.astype(jnp.int32), (1, 128)), chip, far)
     top, bottom = outer[2, :, 7].reshape(edge), outer[2, :, 0].reshape(edge)
     edge_chip, edge_far = neighbours(jnp.where(even, top, bottom), jnp.where(even, bottom, top))
     grouped, outer = lax.optimization_barrier((grouped, outer))

time: 104 us -> 104 us (level)
  no operation moved by 1% of the time
where the time goes in v10:
time: 104 us
  Pallas kernels  35.4 us (34%)
  starting transfers between devices  26.7 us (26%)
  waiting for transfers between devices  22.8 us (22%)
  blocking collectives  14 us (13%)
  local copies, waits for them, and re-layouts  2.96 us (3%)
  between operations  1.65 us (2%)
    pallas_call x3, Pallas kernels, cells(): pl.pallas_call(kernel, grid_spec=pltpu.PrefetchScalarGridSpec(num_scalar_...  24.3 us
    all_to_all x2, waiting for transfers between devices, sliced_body(): recv = lax.all_to_all(send, GROUP, 0, 0, tiled=True)  21 us
    ppermute x8, starting transfers between devices, swap(): return lax.ppermute(value, AXES, pairs + [(b, a) for a, b in pairs])  15.7 us
    all_to_all x1, blocking collectives, sliced_body(): sums = lax.all_to_all(sums, AXES, 0, 0, tiled=True)  14 us
    all_to_all x2, starting transfers between devices, sliced_body(): recv = lax.all_to_all(send, GROUP, 0, 0, tiled=True)  11.1 us
    pallas_call x10, Pallas kernels, call(): pl.pallas_call(kernel, out_shape=[jax.ShapeDtypeStruct(shape, dtype) for...  11 us
  transfers between devices with their start and end apart: 10, of which 4 were waited for; matrix products, arithmetic and copies ran while one was open for 1% of the time, Pallas kernels for 19%

profile of v10, /device:TPU:0, one launch (start us, length us, event | category | flops | bytes accessed | tf_op | source)
XLA Modules:
  0.0 103.6 jit_solution(17485179763964005036)
XLA Ops:
  0.6 2.1 %spread.1 = f32[16,2,4,8,128]{4,3,2,1,0:T(8,128)} custom-call(f32[8,32,128]{2,1,0:T(8,128)} %refs_0_.5, f32[8,32,128]{2,1,0:T(8,128)} %refs_1_.1, f32[8,32,128]{2,1,0:T(8,128)} %refs_2_.1, s32[8,32,128]{2,1,0:T(8,128)} %refs_3_.2, s32[8,32,128]{2,1,0:T(8,128)} %refs_4_.3), custom_call_target="tpu_custom_call" | custom-call | tf_op jit(solution)/shard_map/spread/pallas_call | solution.py:260
  2.7 7.4 %all-to-all-start.16 = ((f32[16,2,4,8,128]{4,3,2,1,0:T(8,128)}), f32[16,2,4,8,128]{4,3,2,1,0:T(8,128)S(1)}, u32[]{:S(2)}, u32[]{:S(2)}) async-start(f32[16,2,4,8,128]{4,3,2,1,0:T(8,128)} %spread.1), calls=%async_computation.16 | async-start | bytes 1048576 | tf_op jit(solution)/shard_map/all_to_all | solution.py:792
  10.2 0.7 copy-done.6
  12.4 12.2 %all-to-all-done.16.refs_1_ = f32[16,2,4,8,128]{4,3,2,1,0:T(8,128)S(1)} async-done(((f32[16,2,4,8,128]{4,3,2,1,0:T(8,128)}), f32[16,2,4,8,128]{4,3,2,1,0:T(8,128)S(1)}, u32[]{:S(2)}, u32[]{:S(2)}) %all-to-all-start.16) | async-done | bytes 524320 | tf_op jit(solution)/shard_map/all_to_all | solution.py:792
  25.9 2.0 %arrange.1 = (f32[3,32,8,128]{3,2,1,0:T(8,128)S(1)}, s32[32,8,128]{2,1,0:T(8,128)S(1)}, s32[32,8,128]{2,1,0:T(8,128)S(1)}, s32[32,8,128]{2,1,0:T(8,128)S(1)}, s32[8,128]{1,0:T(8,128)S(1)}) custom-call(f32[3,32,8,128]{3,2,1,0:T(8,128)S(1)} %get-tuple-element.62.refs_0_, s32[32,8,128]{2,1,0:T(8,128)S(1)} %get-tuple-element.63.refs_1_), custom_call_target="tpu_custom_call" | custom-call | tf_op jit(solution)/shard_map/arrange/pallas_call | solution.py:260
  28.2 8.4 %cells.5.refs_0_ = f32[4,32,8,128]{3,2,1,0:T(8,128)S(1)} custom-call(s32[8,128]{1,0:T(8,128)S(1)} %get-tuple-element.64.refs_0_, f32[3,32,8,128]{3,2,1,0:T(8,128)S(1)} %get-tuple-element.70.refs_1_, s32[32,8,128]{2,1,0:T(8,128)S(1)} %get-tuple-element.66.refs_2_, bf16[256,48]{1,0:T(8,128)(2,1)S(1)} %copy.71.refs_3_.refs_2_, ...), custom_call_target="tpu_custom_call" | custom-call | flops 8053063680 | bytes 393216 | tf_op jit(solution)/shard_map/cells/pallas_call | solution.py:166
  36.6 7.5 %cells.6.refs_1_ = f32[4,32,8,128]{3,2,1,0:T(8,128)S(1)} custom-call(f32[3,32,8,128]{3,2,1,0:T(8,128)S(1)} %get-tuple-element.62.refs_0_, s32[32,8,128]{2,1,0:T(8,128)S(1)} %get-tuple-element.63.refs_1_, bf16[256,48]{1,0:T(8,128)(2,1)S(1)} %copy.71.refs_3_.refs_2_, bf16[4,256,256]{2,1,0:T(8,128)(2,1)S(1)} %copy-done.8, bf16[32,512]{1,0:T(8,128)(2,1)S(1)} %fusion.104.refs_4_, ...), custom_call_target="tpu_custom_call" | custom-call | flops 5368709120 | bytes 262144 | tf_op jit(solution)/shard_map/cells/pallas_call | solution.py:166
  44.2 2.6 %collective-permute-start.68 = (f32[4,8,128]{2,1,0:T(8,128)S(1)}, f32[4,8,128]{2,1,0:T(8,128)S(1)}, u32[]{:S(2)}, u32[]{:S(2)}) collective-permute-start(f32[4,8,128]{2,1,0:T(8,128)S(1)} %bitcast.128), channel_id=1, source_target_pairs={{0,1},{2,3},{11,10},{9,8},{16,17},{18,19},{27,26},{25,24},{28,29},... | collective-permute-start | bytes 49160 | tf_op jit(solution)/shard_map/ppermute | solution.py:777
  46.7 0.8 collective-permute-start.69
  47.6 8.4 %cells.7.refs_2_ = f32[4,32,8,128]{3,2,1,0:T(8,128)S(1)} custom-call(s32[8,128]{1,0:T(8,128)S(1)} %get-tuple-element.64.refs_0_, f32[3,32,8,128]{3,2,1,0:T(8,128)S(1)} %get-tuple-element.70.refs_1_, s32[32,8,128]{2,1,0:T(8,128)S(1)} %get-tuple-element.66.refs_2_, bf16[256,48]{1,0:T(8,128)(2,1)S(1)} %copy.71.refs_3_.refs_2_, ...), custom_call_target="tpu_custom_call" | custom-call | flops 8053063680 | bytes 393216 | tf_op jit(solution)/shard_map/cells/pallas_call | solution.py:166
  56.1 0.9 rhs.1
  57.0 0.7 collective-permute-start.71
  57.7 4.3 %collective-permute-start.70 = (f32[2,256,128]{2,1,0:T(8,128)S(1)}, f32[2,256,128]{2,1,0:T(8,128)S(1)}, u32[]{:S(2)}, u32[]{:S(2)}) collective-permute-start(f32[2,256,128]{2,1,0:T(8,128)S(1)} %rhs.1), channel_id=1, source_target_pairs={{0,1},{2,3},{11,10},{9,8},{16,17},{18,19},{27,26},{25,24},{28,29},... | collective-permute-start | bytes 786440 | tf_op jit(solution)/shard_map/ppermute | solution.py:777
  62.3 0.9 collective-permute-done.70
  63.2 1.5 %basis.2 = (f32[5,256,128]{2,1,0:T(8,128)S(1)}, f32[768,128]{1,0:T(8,128)S(1)}, f32[768,128]{1,0:T(8,128)S(1)}, f32[768,128]{1,0:T(8,128)S(1)}, f32[768,128]{1,0:T(8,128)S(1)}, /*index=5*/f32[768,128]{1,0:T(8,128)S(1)}) custom-call(f32[8,128]{1,0:T(8,128)S(1)} %get-tuple-element.61.scale_ref.refs_0_, f32[256,128]{1,0:T(8,128)S(1)} %get-tuple-element.255.tan_ref.refs_1_, ...), custom_call_target="tpu_custom_call" | custom-call | tf_op jit(solution)/shard_map/basis/pallas_call | solution.py:260
  64.7 0.7 collective-permute-start.72
  65.3 5.9 %collective-permute-start.73 = (f32[256,128]{1,0:T(8,128)S(1)}, f32[256,128]{1,0:T(8,128)S(1)}, u32[]{:S(2)}, u32[]{:S(2)}) collective-permute-start(f32[256,128]{1,0:T(8,128)S(1)} %slice_bitcast_fusion.12.refs_8_), channel_id=1, source_target_pairs={{0,1},{2,3},{11,10},{9,8},{16,17},{18,19},{27,26},{25,24},{28,29},... | collective-permute-start | bytes 393224 | tf_op jit(solution)/shard_map/ppermute | solution.py:777
  71.4 0.8 collective-permute-done.73.refs_9_
  72.2 0.9 basis.3
  73.1 14.0 %all_to_all.148 = f32[32,1,128]{2,1,0:T(1,128)S(1)} all-to-all(f32[32,1,128]{2,1,0:T(1,128)S(1)} %bitcast.81), channel_id=1, replica_groups=mesh['blk'=4,'slab'=2,'micro'=4] {'blk','slab','micro'}, dimensions={0} | all-to-all | bytes 32768 | tf_op jit(solution)/shard_map/all_to_all | solution.py:837
  87.1 1.7 %last.1 = (f32[16,2,2,8,128]{4,3,2,1,0:T(8,128)}, f32[8,128]{1,0:T(8,128)S(1)}) custom-call(f32[8,128]{1,0:T(8,128)S(1)} %get-tuple-element.61.scale_ref.refs_0_, f32[32,128]{1,0:T(8,128)S(1)} %bitcast.80, f32[5,256,128]{2,1,0:T(8,128)S(1)} %get-tuple-element.79.early_ref.refs_6_.refs_2_, f32[4,256,128]{2,1,0:T(8,128)S(1)} %get-tuple-element.86.refs_3_), custom_call_target="tpu_custom_call" | custom-call | tf_op jit(solution)/shard_map/last/pallas_call | solution.py:260
  88.8 3.7 %all-to-all-start.18 = ((f32[16,2,2,8,128]{4,3,2,1,0:T(8,128)}), f32[16,2,2,8,128]{4,3,2,1,0:T(8,128)S(1)}, u32[]{:S(2)}, u32[]{:S(2)}) async-start(f32[16,2,2,8,128]{4,3,2,1,0:T(8,128)} %get-tuple-element.88), calls=%async_computation.18 | async-start | bytes 524288 | tf_op jit(solution)/shard_map/all_to_all | solution.py:842
  93.7 8.8 %all-to-all-done.18.refs_1_ = f32[16,2,2,8,128]{4,3,2,1,0:T(8,128)S(1)} async-done(((f32[16,2,2,8,128]{4,3,2,1,0:T(8,128)}), f32[16,2,2,8,128]{4,3,2,1,0:T(8,128)S(1)}, u32[]{:S(2)}, u32[]{:S(2)}) %all-to-all-start.18) | async-done | bytes 262176 | tf_op jit(solution)/shard_map/all_to_all | solution.py:842
  102.6 1.0 deliver.1
  (55 shorter events, 4.1 us)
Async XLA Ops:
  2.7 21.9 %all-to-all-start.16 = ((f32[16,2,4,8,128]{4,3,2,1,0:T(8,128)}), f32[16,2,4,8,128]{4,3,2,1,0:T(8,128)S(1)}, u32[]{:S(2)}, u32[]{:S(2)}) async-start(f32[16,2,4,8,128]{4,3,2,1,0:T(8,128)} %spread.1), calls=%async_computation.16 | async-start | bytes 1048576 | tf_op jit(solution)/shard_map/all_to_all | solution.py:792
  10.1 0.7 copy-start.6
  10.9 0.7 copy-start.7
  11.6 0.7 copy-start.5
  25.2 11.5 %collective-permute-start.66 = (f32[36,8,128]{2,1,0:T(8,128)S(1)}, f32[36,8,128]{2,1,0:T(8,128)S(1)}, u32[]{:S(2)}, u32[]{:S(2)}) collective-permute-start(f32[36,8,128]{2,1,0:T(8,128)S(1)} %get-tuple-element.67), channel_id=1, source_target_pairs={{0,1},{2,3},{11,10},{9,8},{16,17},{18,19},{27,26},{25,24},{28,29},... | collective-permute-start | bytes 442376 | tf_op jit(solution)/shard_map/ppermute | solution.py:777
  25.2 11.4 %collective-permute-start.67 = (f32[36,8,128]{2,1,0:T(8,128)S(1)}, f32[36,8,128]{2,1,0:T(8,128)S(1)}, u32[]{:S(2)}, u32[]{:S(2)}) collective-permute-start(f32[36,8,128]{2,1,0:T(8,128)S(1)} %get-tuple-element.68), channel_id=1, source_target_pairs={{1,2},{3,11},{10,9},{8,16},{17,18},{19,27},{26,25},{24,28},{29,30}... | collective-permute-start | bytes 442376 | tf_op jit(solution)/shard_map/ppermute | solution.py:777
  25.9 2.3 %copy-start.8 = (bf16[4,256,256]{2,1,0:T(8,128)(2,1)S(1)}, bf16[4,256,256]{2,1,0:T(8,128)(2,1)}, u32[]{:S(2)}) copy-start(bf16[4,256,256]{2,1,0:T(8,128)(2,1)} %refs_4_.5) | copy-start | bytes 1572868
  44.2 11.9 %collective-permute-start.68 = (f32[4,8,128]{2,1,0:T(8,128)S(1)}, f32[4,8,128]{2,1,0:T(8,128)S(1)}, u32[]{:S(2)}, u32[]{:S(2)}) collective-permute-start(f32[4,8,128]{2,1,0:T(8,128)S(1)} %bitcast.128), channel_id=1, source_target_pairs={{0,1},{2,3},{11,10},{9,8},{16,17},{18,19},{27,26},{25,24},{28,29},... | collective-permute-start | bytes 49160 | tf_op jit(solution)/shard_map/ppermute | solution.py:777
  46.7 9.3 %collective-permute-start.69 = (f32[4,8,128]{2,1,0:T(8,128)S(1)}, f32[4,8,128]{2,1,0:T(8,128)S(1)}, u32[]{:S(2)}, u32[]{:S(2)}) collective-permute-start(f32[4,8,128]{2,1,0:T(8,128)S(1)} %bitcast.127), channel_id=1, source_target_pairs={{1,2},{3,11},{10,9},{8,16},{17,18},{19,27},{26,25},{24,28},{29,30}... | collective-permute-start | bytes 49160 | tf_op jit(solution)/shard_map/ppermute | solution.py:777
  57.0 5.2 %collective-permute-start.71 = (f32[2,256,128]{2,1,0:T(8,128)S(1)}, f32[2,256,128]{2,1,0:T(8,128)S(1)}, u32[]{:S(2)}, u32[]{:S(2)}) collective-permute-start(f32[2,256,128]{2,1,0:T(8,128)S(1)} %rhs.1), channel_id=1, source_target_pairs={{1,2},{3,11},{10,9},{8,16},{17,18},{19,27},{26,25},{24,28},{29,30}... | collective-permute-start | bytes 786440 | tf_op jit(solution)/shard_map/ppermute | solution.py:777
  57.7 5.5 %collective-permute-start.70 = (f32[2,256,128]{2,1,0:T(8,128)S(1)}, f32[2,256,128]{2,1,0:T(8,128)S(1)}, u32[]{:S(2)}, u32[]{:S(2)}) collective-permute-start(f32[2,256,128]{2,1,0:T(8,128)S(1)} %rhs.1), channel_id=1, source_target_pairs={{0,1},{2,3},{11,10},{9,8},{16,17},{18,19},{27,26},{25,24},{28,29},... | collective-permute-start | bytes 786440 | tf_op jit(solution)/shard_map/ppermute | solution.py:777
  64.7 6.7 %collective-permute-start.72 = (f32[256,128]{1,0:T(8,128)S(1)}, f32[256,128]{1,0:T(8,128)S(1)}, u32[]{:S(2)}, u32[]{:S(2)}) collective-permute-start(f32[256,128]{1,0:T(8,128)S(1)} %slice_bitcast_fusion.12.refs_8_), channel_id=1, source_target_pairs={{1,2},{3,11},{10,9},{8,16},{17,18},{19,27},{26,25},{24,28},{29,30}... | collective-permute-start | bytes 393224 | tf_op jit(solution)/shard_map/ppermute | solution.py:777
  65.3 6.9 %collective-permute-start.73 = (f32[256,128]{1,0:T(8,128)S(1)}, f32[256,128]{1,0:T(8,128)S(1)}, u32[]{:S(2)}, u32[]{:S(2)}) collective-permute-start(f32[256,128]{1,0:T(8,128)S(1)} %slice_bitcast_fusion.12.refs_8_), channel_id=1, source_target_pairs={{0,1},{2,3},{11,10},{9,8},{16,17},{18,19},{27,26},{25,24},{28,29},... | collective-permute-start | bytes 393224 | tf_op jit(solution)/shard_map/ppermute | solution.py:777
  87.1 15.4 %copy-start.4 = (s32[8,32,128]{2,1,0:T(8,128)S(1)}, s32[8,32,128]{2,1,0:T(8,128)}, u32[]{:S(2)}) copy-start(s32[8,32,128]{2,1,0:T(8,128)} %refs_4_.3) | copy-start | bytes 393220
  88.8 13.7 %copy-start = (f32[8,32,128]{2,1,0:T(8,128)S(1)}, f32[8,32,128]{2,1,0:T(8,128)}, u32[]{:S(2)}) copy-start(f32[8,32,128]{2,1,0:T(8,128)} %refs_2_.1) | copy-start | bytes 393220
  88.8 13.7 %copy-start.1 = (f32[8,32,128]{2,1,0:T(8,128)S(1)}, f32[8,32,128]{2,1,0:T(8,128)}, u32[]{:S(2)}) copy-start(f32[8,32,128]{2,1,0:T(8,128)} %refs_0_.5) | copy-start | bytes 393220
  88.8 13.7 %copy-start.2 = (f32[8,32,128]{2,1,0:T(8,128)S(1)}, f32[8,32,128]{2,1,0:T(8,128)}, u32[]{:S(2)}) copy-start(f32[8,32,128]{2,1,0:T(8,128)} %refs_1_.1) | copy-start | bytes 393220
  88.8 13.7 %copy-start.3 = (s32[8,32,128]{2,1,0:T(8,128)S(1)}, s32[8,32,128]{2,1,0:T(8,128)}, u32[]{:S(2)}) copy-start(s32[8,32,128]{2,1,0:T(8,128)} %refs_3_.2) | copy-start | bytes 393220
  88.8 13.7 %all-to-all-start.18 = ((f32[16,2,2,8,128]{4,3,2,1,0:T(8,128)}), f32[16,2,2,8,128]{4,3,2,1,0:T(8,128)S(1)}, u32[]{:S(2)}, u32[]{:S(2)}) async-start(f32[16,2,2,8,128]{4,3,2,1,0:T(8,128)} %get-tuple-element.88), calls=%async_computation.18 | async-start | bytes 524288 | tf_op jit(solution)/shard_map/all_to_all | solution.py:842
